TPU v7x, 256 devices: a whole 4x4x8 slice. The times are simulated.
256 devices in a mesh: gx: 4 (over x_lo, core), gy: 8 (over y, x_hi), gz: 8 (over z).
Axes of the slice: x: 4 (x_hi: 2, x_lo: 2; x = x_hi * 2 + x_lo), y: 4, z: 8, core: 2. Of those that a mesh axis runs over, the one named last changes fastest.
Arguments:
- phi_start: float32 [128, 384, 2048], P('gx', 'gy', 'gz'), may hold values from -6 to 6
- band_ids: int32 [4, 8, 8, 64], P('gx', 'gy', 'gz'), may hold values from 0 to 95, as said below
- band_count: int32 [4, 8, 8], P('gx', 'gy', 'gz'), may hold values from 2 to 64, as said below
- owners: int32 [4, 8, 8, 64], P('gx', 'gy', 'gz'), may hold values from 0 to 31, as said below
Outputs:
- level_set: float32 [128, 384, 2048], P('gx', 'gy', 'gz')
- brick_stats: float32 [4, 8, 8, 5, 64], P('gx', 'gy', 'gz')
Inputs may be any that keep to these rules, and one draw needn't show every extreme that they name: `band_ids`: a device's 64 entries are distinct brick numbers. `band_count`: some device has 64 live entries and some has 2. `owners`: no owner appears more than 2 times in one device's list; some owner appears 2 times among the first 2 entries of every device's list.
All inputs are finite; a program needn't handle non-finite values.
Results may differ from a plain program's by a relative error of at most 0.0003.
Values sent between devices are 32-bit elements; how exact they have to be, the bound alone decides.
No kernel may reach another device: no remote copies, remote signals or barrier semaphores. Data moves between devices by JAX's collectives and lax.ppermute only.
A program may use at most 128 MiB of HBM per device.

v0:
```python
import jax
import jax.numpy as jnp
from jax import lax
from jax.experimental import pallas as pl
from jax.experimental.pallas import tpu as pltpu
from jax.sharding import PartitionSpec as P

STEPS = 3
BRICK = 16
SLOTS = 64
CX, CY, CZ = 32, 48, 256
ROWS = CX * CY
YT = CY // 8
SUB = 2
WENO_EPS = 1e-06
F32 = jnp.float32
VMEM_LIMIT = 48 * 1024 * 1024


def rcp(value):
    return pltpu.reciprocal(value, approx=True)


def smooth_weights(e_low, e_high, third):
    base = third * third * (4.0 / 3.0) + WENO_EPS
    q_a = rcp(e_low * (e_low - third) + base)
    q_b = rcp(e_low * e_high + base)
    q_c = rcp(e_high * (e_high + third) + base)
    return q_a * q_a, 6.0 * (q_b * q_b), q_c * q_c


def biased_parts(wa_next, wb, wc_prev, t_prev, t_here, t_next):
    x = wc_prev * (t_here - t_prev)
    y = wa_next * (t_next - t_here)
    both = x + y
    both = both + both
    total = (wa_next + wb) + wc_prev
    left = t_here + (both + y) * rcp(total + (wa_next + wa_next))
    right = (both + x) * rcp(total + (wc_prev + wc_prev)) - t_here
    return left, right


def upwind_square(centre, left, right, sigma):
    best = jnp.maximum(sigma * (centre - left), (-sigma) * (centre + right))
    best = jnp.maximum(best, 0.0)
    return best * best


def sigma_of(value):
    return jnp.where(value > 0.0, F32(1.0), F32(-1.0))


def from_values(v_m, v_0, v_1, v_2):
    d_m, d_0, d_1 = v_0 - v_m, v_1 - v_0, v_2 - v_1
    e_0, e_1 = d_0 - d_m, d_1 - d_0
    return e_0, e_1, e_1 - e_0


def z_column(even, odd, sigma_even, sigma_odd):
    def down(part):
        return pltpu.roll(part, 1, 1)

    def up(part):
        return pltpu.roll(part, 127, 1)

    v = {-2: down(even), -1: down(odd), 0: even, 1: odd, 2: up(even), 3: up(odd)}
    d = {k: v[k + 1] - v[k] for k in range(-2, 3)}
    e = {k: d[k] - d[k - 1] for k in range(-1, 3)}
    t = {k: e[k + 1] - e[k] for k in range(-1, 2)}
    t[2] = up(t[0])
    w_0 = smooth_weights(e[0], e[1], t[0])
    w_1 = smooth_weights(e[1], e[2], t[1])
    left_0, right_0 = biased_parts(w_1[0], w_0[1], down(w_1[2]), t[-1], t[0], t[1])
    left_1, right_1 = biased_parts(up(w_0[0]), w_1[1], w_0[2], t[0], t[1], t[2])
    return (
        upwind_square(3.0 * (d[-1] + d[0]), down(left_1), right_0, sigma_even),
        upwind_square(3.0 * (d[0] + d[1]), left_0, right_1, sigma_odd),
    )


def edge_column(window, u_ref, p_ref, u_row, p_row, sigma):
    def rows(start):
        return window[pl.ds(start, 8), :]

    e_0, e_1, t = from_values(rows(u_row - 1), rows(u_row), rows(u_row + 1), rows(u_row + 2))
    w_a, w_b, w_c = smooth_weights(e_0, e_1, t)
    for slot, part in enumerate((w_a, w_b, w_c, t)):
        u_ref[slot, pl.ds(u_row, 8), :] = part
    left, right = biased_parts(
        u_ref[0, pl.ds(p_row + 1, 8), :],
        u_ref[1, pl.ds(p_row, 8), :],
        u_ref[2, pl.ds(p_row - 1, 8), :],
        u_ref[3, pl.ds(p_row - 1, 8), :],
        u_ref[3, pl.ds(p_row, 8), :],
        u_ref[3, pl.ds(p_row + 1, 8), :],
    )
    p_ref[0, pl.ds(p_row, 8), :] = left
    p_ref[1, pl.ds(p_row, 8), :] = right
    centre = 3.0 * (rows(9) - rows(7))
    return upwind_square(
        centre, p_ref[0, pl.ds(7, 8), :], p_ref[1, pl.ds(8, 8), :], sigma
    )


def write_faces(source, xlo, xhi, ylo, yhi, zlo, zhi):
    xlo[...] = source[0:3]
    xhi[...] = source[CX - 3 : CX]

    for x in range(CX):
        for k in range(3):
            ylo[k, x : x + 1, :] = source[x, k : k + 1, :]
            yhi[k, x : x + 1, :] = source[x, CY - 3 + k : CY - 2 + k, :]
    for chunk in range(CX // 8):
        columns = slice(8 * CY * chunk, 8 * CY * (chunk + 1))
        for parity in range(2):
            part = source[8 * chunk : 8 * chunk + 8, :, 128 * parity : 128 * parity + 128]
            part = part.reshape(8 * CY, 128).T
            for k in range(4):
                zlo[2 * k + parity : 2 * k + parity + 1, columns] = part[k : k + 1]
                zhi[2 * k + parity : 2 * k + parity + 1, columns] = part[124 + k : 125 + k]


def pack_kernel(phi, mixed, xlo, xhi, ylo, yhi, zlo, zhi, turned):
    for chunk in range(CX // 8):
        planes = slice(8 * chunk, 8 * chunk + 8)
        for half in range(2):
            part = phi[planes, :, 128 * half : 128 * half + 128]
            part = part.reshape(8 * CY, 128).T
            for c in range(3):
                turned[c, 128 * half : 128 * half + 128, :] = part[:, 128 * c : 128 * c + 128]
        for parity in range(2):
            part = [turned[c, pl.ds(parity, 128, stride=2), :].T for c in range(3)]
            part = jnp.concatenate(part, axis=0)
            mixed[planes, :, 128 * parity : 128 * parity + 128] = part.reshape(8, CY, 128)
    write_faces(mixed, xlo, xhi, ylo, yhi, zlo, zhi)


def unpack_kernel(mixed, out, turned):
    for chunk in range(CX // 8):
        planes = slice(8 * chunk, 8 * chunk + 8)
        for parity in range(2):
            part = mixed[planes, :, 128 * parity : 128 * parity + 128]
            part = part.reshape(8 * CY, 128).T
            for c in range(3):
                turned[c, pl.ds(parity, 128, stride=2), :] = part[:, 128 * c : 128 * c + 128]
        for half in range(2):
            part = [turned[c, 128 * half : 128 * half + 128, :].T for c in range(3)]
            part = jnp.concatenate(part, axis=0)
            out[planes, :, 128 * half : 128 * half + 128] = part.reshape(8, CY, 128)


def step_kernel(
    phi0, zlo0, zhi0, v, zlo_own, zhi_own, x_low, x_high, y_low, y_high, z_low, z_high,
    out, xlo, xhi, ylo, yhi, zlo, zhi,
    vs, summed, u_ref, p_ref, window, zu_ref, zp_ref, edges, fixes,
):
    def fill(x, carry):
        for zt in range(2):
            lanes = pl.ds(128 * zt, 128)
            vs[zt, x, 8 : 8 + CY, :] = v[x, :, lanes]
        return carry

    lax.fori_loop(0, CX, fill, 0)
    for x in range(CX):
        for zt in range(2):
            for k in range(3):
                lanes = slice(128 * zt, 128 * zt + 128)
                vs[zt, x, 5 + k : 6 + k, :] = y_low[k, x : x + 1, lanes]
                vs[zt, x, 8 + CY + k : 9 + CY + k, :] = y_high[k, x : x + 1, lanes]

    window[pl.ds(5, 3), :] = z_low[5:8, :]
    window[pl.ds(8, 8), :] = zlo_own[...]
    fixed = edge_column(window, zu_ref, zp_ref, 6, 7, sigma_of(zlo0[...]))
    for parity, lane_at, cell_at in ((0, 0, 0), (0, 1, 2), (1, 0, 1)):
        edges[parity, lane_at : lane_at + 1, :] = fixed[cell_at : cell_at + 1]
    window[pl.ds(8, 8), :] = zhi_own[...]
    window[pl.ds(16, 3), :] = z_high[0:3, :]
    fixed = edge_column(window, zu_ref, zp_ref, 9, 8, sigma_of(zhi0[...]))
    for parity, lane_at, cell_at in ((0, 127, 6), (1, 126, 5), (1, 127, 7)):
        edges[parity, lane_at : lane_at + 1, :] = fixed[cell_at : cell_at + 1]
    for parity in range(2):
        fixes[parity] = edges[parity].T

    def x_pass(yt, carry):
        row = pl.multiple_of(8 * yt, 8)
        for zt in range(2):
            lanes = pl.ds(128 * zt, 128)

            def cell(x):
                if x < 0:
                    return x_low[3 + x, pl.ds(row, 8), lanes]
                if x >= CX:
                    return x_high[x - CX, pl.ds(row, 8), lanes]
                return v[x, pl.ds(row, 8), lanes]

            d, e, t, weights, lefts, rights = {}, {}, {}, {}, {}, {}
            d[-3] = cell(-2) - cell(-3)
            d[-2] = cell(-1) - cell(-2)
            e[-2] = d[-2] - d[-3]
            for j in range(-2, CX + 1):
                d[j + 1] = cell(j + 2) - cell(j + 1)
                e[j + 1] = d[j + 1] - d[j]
                t[j] = e[j + 1] - e[j]
                weights[j] = smooth_weights(e[j], e[j + 1], t[j])
                p = j - 1
                if p >= -1:
                    lefts[p], rights[p] = biased_parts(
                        weights[p + 1][0], weights[p][1], weights[p - 1][2], t[p - 1], t[p], t[p + 1]
                    )
                if p >= 0:
                    sigma = sigma_of(phi0[p, pl.ds(row, 8), lanes])
                    centre = 3.0 * (d[p - 1] + d[p])
                    summed[zt, p, pl.ds(row, 8), :] = upwind_square(
                        centre, lefts[p - 1], rights[p], sigma
                    )
        return carry

    lax.fori_loop(0, YT, x_pass, 0)

    lane = lax.broadcasted_iota(jnp.int32, (8, 128), 1)
    fix_even = (lane < 2) | (lane == 127)
    fix_odd = (lane < 1) | (lane > 125)

    def y_weights(x, sub, zt, k):
        start = 6 + 8 * k
        e_0, e_1, t = from_values(
            *[vs[zt, x, pl.ds(start + shift, 8), :] for shift in (-1, 0, 1, 2)]
        )
        w_a, w_b, w_c = smooth_weights(e_0, e_1, t)
        for slot, part in enumerate((w_a, w_b, w_c, t)):
            u_ref[sub, zt, slot, pl.ds(8 * k, 8), :] = part

    def y_parts(sub, zt, k):
        def read(slot, row):
            return u_ref[sub, zt, slot, pl.ds(row, 8), :]

        row = 8 * k + 1
        left, right = biased_parts(
            read(0, row + 1), read(1, row), read(2, row - 1),
            read(3, row - 1), read(3, row), read(3, row + 1),
        )
        p_ref[sub, zt, 0, pl.ds(8 * k, 8), :] = left
        p_ref[sub, zt, 1, pl.ds(8 * k, 8), :] = right

    def update(x, sub, k):
        rows = pl.ds(8 * k, 8)
        values, signs, sigmas, totals = [], [], [], []
        for zt in range(2):
            phi = phi0[x, rows, pl.ds(128 * zt, 128)]
            sigma = sigma_of(phi)
            centre = 3.0 * (
                vs[zt, x, pl.ds(9 + 8 * k, 8), :] - vs[zt, x, pl.ds(7 + 8 * k, 8), :]
            )
            totals.append(
                summed[zt, x, rows, :]
                + upwind_square(
                    centre, p_ref[sub, zt, 0, rows, :], p_ref[sub, zt, 1, pl.ds(8 * k + 1, 8), :], sigma
                )
            )
            values.append(vs[zt, x, pl.ds(8 + 8 * k, 8), :])
            sigmas.append(sigma)
            signs.append(phi * lax.rsqrt(phi * phi + 1.0))
        along = z_column(*values, *sigmas)
        flat = pl.multiple_of(x * CY, 8) + 8 * k
        along = (
            jnp.where(fix_even, fixes[0, pl.ds(flat, 8), :], along[0]),
            jnp.where(fix_odd, fixes[1, pl.ds(flat, 8), :], along[1]),
        )
        for zt in range(2):
            total = totals[zt] + along[zt]
            root = total * lax.rsqrt(jnp.maximum(total, 1e-30))
            out[x, rows, pl.ds(128 * zt, 128)] = values[zt] - signs[zt] * (0.05 * root - 0.3)

    def yz_pass(group, carry):
        for sub in range(SUB):
            for zt in range(2):
                for k in range(YT + 1):
                    y_weights(group * SUB + sub, sub, zt, k)
        for sub in range(SUB):
            for zt in range(2):
                for k in range(YT + 1):
                    y_parts(sub, zt, k)
        for sub in range(SUB):
            for k in range(YT):
                update(group * SUB + sub, sub, k)
        return carry

    lax.fori_loop(0, CX // SUB, yz_pass, 0)
    write_faces(out, xlo, xhi, ylo, yhi, zlo, zhi)


FACES = [
    jax.ShapeDtypeStruct((3, CY, CZ), F32),
    jax.ShapeDtypeStruct((3, CY, CZ), F32),
    jax.ShapeDtypeStruct((3, CX, CZ), F32),
    jax.ShapeDtypeStruct((3, CX, CZ), F32),
    jax.ShapeDtypeStruct((8, ROWS), F32),
    jax.ShapeDtypeStruct((8, ROWS), F32),
]
BLOCK = jax.ShapeDtypeStruct((CX, CY, CZ), F32)


def vmem_specs(count):
    return [pl.BlockSpec(memory_space=pltpu.VMEM)] * count


def pack(phi):
    return pl.pallas_call(
        pack_kernel,
        out_shape=[BLOCK] + FACES,
        in_specs=vmem_specs(1),
        out_specs=vmem_specs(7),
        scratch_shapes=[pltpu.VMEM((3, CZ, 128), F32)],
        compiler_params=pltpu.CompilerParams(vmem_limit_bytes=VMEM_LIMIT),
        name="pack",
    )(phi)


def unpack(mixed):
    return pl.pallas_call(
        unpack_kernel,
        out_shape=BLOCK,
        in_specs=vmem_specs(1),
        out_specs=vmem_specs(1)[0],
        scratch_shapes=[pltpu.VMEM((3, CZ, 128), F32)],
        compiler_params=pltpu.CompilerParams(vmem_limit_bytes=VMEM_LIMIT),
        name="unpack",
    )(mixed)


def step(phi0, zlo0, zhi0, v, zlo_own, zhi_own, halos):
    return pl.pallas_call(
        step_kernel,
        out_shape=[BLOCK] + FACES,
        in_specs=vmem_specs(12),
        out_specs=vmem_specs(7),
        scratch_shapes=[
            pltpu.VMEM((2, CX, 64, 128), F32),
            pltpu.VMEM((2, CX, CY, 128), F32),
            pltpu.VMEM((SUB, 2, 4, 64, 128), F32),
            pltpu.VMEM((SUB, 2, 2, 64, 128), F32),
            pltpu.VMEM((24, ROWS), F32),
            pltpu.VMEM((4, 24, ROWS), F32),
            pltpu.VMEM((2, 24, ROWS), F32),
            pltpu.VMEM((2, 128, ROWS), F32),
            pltpu.VMEM((2, ROWS, 128), F32),
        ],
        compiler_params=pltpu.CompilerParams(vmem_limit_bytes=VMEM_LIMIT),
        name="step",
    )(phi0, zlo0, zhi0, v, zlo_own, zhi_own, *halos)


HALF_COS = [
    0.9999999991256178, -0.23370050635094053, 0.019968606689123116,
    -0.0008935362743290266, 2.3601076640059624e-05,
]
BAND_SQUARE = 1.5 * 1.5


def half_cosine(value):
    square = jnp.minimum(value * value, BAND_SQUARE)
    shape = F32(HALF_COS[4] / BAND_SQUARE**5)
    for k in (3, 2, 1, 0):
        shape = shape * square + F32(HALF_COS[k] / BAND_SQUARE ** (k + 1))
    return (BAND_SQUARE - square) * shape


def five_terms(centre, keep, dx, sx, dy, sy, dz, sz, dxy, dxz, dyz):
    twice = centre + centre
    xx, yy, zz = dx * dx, dy * dy, dz * dz
    squares = jnp.maximum(xx + yy + zz, 1.0)
    root = lax.rsqrt(squares)
    bend = (sx - twice) * (yy + zz) + (sy - twice) * (xx + zz) + (sz - twice) * (xx + yy)
    bend = bend - 0.5 * (dx * (dy * dxy + dz * dxz) + dy * dz * dyz)
    cosine = half_cosine(centre)
    spread = cosine * cosine
    if keep is not None:
        spread = jnp.where(keep, spread, 0.0)
    return (
        spread * (squares * root),
        spread * bend * (root * root),
        spread * dx,
        spread * dy,
        spread * dz,
    )


def brick_kernel(v, x_low, x_high, y_low, y_high, z_window, places, z_places, record, vs, stack):
    def fill(x, carry):
        for zt in range(2):
            vs[zt, x + 1, 8 : 8 + CY, :] = v[x, :, pl.ds(128 * zt, 128)]
        return carry

    lax.fori_loop(0, CX, fill, 0)
    for zt in range(2):
        lanes = slice(128 * zt, 128 * zt + 128)
        vs[zt, 0, 8 : 8 + CY, :] = x_low[0, :, lanes]
        vs[zt, CX + 1, 8 : 8 + CY, :] = x_high[0, :, lanes]
        for x in range(CX + 2):
            vs[zt, x, 7:8, :] = y_low[x : x + 1, lanes]
            vs[zt, x, 8 + CY : 9 + CY, :] = y_high[x : x + 1, lanes]

    lane = lax.broadcasted_iota(jnp.int32, (8, 128), 1)
    keeps = (lane != 0, lane != 127)

    def down(part):
        return pltpu.roll(part, 1, 1)

    def up(part):
        return pltpu.roll(part, 127, 1)

    def neighbours(pair):
        return ((down(pair[1]), pair[1]), (pair[0], up(pair[0])))

    def tile_terms(x, k):
        def read(zt, plane, shift):
            return vs[zt, plane, pl.ds(8 + 8 * k + shift, 8), :]

        two = range(2)
        centre = [read(zt, x + 1, 0) for zt in two]
        high = [read(zt, x + 2, 0) for zt in two]
        low = [read(zt, x, 0) for zt in two]
        dx = [high[zt] - low[zt] for zt in two]
        sx = [high[zt] + low[zt] for zt in two]
        right = [read(zt, x + 1, 1) for zt in two]
        left = [read(zt, x + 1, -1) for zt in two]
        dy = [right[zt] - left[zt] for zt in two]
        sy = [right[zt] + left[zt] for zt in two]
        dxy = [
            (read(zt, x + 2, 1) - read(zt, x, 1)) - (read(zt, x + 2, -1) - read(zt, x, -1))
            for zt in two
        ]
        around, dx_around, dy_around = neighbours(centre), neighbours(dx), neighbours(dy)
        results = []
        for zt in two:
            results.append(
                five_terms(
                    centre[zt], keeps[zt], dx[zt], sx[zt], dy[zt], sy[zt],
                    around[zt][1] - around[zt][0], around[zt][1] + around[zt][0],
                    dxy[zt],
                    dx_around[zt][1] - dx_around[zt][0],
                    dy_around[zt][1] - dy_around[zt][0],
                )
            )
        return [results[0][n] + results[1][n] for n in range(5)]

    zeros = jnp.zeros((8, 128), F32)
    for bx in range(2):

        def body(step_at, sums):
            sums = list(sums)
            for sub in range(2):
                x = BRICK * bx + 2 * step_at + sub
                for k in range(YT):
                    parts = tile_terms(x, k)
                    for n in range(5):
                        slot = 5 * (k // 2) + n
                        sums[slot] = sums[slot] + parts[n]
            return tuple(sums)

        sums = lax.fori_loop(0, BRICK // 2, body, (zeros,) * 15)
        for by in range(3):
            for n in range(5):
                row = 8 * (3 * bx + by) + n
                stack[row : row + 1, :] = jnp.sum(sums[5 * by + n], axis=0, keepdims=True)
            row = 8 * (3 * bx + by)
            stack[row + 5 : row + 8, :] = jnp.zeros((3, 128), F32)

    total = jnp.zeros((8, SLOTS), F32)
    for b in range(6):
        total = total + jnp.dot(
            stack[8 * b : 8 * b + 8, :], places[b],
            precision=lax.Precision.HIGHEST, preferred_element_type=F32,
        )
    for side in range(2):
        planes = [z_window[3 * side + k] for k in range(3)]

        def cut(plane, step_x, step_y):
            return planes[plane][1 + step_x : 33 + step_x, 1 + step_y : 49 + step_y]

        high, low = cut(1, 1, 0), cut(1, -1, 0)
        right, left = cut(1, 0, 1), cut(1, 0, -1)
        over, under = cut(2, 0, 0), cut(0, 0, 0)
        terms = five_terms(
            cut(1, 0, 0), None,
            high - low, high + low, right - left, right + left, over - under, over + under,
            (cut(1, 1, 1) - cut(1, -1, 1)) - (cut(1, 1, -1) - cut(1, -1, -1)),
            (cut(2, 1, 0) - cut(2, -1, 0)) - (cut(0, 1, 0) - cut(0, -1, 0)),
            (cut(2, 0, 1) - cut(2, 0, -1)) - (cut(0, 0, 1) - cut(0, 0, -1)),
        )
        for bx in range(2):
            rows = [jnp.sum(term[16 * bx : 16 * bx + 16], axis=0, keepdims=True) for term in terms]
            rows = jnp.concatenate(rows + [jnp.zeros((3, CY), F32)], axis=0)
            total = total + jnp.dot(
                rows, z_places[2 * side + bx],
                precision=lax.Precision.HIGHEST, preferred_element_type=F32,
            )
    scale = 2.0 / 3.0 / (BRICK * BRICK)
    row = lax.broadcasted_iota(jnp.int32, (8, SLOTS), 0)
    record[...] = total * jnp.where(row == 1, F32(scale), F32(0.5 * scale))


def bricks(v, x_low, x_high, y_low, y_high, z_window, places, z_places):
    return pl.pallas_call(
        brick_kernel,
        out_shape=jax.ShapeDtypeStruct((8, SLOTS), F32),
        in_specs=vmem_specs(8),
        out_specs=vmem_specs(1)[0],
        scratch_shapes=[
            pltpu.VMEM((2, CX + 2, 64, 128), F32),
            pltpu.VMEM((48, 128), F32),
        ],
        compiler_params=pltpu.CompilerParams(vmem_limit_bytes=VMEM_LIMIT),
        name="bricks",
    )(v, x_low, x_high, y_low, y_high, z_window, places, z_places)


def shift(value, axis, direction):
    count = lax.axis_size(axis)
    pairs = [(i, (i + direction) % count) for i in range(count)]
    return lax.ppermute(value, axis, pairs)


def place_tables(device_ids, live_count, targets):
    entries = jnp.arange(device_ids.shape[0], dtype=jnp.int32)
    is_live = entries < live_count
    earlier = entries[None, :] < entries[:, None]
    same_owner = targets[None, :] == targets[:, None]
    rank = jnp.sum((earlier & same_owner & is_live[None, :]).astype(jnp.int32), axis=1)
    columns = jnp.where(is_live, targets * 2 + rank, SLOTS)
    count = (CX // BRICK) * (CY // BRICK) * (CZ // BRICK)
    brick = jnp.arange(count, dtype=jnp.int32)
    slot = jnp.arange(SLOTS, dtype=jnp.int32)
    hits = (device_ids[:, None, None] == brick[None, :, None]) & (
        columns[:, None, None] == slot[None, None, :]
    )
    table = jnp.any(hits, axis=0).astype(F32)
    table = table.reshape(2, 3, 16, SLOTS)
    places = jnp.repeat(table.reshape(6, 16, SLOTS), 8, axis=1)
    z_places = [
        jnp.repeat(table[bx, :, end], BRICK, axis=0) for end in (0, 15) for bx in range(2)
    ]
    return places, jnp.stack(z_places, axis=0)


def exchange(faces):
    xlo, xhi, ylo, yhi, zlo, zhi = faces
    return (
        shift(xhi, "gx", 1), shift(xlo, "gx", -1),
        shift(yhi, "gy", 1), shift(ylo, "gy", -1),
        shift(zhi, "gz", 1), shift(zlo, "gz", -1),
    )


def per_device(phi_start, band_ids, band_count, owners):
    places, z_places = place_tables(
        band_ids.reshape(-1), band_count.reshape(()), owners.reshape(-1)
    )
    phi0, *faces = pack(phi_start)
    zlo0, zhi0 = faces[4:]
    v = phi0
    for _ in range(STEPS):
        v, *faces = step(phi0, zlo0, zhi0, v, faces[4], faces[5], exchange(faces))
    level_set = unpack(v)

    xlo, xhi, ylo, yhi, zlo, zhi = faces
    x_low, x_high = shift(xhi[2:3], "gx", 1), shift(xlo[0:1], "gx", -1)
    first = jnp.concatenate([x_low[:, 0], ylo[0], x_high[:, 0]], axis=0)
    last = jnp.concatenate([x_low[:, CY - 1], yhi[2], x_high[:, CY - 1]], axis=0)
    y_low, y_high = shift(last, "gy", 1), shift(first, "gy", -1)

    def plane(body, lane):
        middle = jnp.concatenate(
            [x_low[:, :, lane], body.reshape(CX, CY), x_high[:, :, lane]], axis=0
        )
        return jnp.concatenate([y_low[:, lane, None], middle, y_high[:, lane, None]], axis=1)

    bottom, above = plane(zlo[0], 0), plane(zlo[1], 128)
    below, top = plane(zhi[6], 127), plane(zhi[7], 255)
    under, over = shift(top, "gz", 1), shift(bottom, "gz", -1)
    z_window = jnp.stack([under, bottom, above, below, top, over], axis=0)
    record = bricks(v, x_low, x_high, y_low, y_high, z_window, places, z_places)
    totals = lax.all_to_all(record[:5], ("gx", "gy"), split_axis=1, concat_axis=1, tiled=True)
    return level_set, totals.reshape(1, 1, 1, 5, SLOTS)


def solution(mesh):
    placed = (
        P("gx", "gy", "gz"),
        P("gx", "gy", "gz", None),
        P("gx", "gy", "gz"),
        P("gx", "gy", "gz", None),
    )
    return jax.shard_map(
        per_device,
        mesh=mesh,
        in_specs=placed,
        out_specs=(P("gx", "gy", "gz"), P("gx", "gy", "gz", None, None)),
        check_vma=False,
    )
```

profile of v0, /device:TPU:1, one launch (start us, length us, event | category | flops | bytes accessed | tf_op | source)
XLA Modules:
  0.0 142.1 jit_solution(311576071401540620)
XLA Ops:
  0.6 1.4 copy-done
  2.0 1.6 %pack.1 = (f32[32,48,256]{2,1,0:T(8,128)S(1)}, f32[3,48,256]{2,1,0:T(8,128)S(1)}, f32[3,48,256]{2,1,0:T(8,128)S(1)}, f32[3,32,256]{2,1,0:T(8,128)S(1)}, f32[3,32...) custom-call(f32[32,48,256]{2,1,0:T(8,128)S(1)} %copy-done), custom_call_target="tpu_custom_call" | custom-call | tf_op jit(solution)/shard_map/pack/pallas_call | solution.py:308
  3.7 2.5 %collective-permute-start.4 = (f32[8,1536]{1,0:T(8,128)S(1)}, f32[8,1536]{1,0:T(8,128)S(1)}, u32[]{:S(2)}, u32[]{:S(2)}) collective-permute-start(f32[8,1536]{1,0:T(8,128)S(1)} %get-tuple-element.32.zhi0.zhi_own), channel_id=1, source_target_pairs={{0,1},{1,2},{2,3},{3,4},{4,5},{5,6},{6,7},{7,0},{8,9},{9,10},{10,1... | collective-permute-start | bytes 147464 | tf_op jit(solution)/shard_map/ppermute | solution.py:521
  6.2 4.0 %collective-permute-start.5 = (f32[8,1536]{1,0:T(8,128)S(1)}, f32[8,1536]{1,0:T(8,128)S(1)}, u32[]{:S(2)}, u32[]{:S(2)}) collective-permute-start(f32[8,1536]{1,0:T(8,128)S(1)} %get-tuple-element.31.zlo0.zlo_own), channel_id=1, source_target_pairs={{0,7},{1,0},{2,1},{3,2},{4,3},{5,4},{6,5},{7,6},{8,15},{9,8},{10,9... | collective-permute-start | bytes 147464 | tf_op jit(solution)/shard_map/ppermute | solution.py:521
  10.2 2.1 %collective-permute-start = (f32[3,48,256]{2,1,0:T(8,128)S(1)}, f32[3,48,256]{2,1,0:T(8,128)S(1)}, u32[]{:S(2)}, u32[]{:S(2)}) collective-permute-start(f32[3,48,256]{2,1,0:T(8,128)S(1)} %get-tuple-element.33), channel_id=1, source_target_pairs={{0,64},{64,128},{128,192},{192,0},{1,65},{65,129},{129,193},{193,1... | collective-permute-start | bytes 442376 | tf_op jit(solution)/shard_map/ppermute | solution.py:521
  12.3 2.5 %collective-permute-start.2 = (f32[3,32,256]{2,1,0:T(8,128)S(1)}, f32[3,32,256]{2,1,0:T(8,128)S(1)}, u32[]{:S(2)}, u32[]{:S(2)}) collective-permute-start(f32[3,32,256]{2,1,0:T(8,128)S(1)} %get-tuple-element.35), channel_id=1, source_target_pairs={{0,8},{8,16},{16,24},{24,32},{32,40},{40,48},{48,56},{56,0},{1,9},... | collective-permute-start | bytes 294920 | tf_op jit(solution)/shard_map/ppermute | solution.py:521
  16.4 2.6 %collective-permute-start.3 = (f32[3,32,256]{2,1,0:T(8,128)S(1)}, f32[3,32,256]{2,1,0:T(8,128)S(1)}, u32[]{:S(2)}, u32[]{:S(2)}) collective-permute-start(f32[3,32,256]{2,1,0:T(8,128)S(1)} %get-tuple-element.36), channel_id=1, source_target_pairs={{0,56},{8,0},{16,8},{24,16},{32,24},{40,32},{48,40},{56,48},{1,57}... | collective-permute-start | bytes 294920 | tf_op jit(solution)/shard_map/ppermute | solution.py:521
  21.1 1.2 collective-permute-done.2.y_low
  26.9 13.7 %step.3 = (f32[32,48,256]{2,1,0:T(8,128)S(1)}, f32[3,48,256]{2,1,0:T(8,128)S(1)}, f32[3,48,256]{2,1,0:T(8,128)S(1)}, f32[3,32,256]{2,1,0:T(8,128)S(1)}, f32[3,32...) custom-call(f32[32,48,256]{2,1,0:T(8,128)S(1)} %get-tuple-element.30.phi0.v, ...), custom_call_target="tpu_custom_call" | custom-call | tf_op jit(solution)/shard_map/step/pallas_call | solution.py:332
  40.8 2.7 %collective-permute-start.11 = (f32[8,1536]{1,0:T(8,128)S(1)}, f32[8,1536]{1,0:T(8,128)S(1)}, u32[]{:S(2)}, u32[]{:S(2)}) collective-permute-start(f32[8,1536]{1,0:T(8,128)S(1)} %get-tuple-element.38.zlo_own), channel_id=1, source_target_pairs={{0,7},{1,0},{2,1},{3,2},{4,3},{5,4},{6,5},{7,6},{8,15},{9,8},{10,9... | collective-permute-start | bytes 147464 | tf_op jit(solution)/shard_map/ppermute | solution.py:521
  43.6 2.8 %collective-permute-start.6 = (f32[3,48,256]{2,1,0:T(8,128)S(1)}, f32[3,48,256]{2,1,0:T(8,128)S(1)}, u32[]{:S(2)}, u32[]{:S(2)}) collective-permute-start(f32[3,48,256]{2,1,0:T(8,128)S(1)} %get-tuple-element.40), channel_id=1, source_target_pairs={{0,64},{64,128},{128,192},{192,0},{1,65},{65,129},{129,193},{193,1... | collective-permute-start | bytes 442376 | tf_op jit(solution)/shard_map/ppermute | solution.py:521
  46.5 2.3 %collective-permute-start.8 = (f32[3,32,256]{2,1,0:T(8,128)S(1)}, f32[3,32,256]{2,1,0:T(8,128)S(1)}, u32[]{:S(2)}, u32[]{:S(2)}) collective-permute-start(f32[3,32,256]{2,1,0:T(8,128)S(1)} %get-tuple-element.42), channel_id=1, source_target_pairs={{0,8},{8,16},{16,24},{24,32},{32,40},{40,48},{48,56},{56,0},{1,9},... | collective-permute-start | bytes 294920 | tf_op jit(solution)/shard_map/ppermute | solution.py:521
  48.8 2.8 %collective-permute-start.9 = (f32[3,32,256]{2,1,0:T(8,128)S(1)}, f32[3,32,256]{2,1,0:T(8,128)S(1)}, u32[]{:S(2)}, u32[]{:S(2)}) collective-permute-start(f32[3,32,256]{2,1,0:T(8,128)S(1)} %get-tuple-element.43), channel_id=1, source_target_pairs={{0,56},{8,0},{16,8},{24,16},{32,24},{40,32},{48,40},{56,48},{1,57}... | collective-permute-start | bytes 294920 | tf_op jit(solution)/shard_map/ppermute | solution.py:521
  51.6 5.8 %collective-permute-done.8.y_low = f32[3,32,256]{2,1,0:T(8,128)S(1)} collective-permute-done((f32[3,32,256]{2,1,0:T(8,128)S(1)}, f32[3,32,256]{2,1,0:T(8,128)S(1)}, u32[]{:S(2)}, u32[]{:S(2)}) %collective-permute-start.8) | collective-permute-done | bytes 98336 | tf_op jit(solution)/shard_map/ppermute | solution.py:521
  59.0 13.7 %step.4 = (f32[32,48,256]{2,1,0:T(8,128)S(1)}, f32[3,48,256]{2,1,0:T(8,128)S(1)}, f32[3,48,256]{2,1,0:T(8,128)S(1)}, f32[3,32,256]{2,1,0:T(8,128)S(1)}, f32[3,32...) custom-call(f32[32,48,256]{2,1,0:T(8,128)S(1)} %get-tuple-element.30.phi0.v, ...), custom_call_target="tpu_custom_call" | custom-call | tf_op jit(solution)/shard_map/step/pallas_call | solution.py:332
  72.8 1.5 %collective-permute-start.12 = (f32[3,48,256]{2,1,0:T(8,128)S(1)}, f32[3,48,256]{2,1,0:T(8,128)S(1)}, u32[]{:S(2)}, u32[]{:S(2)}) collective-permute-start(f32[3,48,256]{2,1,0:T(8,128)S(1)} %get-tuple-element.47), channel_id=1, source_target_pairs={{0,64},{64,128},{128,192},{192,0},{1,65},{65,129},{129,193},{193,1... | collective-permute-start | bytes 442376 | tf_op jit(solution)/shard_map/ppermute | solution.py:521
  74.3 1.0 collective-permute-start.14
  75.3 4.1 %collective-permute-start.15 = (f32[3,32,256]{2,1,0:T(8,128)S(1)}, f32[3,32,256]{2,1,0:T(8,128)S(1)}, u32[]{:S(2)}, u32[]{:S(2)}) collective-permute-start(f32[3,32,256]{2,1,0:T(8,128)S(1)} %get-tuple-element.50), channel_id=1, source_target_pairs={{0,56},{8,0},{16,8},{24,16},{32,24},{40,32},{48,40},{56,48},{1,57}... | collective-permute-start | bytes 294920 | tf_op jit(solution)/shard_map/ppermute | solution.py:521
  79.4 2.9 %collective-permute-start.17 = (f32[8,1536]{1,0:T(8,128)S(1)}, f32[8,1536]{1,0:T(8,128)S(1)}, u32[]{:S(2)}, u32[]{:S(2)}) collective-permute-start(f32[8,1536]{1,0:T(8,128)S(1)} %get-tuple-element.45.zlo_own), channel_id=1, source_target_pairs={{0,7},{1,0},{2,1},{3,2},{4,3},{5,4},{6,5},{7,6},{8,15},{9,8},{10,9... | collective-permute-start | bytes 147464 | tf_op jit(solution)/shard_map/ppermute | solution.py:521
  82.3 1.2 collective-permute-done.17.z_high
  83.5 13.7 %step.5 = (f32[32,48,256]{2,1,0:T(8,128)S(1)}, f32[3,48,256]{2,1,0:T(8,128)S(1)}, f32[3,48,256]{2,1,0:T(8,128)S(1)}, f32[3,32,256]{2,1,0:T(8,128)S(1)}, f32[3,32...) custom-call(f32[32,48,256]{2,1,0:T(8,128)S(1)} %get-tuple-element.30.phi0.v, ...), custom_call_target="tpu_custom_call" | custom-call | tf_op jit(solution)/shard_map/step/pallas_call | solution.py:332
  97.9 3.2 %collective-permute-start.18 = (f32[1,48,256]{2,1,0:T(8,128)S(1)}, f32[1,48,256]{2,1,0:T(8,128)S(1)}, u32[]{:S(2)}, u32[]{:S(2)}) collective-permute-start(f32[1,48,256]{2,1,0:T(8,128)S(1)} %slice.99), channel_id=1, source_target_pairs={{0,64},{64,128},{128,192},{192,0},{1,65},{65,129},{129,193},{193,1... | collective-permute-start | bytes 147464 | tf_op jit(solution)/shard_map/ppermute | solution.py:521
  102.2 3.3 %collective-permute-done.19.x_high = f32[1,48,256]{2,1,0:T(8,128)S(1)} collective-permute-done((f32[1,48,256]{2,1,0:T(8,128)S(1)}, f32[1,48,256]{2,1,0:T(8,128)S(1)}, u32[]{:S(2)}, u32[]{:S(2)}) %collective-permute-start.19) | collective-permute-done | bytes 49184 | tf_op jit(solution)/shard_map/ppermute | solution.py:521
  105.5 3.9 %collective-permute-start.21 = (f32[34,256]{1,0:T(8,128)S(1)}, f32[34,256]{1,0:T(8,128)S(1)}, u32[]{:S(2)}, u32[]{:S(2)}) collective-permute-start(f32[34,256]{1,0:T(8,128)S(1)} %pad_maximum_fusion.2), channel_id=1, source_target_pairs={{0,56},{8,0},{16,8},{24,16},{32,24},{40,32},{48,40},{56,48},{1,57}... | collective-permute-start | bytes 104456 | tf_op jit(solution)/shard_map/ppermute | solution.py:521
  110.7 5.3 %collective-permute-done.20.y_low = f32[34,256]{1,0:T(8,128)S(1)} collective-permute-done((f32[34,256]{1,0:T(8,128)S(1)}, f32[34,256]{1,0:T(8,128)S(1)}, u32[]{:S(2)}, u32[]{:S(2)}) %collective-permute-start.20) | collective-permute-done | bytes 34848 | tf_op jit(solution)/shard_map/ppermute | solution.py:521
  116.5 3.7 %collective-permute-done.22 = f32[34,50]{1,0:T(8,128)S(1)} collective-permute-done((f32[34,50]{1,0:T(8,128)S(1)}, f32[34,50]{1,0:T(8,128)S(1)}, u32[]{:S(2)}, u32[]{:S(2)}) %collective-permute-start.22) | collective-permute-done | bytes 6832 | tf_op jit(solution)/shard_map/ppermute | solution.py:521
  120.3 1.5 %collective-permute-start.23 = (f32[34,50]{1,0:T(8,128)S(1)}, f32[34,50]{1,0:T(8,128)S(1)}, u32[]{:S(2)}, u32[]{:S(2)}) collective-permute-start(f32[34,50]{1,0:T(8,128)S(1)} %get-tuple-element.77), channel_id=1, source_target_pairs={{0,7},{1,0},{2,1},{3,2},{4,3},{5,4},{6,5},{7,6},{8,15},{9,8},{10,9... | collective-permute-start | bytes 20408 | tf_op jit(solution)/shard_map/ppermute | solution.py:521
  122.1 0.9 collective-permute-done.23
  123.0 4.7 %bricks.1 = f32[8,64]{1,0:T(8,128)S(1)} custom-call(f32[32,48,256]{2,1,0:T(8,128)S(1)} %get-tuple-element.51.mixed.v, f32[1,48,256]{2,1,0:T(8,128)S(1)} %collective-permute-done.18.x_low, f32[1,48,256]{2,1,0:T(8,128)S(1)} %collective-permute-done.19.x_high, f32[34,256]{1,0:T(8,128)S(1)} %collective-permute-done.20.y_low, ...), custom_call_target="tpu_custom_call" | custom-call | tf_op jit(solution)/shard_map/bricks/pallas_call | solution.py:504
  128.4 5.9 %all-to-all-start = ((f32[5,32,2]{0,2,1:T(2,128)}), f32[5,32,2]{0,2,1:T(2,128)S(1)}, u32[]{:S(2)}, u32[]{:S(2)}) async-start(f32[5,32,2]{0,2,1:T(2,128)} %bitcast.22), calls=%async_computation | async-start | bytes 65536 | tf_op jit(solution)/shard_map/all_to_all | solution.py:583
  134.3 2.2 %unpack.1 = f32[32,48,256]{2,1,0:T(8,128)} custom-call(f32[32,48,256]{2,1,0:T(8,128)S(1)} %get-tuple-element.51.mixed.v), custom_call_target="tpu_custom_call" | custom-call | tf_op jit(solution)/shard_map/unpack/pallas_call | solution.py:320
  136.5 5.0 %all-to-all-done = f32[5,32,2]{0,2,1:T(2,128)S(1)} async-done(((f32[5,32,2]{0,2,1:T(2,128)}), f32[5,32,2]{0,2,1:T(2,128)S(1)}, u32[]{:S(2)}, u32[]{:S(2)}) %all-to-all-start) | async-done | bytes 1312 | tf_op jit(solution)/shard_map/all_to_all | solution.py:583
  (101 shorter events, 14.9 us)
Async XLA Ops:
  0.6 1.4 copy-start
  2.0 13.4 %copy-start.15 = (s32[1,1,1,64]{3,2,1,0:T(1,128)S(1)}, s32[1,1,1,64]{3,2,1,0:T(1,128)}, u32[]{:S(2)}) copy-start(s32[1,1,1,64]{3,2,1,0:T(1,128)} %param.7) | copy-start | bytes 772
  2.0 13.6 %copy-start.16 = (s32[1,1,1,64]{3,2,1,0:T(1,128)S(1)}, s32[1,1,1,64]{3,2,1,0:T(1,128)}, u32[]{:S(2)}) copy-start(s32[1,1,1,64]{3,2,1,0:T(1,128)} %param.5) | copy-start | bytes 772
  3.6 37.0 %copy-start.1 = (f32[8,1536]{1,0:T(8,128)}, f32[8,1536]{1,0:T(8,128)S(1)}, u32[]{:S(2)}) copy-start(f32[8,1536]{1,0:T(8,128)S(1)} %get-tuple-element.31.zlo0.zlo_own) | copy-start | bytes 147460
  3.6 37.0 %copy-start.3 = (f32[8,1536]{1,0:T(8,128)}, f32[8,1536]{1,0:T(8,128)S(1)}, u32[]{:S(2)}) copy-start(f32[8,1536]{1,0:T(8,128)S(1)} %get-tuple-element.32.zhi0.zhi_own) | copy-start | bytes 147460
  3.7 12.1 %collective-permute-start.4 = (f32[8,1536]{1,0:T(8,128)S(1)}, f32[8,1536]{1,0:T(8,128)S(1)}, u32[]{:S(2)}, u32[]{:S(2)}) collective-permute-start(f32[8,1536]{1,0:T(8,128)S(1)} %get-tuple-element.32.zhi0.zhi_own), channel_id=1, source_target_pairs={{0,1},{1,2},{2,3},{3,4},{4,5},{5,6},{6,7},{7,0},{8,9},{9,10},{10,1... | collective-permute-start | bytes 147464 | tf_op jit(solution)/shard_map/ppermute | solution.py:521
  6.2 14.2 %collective-permute-start.5 = (f32[8,1536]{1,0:T(8,128)S(1)}, f32[8,1536]{1,0:T(8,128)S(1)}, u32[]{:S(2)}, u32[]{:S(2)}) collective-permute-start(f32[8,1536]{1,0:T(8,128)S(1)} %get-tuple-element.31.zlo0.zlo_own), channel_id=1, source_target_pairs={{0,7},{1,0},{2,1},{3,2},{4,3},{5,4},{6,5},{7,6},{8,15},{9,8},{10,9... | collective-permute-start | bytes 147464 | tf_op jit(solution)/shard_map/ppermute | solution.py:521
  10.2 13.3 %collective-permute-start = (f32[3,48,256]{2,1,0:T(8,128)S(1)}, f32[3,48,256]{2,1,0:T(8,128)S(1)}, u32[]{:S(2)}, u32[]{:S(2)}) collective-permute-start(f32[3,48,256]{2,1,0:T(8,128)S(1)} %get-tuple-element.33), channel_id=1, source_target_pairs={{0,64},{64,128},{128,192},{192,0},{1,65},{65,129},{129,193},{193,1... | collective-permute-start | bytes 442376 | tf_op jit(solution)/shard_map/ppermute | solution.py:521
  12.3 11.3 %collective-permute-start.1 = (f32[3,48,256]{2,1,0:T(8,128)S(1)}, f32[3,48,256]{2,1,0:T(8,128)S(1)}, u32[]{:S(2)}, u32[]{:S(2)}) collective-permute-start(f32[3,48,256]{2,1,0:T(8,128)S(1)} %get-tuple-element.34), channel_id=1, source_target_pairs={{0,192},{64,0},{128,64},{192,128},{1,193},{65,1},{129,65},{193,129... | collective-permute-start | bytes 442376 | tf_op jit(solution)/shard_map/ppermute | solution.py:521
  12.3 10.0 %collective-permute-start.2 = (f32[3,32,256]{2,1,0:T(8,128)S(1)}, f32[3,32,256]{2,1,0:T(8,128)S(1)}, u32[]{:S(2)}, u32[]{:S(2)}) collective-permute-start(f32[3,32,256]{2,1,0:T(8,128)S(1)} %get-tuple-element.35), channel_id=1, source_target_pairs={{0,8},{8,16},{16,24},{24,32},{32,40},{40,48},{48,56},{56,0},{1,9},... | collective-permute-start | bytes 294920 | tf_op jit(solution)/shard_map/ppermute | solution.py:521
  16.4 6.5 %collective-permute-start.3 = (f32[3,32,256]{2,1,0:T(8,128)S(1)}, f32[3,32,256]{2,1,0:T(8,128)S(1)}, u32[]{:S(2)}, u32[]{:S(2)}) collective-permute-start(f32[3,32,256]{2,1,0:T(8,128)S(1)} %get-tuple-element.36), channel_id=1, source_target_pairs={{0,56},{8,0},{16,8},{24,16},{32,24},{40,32},{48,40},{56,48},{1,57}... | collective-permute-start | bytes 294920 | tf_op jit(solution)/shard_map/ppermute | solution.py:521
  23.5 0.9 copy-start.6
  26.9 13.8 %copy-start.14 = (f32[96,64]{1,0:T(8,128)S(1)}, f32[96,64]{1,0:T(8,128)}, u32[]{:S(2)}) copy-start(f32[96,64]{1,0:T(8,128)} %copy.12) | copy-start | bytes 73732
  40.7 8.1 %collective-permute-start.10 = (f32[8,1536]{1,0:T(8,128)S(1)}, f32[8,1536]{1,0:T(8,128)S(1)}, u32[]{:S(2)}, u32[]{:S(2)}) collective-permute-start(f32[8,1536]{1,0:T(8,128)S(1)} %get-tuple-element.39.zhi_own), channel_id=1, source_target_pairs={{0,1},{1,2},{2,3},{3,4},{4,5},{5,6},{6,7},{7,0},{8,9},{9,10},{10,1... | collective-permute-start | bytes 147464 | tf_op jit(solution)/shard_map/ppermute | solution.py:521
  40.8 10.8 %collective-permute-start.11 = (f32[8,1536]{1,0:T(8,128)S(1)}, f32[8,1536]{1,0:T(8,128)S(1)}, u32[]{:S(2)}, u32[]{:S(2)}) collective-permute-start(f32[8,1536]{1,0:T(8,128)S(1)} %get-tuple-element.38.zlo_own), channel_id=1, source_target_pairs={{0,7},{1,0},{2,1},{3,2},{4,3},{5,4},{6,5},{7,6},{8,15},{9,8},{10,9... | collective-permute-start | bytes 147464 | tf_op jit(solution)/shard_map/ppermute | solution.py:521
  43.6 13.8 %collective-permute-start.6 = (f32[3,48,256]{2,1,0:T(8,128)S(1)}, f32[3,48,256]{2,1,0:T(8,128)S(1)}, u32[]{:S(2)}, u32[]{:S(2)}) collective-permute-start(f32[3,48,256]{2,1,0:T(8,128)S(1)} %get-tuple-element.40), channel_id=1, source_target_pairs={{0,64},{64,128},{128,192},{192,0},{1,65},{65,129},{129,193},{193,1... | collective-permute-start | bytes 442376 | tf_op jit(solution)/shard_map/ppermute | solution.py:521
  46.3 11.1 %collective-permute-start.7 = (f32[3,48,256]{2,1,0:T(8,128)S(1)}, f32[3,48,256]{2,1,0:T(8,128)S(1)}, u32[]{:S(2)}, u32[]{:S(2)}) collective-permute-start(f32[3,48,256]{2,1,0:T(8,128)S(1)} %get-tuple-element.41), channel_id=1, source_target_pairs={{0,192},{64,0},{128,64},{192,128},{1,193},{65,1},{129,65},{193,129... | collective-permute-start | bytes 442376 | tf_op jit(solution)/shard_map/ppermute | solution.py:521
  46.5 10.9 %collective-permute-start.8 = (f32[3,32,256]{2,1,0:T(8,128)S(1)}, f32[3,32,256]{2,1,0:T(8,128)S(1)}, u32[]{:S(2)}, u32[]{:S(2)}) collective-permute-start(f32[3,32,256]{2,1,0:T(8,128)S(1)} %get-tuple-element.42), channel_id=1, source_target_pairs={{0,8},{8,16},{16,24},{24,32},{32,40},{40,48},{48,56},{56,0},{1,9},... | collective-permute-start | bytes 294920 | tf_op jit(solution)/shard_map/ppermute | solution.py:521
  48.8 8.6 %collective-permute-start.9 = (f32[3,32,256]{2,1,0:T(8,128)S(1)}, f32[3,32,256]{2,1,0:T(8,128)S(1)}, u32[]{:S(2)}, u32[]{:S(2)}) collective-permute-start(f32[3,32,256]{2,1,0:T(8,128)S(1)} %get-tuple-element.43), channel_id=1, source_target_pairs={{0,56},{8,0},{16,8},{24,16},{32,24},{40,32},{48,40},{56,48},{1,57}... | collective-permute-start | bytes 294920 | tf_op jit(solution)/shard_map/ppermute | solution.py:521
  72.7 6.7 %collective-permute-start.16 = (f32[8,1536]{1,0:T(8,128)S(1)}, f32[8,1536]{1,0:T(8,128)S(1)}, u32[]{:S(2)}, u32[]{:S(2)}) collective-permute-start(f32[8,1536]{1,0:T(8,128)S(1)} %get-tuple-element.46.zhi_own), channel_id=1, source_target_pairs={{0,1},{1,2},{2,3},{3,4},{4,5},{5,6},{6,7},{7,0},{8,9},{9,10},{10,1... | collective-permute-start | bytes 147464 | tf_op jit(solution)/shard_map/ppermute | solution.py:521
  72.8 10.6 %collective-permute-start.12 = (f32[3,48,256]{2,1,0:T(8,128)S(1)}, f32[3,48,256]{2,1,0:T(8,128)S(1)}, u32[]{:S(2)}, u32[]{:S(2)}) collective-permute-start(f32[3,48,256]{2,1,0:T(8,128)S(1)} %get-tuple-element.47), channel_id=1, source_target_pairs={{0,64},{64,128},{128,192},{192,0},{1,65},{65,129},{129,193},{193,1... | collective-permute-start | bytes 442376 | tf_op jit(solution)/shard_map/ppermute | solution.py:521
  74.3 9.1 %collective-permute-start.13 = (f32[3,48,256]{2,1,0:T(8,128)S(1)}, f32[3,48,256]{2,1,0:T(8,128)S(1)}, u32[]{:S(2)}, u32[]{:S(2)}) collective-permute-start(f32[3,48,256]{2,1,0:T(8,128)S(1)} %get-tuple-element.48), channel_id=1, source_target_pairs={{0,192},{64,0},{128,64},{192,128},{1,193},{65,1},{129,65},{193,129... | collective-permute-start | bytes 442376 | tf_op jit(solution)/shard_map/ppermute | solution.py:521
  74.3 9.1 %collective-permute-start.14 = (f32[3,32,256]{2,1,0:T(8,128)S(1)}, f32[3,32,256]{2,1,0:T(8,128)S(1)}, u32[]{:S(2)}, u32[]{:S(2)}) collective-permute-start(f32[3,32,256]{2,1,0:T(8,128)S(1)} %get-tuple-element.49), channel_id=1, source_target_pairs={{0,8},{8,16},{16,24},{24,32},{32,40},{40,48},{48,56},{56,0},{1,9},... | collective-permute-start | bytes 294920 | tf_op jit(solution)/shard_map/ppermute | solution.py:521
  75.3 8.1 %collective-permute-start.15 = (f32[3,32,256]{2,1,0:T(8,128)S(1)}, f32[3,32,256]{2,1,0:T(8,128)S(1)}, u32[]{:S(2)}, u32[]{:S(2)}) collective-permute-start(f32[3,32,256]{2,1,0:T(8,128)S(1)} %get-tuple-element.50), channel_id=1, source_target_pairs={{0,56},{8,0},{16,8},{24,16},{32,24},{40,32},{48,40},{56,48},{1,57}... | collective-permute-start | bytes 294920 | tf_op jit(solution)/shard_map/ppermute | solution.py:521
  79.4 4.0 %collective-permute-start.17 = (f32[8,1536]{1,0:T(8,128)S(1)}, f32[8,1536]{1,0:T(8,128)S(1)}, u32[]{:S(2)}, u32[]{:S(2)}) collective-permute-start(f32[8,1536]{1,0:T(8,128)S(1)} %get-tuple-element.45.zlo_own), channel_id=1, source_target_pairs={{0,7},{1,0},{2,1},{3,2},{4,3},{5,4},{6,5},{7,6},{8,15},{9,8},{10,9... | collective-permute-start | bytes 147464 | tf_op jit(solution)/shard_map/ppermute | solution.py:521
  97.9 4.3 %collective-permute-start.18 = (f32[1,48,256]{2,1,0:T(8,128)S(1)}, f32[1,48,256]{2,1,0:T(8,128)S(1)}, u32[]{:S(2)}, u32[]{:S(2)}) collective-permute-start(f32[1,48,256]{2,1,0:T(8,128)S(1)} %slice.99), channel_id=1, source_target_pairs={{0,64},{64,128},{128,192},{192,0},{1,65},{65,129},{129,193},{193,1... | collective-permute-start | bytes 147464 | tf_op jit(solution)/shard_map/ppermute | solution.py:521
  102.0 3.5 %collective-permute-start.19 = (f32[1,48,256]{2,1,0:T(8,128)S(1)}, f32[1,48,256]{2,1,0:T(8,128)S(1)}, u32[]{:S(2)}, u32[]{:S(2)}) collective-permute-start(f32[1,48,256]{2,1,0:T(8,128)S(1)} %slice.100), channel_id=1, source_target_pairs={{0,192},{64,0},{128,64},{192,128},{1,193},{65,1},{129,65},{193,129... | collective-permute-start | bytes 147464 | tf_op jit(solution)/shard_map/ppermute | solution.py:521
  105.5 5.1 %collective-permute-start.21 = (f32[34,256]{1,0:T(8,128)S(1)}, f32[34,256]{1,0:T(8,128)S(1)}, u32[]{:S(2)}, u32[]{:S(2)}) collective-permute-start(f32[34,256]{1,0:T(8,128)S(1)} %pad_maximum_fusion.2), channel_id=1, source_target_pairs={{0,56},{8,0},{16,8},{24,16},{32,24},{40,32},{48,40},{56,48},{1,57}... | collective-permute-start | bytes 104456 | tf_op jit(solution)/shard_map/ppermute | solution.py:521
  109.5 6.5 %collective-permute-start.20 = (f32[34,256]{1,0:T(8,128)S(1)}, f32[34,256]{1,0:T(8,128)S(1)}, u32[]{:S(2)}, u32[]{:S(2)}) collective-permute-start(f32[34,256]{1,0:T(8,128)S(1)} %pad_maximum_fusion.1), channel_id=1, source_target_pairs={{0,8},{8,16},{16,24},{24,32},{32,40},{40,48},{48,56},{56,0},{1,9},... | collective-permute-start | bytes 104456 | tf_op jit(solution)/shard_map/ppermute | solution.py:521
  116.2 4.1 %collective-permute-start.22 = (f32[34,50]{1,0:T(8,128)S(1)}, f32[34,50]{1,0:T(8,128)S(1)}, u32[]{:S(2)}, u32[]{:S(2)}) collective-permute-start(f32[34,50]{1,0:T(8,128)S(1)} %pad_maximum_fusion.3), channel_id=1, source_target_pairs={{0,1},{1,2},{2,3},{3,4},{4,5},{5,6},{6,7},{7,0},{8,9},{9,10},{10,1... | collective-permute-start | bytes 20408 | tf_op jit(solution)/shard_map/ppermute | solution.py:521
  120.3 2.7 %collective-permute-start.23 = (f32[34,50]{1,0:T(8,128)S(1)}, f32[34,50]{1,0:T(8,128)S(1)}, u32[]{:S(2)}, u32[]{:S(2)}) collective-permute-start(f32[34,50]{1,0:T(8,128)S(1)} %get-tuple-element.77), channel_id=1, source_target_pairs={{0,7},{1,0},{2,1},{3,2},{4,3},{5,4},{6,5},{7,6},{8,15},{9,8},{10,9... | collective-permute-start | bytes 20408 | tf_op jit(solution)/shard_map/ppermute | solution.py:521
  128.4 13.1 %all-to-all-start = ((f32[5,32,2]{0,2,1:T(2,128)}), f32[5,32,2]{0,2,1:T(2,128)S(1)}, u32[]{:S(2)}, u32[]{:S(2)}) async-start(f32[5,32,2]{0,2,1:T(2,128)} %bitcast.22), calls=%async_computation | async-start | bytes 65536 | tf_op jit(solution)/shard_map/all_to_all | solution.py:583
  (10 other events, 7.3 us)
where the time goes:
time: 143 us; the launch traced here: 142 us
  Pallas kernels  49.6 us (35%)
  starting transfers between devices  48.7 us (34%)
  waiting for transfers between devices  27.3 us (19%)
  local copies, waits for them, and re-layouts  13.4 us (9%)
  between operations  1.62 us (1%)
  other arithmetic  1.48 us (1%)
    ppermute x24, starting transfers between devices, shift(): return lax.ppermute(value, axis, pairs)  42.8 us
    pallas_call x3, Pallas kernels, step(): pl.pallas_call(step_kernel, out_shape=[BLOCK] + FACES, in_specs=vmem_spec...  41.2 us
    ppermute x24, waiting for transfers between devices, shift(): return lax.ppermute(value, axis, pairs)  22.3 us
    unnamed x38, local copies, waits for them, and re-layouts  10.2 us
    all_to_all x1, starting transfers between devices, per_device(): lax.all_to_all(record[:5], ('gx', 'gy'), split_axis=1, concat_axis=1, til...  5.89 us
    all_to_all x1, waiting for transfers between devices, per_device(): lax.all_to_all(record[:5], ('gx', 'gy'), split_axis=1, concat_axis=1, til...  5 us
    pallas_call x1, Pallas kernels, bricks(): pl.pallas_call(brick_kernel, out_shape=jax.ShapeDtypeStruct((8, SLOTS), F...  4.65 us
  transfers between devices with their start and end apart: 25, of which 10 were waited for; matrix products, arithmetic and copies ran while one was open for 3% of the time, Pallas kernels for 2%

commit v1 on v0

--- a/solution.py
+++ b/solution.py
@@ -1,3 +1,5 @@
+import functools
+
 import jax
 import jax.numpy as jnp
 from jax import lax
@@ -11,10 +13,9 @@
 CX, CY, CZ = 32, 48, 256
 ROWS = CX * CY
 YT = CY // 8
-SUB = 2
 WENO_EPS = 1e-06
 F32 = jnp.float32
-VMEM_LIMIT = 48 * 1024 * 1024
+VMEM_LIMIT = 24 * 1024 * 1024
 
 
 def rcp(value):
@@ -22,10 +23,11 @@
 
 
 def smooth_weights(e_low, e_high, third):
-    base = third * third * (4.0 / 3.0) + WENO_EPS
-    q_a = rcp(e_low * (e_low - third) + base)
-    q_b = rcp(e_low * e_high + base)
-    q_c = rcp(e_high * (e_high + third) + base)
+    twice = third + third
+    middle = e_low * e_high + (third * third * (4.0 / 3.0) + WENO_EPS)
+    q_a = rcp(middle - e_low * twice)
+    q_b = rcp(middle)
+    q_c = rcp(middle + e_high * twice)
     return q_a * q_a, 6.0 * (q_b * q_b), q_c * q_c
 
 
@@ -36,12 +38,16 @@
     both = both + both
     total = (wa_next + wb) + wc_prev
     left = t_here + (both + y) * rcp(total + (wa_next + wa_next))
-    right = (both + x) * rcp(total + (wc_prev + wc_prev)) - t_here
+    right = t_here - (both + x) * rcp(total + (wc_prev + wc_prev))
     return left, right
 
 
 def upwind_square(centre, left, right, sigma):
-    best = jnp.maximum(sigma * (centre - left), (-sigma) * (centre + right))
+    return upwind_pair(centre - left, right - centre, sigma)
+
+
+def upwind_pair(left, right_back, sigma):
+    best = jnp.maximum(sigma * left, sigma * right_back)
     best = jnp.maximum(best, 0.0)
     return best * best
 
@@ -56,26 +62,32 @@
     return e_0, e_1, e_1 - e_0
 
 
-def z_column(even, odd, sigma_even, sigma_odd):
-    def down(part):
-        return pltpu.roll(part, 1, 1)
-
-    def up(part):
-        return pltpu.roll(part, 127, 1)
-
-    v = {-2: down(even), -1: down(odd), 0: even, 1: odd, 2: up(even), 3: up(odd)}
+def lane_down(part):
+    return pltpu.roll(part, 1, 1)
+
+
+def lane_up(part):
+    return pltpu.roll(part, 127, 1)
+
+
+def z_stage_weights(even, odd, even_down, odd_down, even_up, odd_up):
+    v = {-2: even_down, -1: odd_down, 0: even, 1: odd, 2: even_up, 3: odd_up}
     d = {k: v[k + 1] - v[k] for k in range(-2, 3)}
     e = {k: d[k] - d[k - 1] for k in range(-1, 3)}
     t = {k: e[k + 1] - e[k] for k in range(-1, 2)}
-    t[2] = up(t[0])
     w_0 = smooth_weights(e[0], e[1], t[0])
     w_1 = smooth_weights(e[1], e[2], t[1])
-    left_0, right_0 = biased_parts(w_1[0], w_0[1], down(w_1[2]), t[-1], t[0], t[1])
-    left_1, right_1 = biased_parts(up(w_0[0]), w_1[1], w_0[2], t[0], t[1], t[2])
     return (
-        upwind_square(3.0 * (d[-1] + d[0]), down(left_1), right_0, sigma_even),
-        upwind_square(3.0 * (d[0] + d[1]), left_0, right_1, sigma_odd),
+        w_1[0], w_0[1], lane_down(w_1[2]), t[-1], t[0], t[1],
+        lane_up(w_0[0]), w_1[1], w_0[2], lane_up(t[0]),
+        3.0 * (d[-1] + d[0]), 3.0 * (d[0] + d[1]),
     )
+
+
+def z_stage_parts(wa_0, wb_0, wc_0, t_m, t_0, t_1, wa_1, wb_1, wc_1, t_2, centre_0, centre_1):
+    left_0, right_0 = biased_parts(wa_0, wb_0, wc_0, t_m, t_0, t_1)
+    left_1, right_1 = biased_parts(wa_1, wb_1, wc_1, t_0, t_1, t_2)
+    return centre_0, lane_down(left_1), right_0 - centre_0, centre_1 - left_0, right_1 - centre_1
 
 
 def edge_column(window, u_ref, p_ref, u_row, p_row, sigma):
@@ -102,14 +114,7 @@
     )
 
 
-def write_faces(source, xlo, xhi, ylo, yhi, zlo, zhi):
-    xlo[...] = source[0:3]
-    xhi[...] = source[CX - 3 : CX]
-
-    for x in range(CX):
-        for k in range(3):
-            ylo[k, x : x + 1, :] = source[x, k : k + 1, :]
-            yhi[k, x : x + 1, :] = source[x, CY - 3 + k : CY - 2 + k, :]
+def z_faces(source, zlo, zhi):
     for chunk in range(CX // 8):
         columns = slice(8 * CY * chunk, 8 * CY * (chunk + 1))
         for parity in range(2):
@@ -120,7 +125,33 @@
                 zhi[2 * k + parity : 2 * k + parity + 1, columns] = part[124 + k : 125 + k]
 
 
-def pack_kernel(phi, mixed, xlo, xhi, ylo, yhi, zlo, zhi, turned):
+def y_faces(source, ylo, yhi, width):
+    for x in range(CX):
+        for k in range(width):
+            ylo[k, x : x + 1, :] = source[x, k : k + 1, :]
+            yhi[k, x : x + 1, :] = source[x, CY - width + k : CY - width + 1 + k, :]
+
+
+def write_swap(parity, low, high, out_a, out_b):
+    odd = parity == 1
+    out_a[...] = jnp.where(odd, low, high)
+    out_b[...] = jnp.where(odd, high, low)
+
+
+def write_faces(parity, source, xa, xb, ya, yb, za, zb, yf, zf):
+    y_faces(source, yf.at[0], yf.at[1], 3)
+    write_swap(parity[1], yf[0], yf[1], ya, yb)
+    write_swap(parity[0], source[0:3], source[CX - 3 : CX], xa, xb)
+    z_faces(source, zf.at[0], zf.at[1])
+    write_swap(parity[2], zf[0], zf[1], za, zb)
+
+
+def low_high(parity, part_a, part_b):
+    odd = parity == 1
+    return jnp.where(odd, part_a, part_b), jnp.where(odd, part_b, part_a)
+
+
+def pack_kernel(parity, phi, mixed, sigma, pace, xa, xb, ya, yb, za, zb, turned, yf, zf):
     for chunk in range(CX // 8):
         planes = slice(8 * chunk, 8 * chunk + 8)
         for half in range(2):
@@ -128,11 +159,18 @@
             part = part.reshape(8 * CY, 128).T
             for c in range(3):
                 turned[c, 128 * half : 128 * half + 128, :] = part[:, 128 * c : 128 * c + 128]
-        for parity in range(2):
-            part = [turned[c, pl.ds(parity, 128, stride=2), :].T for c in range(3)]
+        for which in range(2):
+            part = [turned[c, pl.ds(which, 128, stride=2), :].T for c in range(3)]
             part = jnp.concatenate(part, axis=0)
-            mixed[planes, :, 128 * parity : 128 * parity + 128] = part.reshape(8, CY, 128)
-    write_faces(mixed, xlo, xhi, ylo, yhi, zlo, zhi)
+            mixed[planes, :, 128 * which : 128 * which + 128] = part.reshape(8, CY, 128)
+    def signs(x, carry):
+        value = mixed[x]
+        sigma[x] = sigma_of(value)
+        pace[x] = (0.05 * value) * lax.rsqrt(value * value + 1.0)
+        return carry
+
+    lax.fori_loop(0, CX, signs, 0)
+    write_faces(parity, mixed, xa, xb, ya, yb, za, zb, yf, zf)
 
 
 def unpack_kernel(mixed, out, turned):
@@ -150,36 +188,42 @@
 
 
 def step_kernel(
-    phi0, zlo0, zhi0, v, zlo_own, zhi_own, x_low, x_high, y_low, y_high, z_low, z_high,
-    out, xlo, xhi, ylo, yhi, zlo, zhi,
-    vs, summed, u_ref, p_ref, window, zu_ref, zp_ref, edges, fixes,
+    last,
+    parity, sigma_in, pace, za0, zb0, v, za_own, zb_own, xa_in, xb_in, ya_in, yb_in, za_in, zb_in,
+    out, xa, xb, ya, yb, za, zb,
+    vs, summed, u_ref, p_ref, window, zu_ref, zp_ref, edges, fixes, yf, zf, xh,
+    rolled, zs, zp, tots,
 ):
     def fill(x, carry):
         for zt in range(2):
-            lanes = pl.ds(128 * zt, 128)
-            vs[zt, x, 8 : 8 + CY, :] = v[x, :, lanes]
+            vs[zt, x, 8 : 8 + CY, :] = v[x, :, pl.ds(128 * zt, 128)]
         return carry
 
     lax.fori_loop(0, CX, fill, 0)
+    yf[0], yf[1] = low_high(parity[1], ya_in[...], yb_in[...])
     for x in range(CX):
         for zt in range(2):
+            lanes = slice(128 * zt, 128 * zt + 128)
             for k in range(3):
-                lanes = slice(128 * zt, 128 * zt + 128)
-                vs[zt, x, 5 + k : 6 + k, :] = y_low[k, x : x + 1, lanes]
-                vs[zt, x, 8 + CY + k : 9 + CY + k, :] = y_high[k, x : x + 1, lanes]
-
-    window[pl.ds(5, 3), :] = z_low[5:8, :]
-    window[pl.ds(8, 8), :] = zlo_own[...]
-    fixed = edge_column(window, zu_ref, zp_ref, 6, 7, sigma_of(zlo0[...]))
-    for parity, lane_at, cell_at in ((0, 0, 0), (0, 1, 2), (1, 0, 1)):
-        edges[parity, lane_at : lane_at + 1, :] = fixed[cell_at : cell_at + 1]
-    window[pl.ds(8, 8), :] = zhi_own[...]
-    window[pl.ds(16, 3), :] = z_high[0:3, :]
-    fixed = edge_column(window, zu_ref, zp_ref, 9, 8, sigma_of(zhi0[...]))
-    for parity, lane_at, cell_at in ((0, 127, 6), (1, 126, 5), (1, 127, 7)):
-        edges[parity, lane_at : lane_at + 1, :] = fixed[cell_at : cell_at + 1]
-    for parity in range(2):
-        fixes[parity] = edges[parity].T
+                vs[zt, x, 5 + k : 6 + k, :] = yf[0, k, x : x + 1, lanes]
+                vs[zt, x, 8 + CY + k : 9 + CY + k, :] = yf[1, k, x : x + 1, lanes]
+    xh[0], xh[1] = low_high(parity[0], xa_in[...], xb_in[...])
+
+    z_low, z_high = low_high(parity[2], za_in[...], zb_in[...])
+    zlo0, zhi0 = low_high(parity[2], za0[...], zb0[...])
+    zlo_own, zhi_own = low_high(parity[2], za_own[...], zb_own[...])
+    window[5:8, :] = z_low[5:8]
+    window[8:16, :] = zlo_own
+    fixed = edge_column(window, zu_ref, zp_ref, 6, 7, sigma_of(zlo0))
+    for half, lane_at, cell_at in ((0, 0, 0), (0, 1, 2), (1, 0, 1)):
+        edges[half, lane_at : lane_at + 1, :] = fixed[cell_at : cell_at + 1]
+    window[8:16, :] = zhi_own
+    window[16:19, :] = z_high[0:3]
+    fixed = edge_column(window, zu_ref, zp_ref, 9, 8, sigma_of(zhi0))
+    for half, lane_at, cell_at in ((0, 127, 6), (1, 126, 5), (1, 127, 7)):
+        edges[half, lane_at : lane_at + 1, :] = fixed[cell_at : cell_at + 1]
+    for half in range(2):
+        fixes[half] = edges[half].T
 
     def x_pass(yt, carry):
         row = pl.multiple_of(8 * yt, 8)
@@ -188,9 +232,9 @@
 
             def cell(x):
                 if x < 0:
-                    return x_low[3 + x, pl.ds(row, 8), lanes]
+                    return xh[0, 3 + x, pl.ds(row, 8), lanes]
                 if x >= CX:
-                    return x_high[x - CX, pl.ds(row, 8), lanes]
+                    return xh[1, x - CX, pl.ds(row, 8), lanes]
                 return v[x, pl.ds(row, 8), lanes]
 
             d, e, t, weights, lefts, rights = {}, {}, {}, {}, {}, {}
@@ -208,7 +252,7 @@
                         weights[p + 1][0], weights[p][1], weights[p - 1][2], t[p - 1], t[p], t[p + 1]
                     )
                 if p >= 0:
-                    sigma = sigma_of(phi0[p, pl.ds(row, 8), lanes])
+                    sigma = sigma_in[p, pl.ds(row, 8), lanes]
                     centre = 3.0 * (d[p - 1] + d[p])
                     summed[zt, p, pl.ds(row, 8), :] = upwind_square(
                         centre, lefts[p - 1], rights[p], sigma
@@ -221,99 +265,142 @@
     fix_even = (lane < 2) | (lane == 127)
     fix_odd = (lane < 1) | (lane > 125)
 
-    def y_weights(x, sub, zt, k):
+    def y_weights(x, zt, k):
         start = 6 + 8 * k
         e_0, e_1, t = from_values(
             *[vs[zt, x, pl.ds(start + shift, 8), :] for shift in (-1, 0, 1, 2)]
         )
         w_a, w_b, w_c = smooth_weights(e_0, e_1, t)
         for slot, part in enumerate((w_a, w_b, w_c, t)):
-            u_ref[sub, zt, slot, pl.ds(8 * k, 8), :] = part
-
-    def y_parts(sub, zt, k):
+            u_ref[zt, slot, pl.ds(8 * k, 8), :] = part
+
+    def y_parts(zt, k):
         def read(slot, row):
-            return u_ref[sub, zt, slot, pl.ds(row, 8), :]
+            return u_ref[zt, slot, pl.ds(row, 8), :]
 
         row = 8 * k + 1
         left, right = biased_parts(
             read(0, row + 1), read(1, row), read(2, row - 1),
             read(3, row - 1), read(3, row), read(3, row + 1),
         )
-        p_ref[sub, zt, 0, pl.ds(8 * k, 8), :] = left
-        p_ref[sub, zt, 1, pl.ds(8 * k, 8), :] = right
-
-    def update(x, sub, k):
-        rows = pl.ds(8 * k, 8)
-        values, signs, sigmas, totals = [], [], [], []
+        p_ref[zt, 0, pl.ds(8 * k, 8), :] = left
+        p_ref[zt, 1, pl.ds(8 * k, 8), :] = right
+
+    def tile(x, zt, k):
+        return v[x, 8 * k : 8 * k + 8, 128 * zt : 128 * zt + 128]
+
+    def sigma_at(x, zt, k):
+        return sigma_in[x, 8 * k : 8 * k + 8, 128 * zt : 128 * zt + 128]
+
+    def stage_0(x):
+        for k in range(YT):
+            rows = slice(8 * k, 8 * k + 8)
+            for slot, part in enumerate((tile(x, 0, k), tile(x, 1, k))):
+                rolled[slot, rows, :] = lane_down(part)
+                rolled[2 + slot, rows, :] = lane_up(part)
         for zt in range(2):
-            phi = phi0[x, rows, pl.ds(128 * zt, 128)]
-            sigma = sigma_of(phi)
-            centre = 3.0 * (
-                vs[zt, x, pl.ds(9 + 8 * k, 8), :] - vs[zt, x, pl.ds(7 + 8 * k, 8), :]
+            for k in range(YT + 1):
+                y_weights(x, zt, k)
+
+    def stage_1(x):
+        for k in range(YT):
+            rows = slice(8 * k, 8 * k + 8)
+            parts = z_stage_weights(
+                tile(x, 0, k), tile(x, 1, k), *[rolled[slot, rows, :] for slot in range(4)]
             )
-            totals.append(
-                summed[zt, x, rows, :]
-                + upwind_square(
-                    centre, p_ref[sub, zt, 0, rows, :], p_ref[sub, zt, 1, pl.ds(8 * k + 1, 8), :], sigma
+            for slot, part in enumerate(parts):
+                zs[slot, rows, :] = part
+        for zt in range(2):
+            for k in range(YT + 1):
+                y_parts(zt, k)
+
+    def stage_2(x):
+        for k in range(YT):
+            rows = slice(8 * k, 8 * k + 8)
+            parts = z_stage_parts(*[zs[slot, rows, :] for slot in range(12)])
+            for slot, part in enumerate(parts):
+                zp[slot, rows, :] = part
+        for zt in range(2):
+            for k in range(YT):
+                rows = slice(8 * k, 8 * k + 8)
+                centre = 3.0 * (
+                    vs[zt, x, 9 + 8 * k : 17 + 8 * k, :] - vs[zt, x, 7 + 8 * k : 15 + 8 * k, :]
                 )
-            )
-            values.append(vs[zt, x, pl.ds(8 + 8 * k, 8), :])
-            sigmas.append(sigma)
-            signs.append(phi * lax.rsqrt(phi * phi + 1.0))
-        along = z_column(*values, *sigmas)
-        flat = pl.multiple_of(x * CY, 8) + 8 * k
-        along = (
-            jnp.where(fix_even, fixes[0, pl.ds(flat, 8), :], along[0]),
-            jnp.where(fix_odd, fixes[1, pl.ds(flat, 8), :], along[1]),
-        )
-        for zt in range(2):
-            total = totals[zt] + along[zt]
-            root = total * lax.rsqrt(jnp.maximum(total, 1e-30))
-            out[x, rows, pl.ds(128 * zt, 128)] = values[zt] - signs[zt] * (0.05 * root - 0.3)
-
-    def yz_pass(group, carry):
-        for sub in range(SUB):
+                tots[zt, rows, :] = summed[zt, x, rows, :] + upwind_square(
+                    centre, p_ref[zt, 0, rows, :], p_ref[zt, 1, 8 * k + 1 : 8 * k + 9, :],
+                    sigma_at(x, zt, k),
+                )
+
+    def stage_3(x):
+        flat = pl.multiple_of(x * CY, 8)
+        for k in range(YT):
+            rows = slice(8 * k, 8 * k + 8)
             for zt in range(2):
-                for k in range(YT + 1):
-                    y_weights(group * SUB + sub, sub, zt, k)
-        for sub in range(SUB):
-            for zt in range(2):
-                for k in range(YT + 1):
-                    y_parts(sub, zt, k)
-        for sub in range(SUB):
-            for k in range(YT):
-                update(group * SUB + sub, sub, k)
+                sigma = sigma_at(x, zt, k)
+                if zt == 0:
+                    along = upwind_pair(zp[0, rows, :] - zp[1, rows, :], zp[2, rows, :], sigma)
+                    edge = fix_even
+                else:
+                    along = upwind_pair(zp[3, rows, :], zp[4, rows, :], sigma)
+                    edge = fix_odd
+                along = jnp.where(edge, fixes[zt, pl.ds(flat + 8 * k, 8), :], along)
+                total = tots[zt, rows, :] + along
+                root = total * lax.rsqrt(jnp.maximum(total, 1e-30))
+                lanes = slice(128 * zt, 128 * zt + 128)
+                out[x, rows, lanes] = v[x, rows, lanes] - pace[x, rows, lanes] * (root - 6.0)
+
+    stages = (stage_3, stage_2, stage_1, stage_0)
+
+    def run(at, low, high):
+        for delay, stage in zip((3, 2, 1, 0), stages):
+            if low <= delay <= high:
+                stage(at - delay)
+
+    def yz_pass(at, carry):
+        run(at, 0, 3)
         return carry
 
-    lax.fori_loop(0, CX // SUB, yz_pass, 0)
-    write_faces(out, xlo, xhi, ylo, yhi, zlo, zhi)
-
-
-FACES = [
-    jax.ShapeDtypeStruct((3, CY, CZ), F32),
-    jax.ShapeDtypeStruct((3, CY, CZ), F32),
-    jax.ShapeDtypeStruct((3, CX, CZ), F32),
-    jax.ShapeDtypeStruct((3, CX, CZ), F32),
-    jax.ShapeDtypeStruct((8, ROWS), F32),
-    jax.ShapeDtypeStruct((8, ROWS), F32),
-]
+    for at in range(3):
+        run(at, 0, at)
+    lax.fori_loop(3, CX, yz_pass, 0)
+    for at in range(3):
+        run(CX + at, at + 1, 3)
+    if last:
+        xa_out, xb_out = (out[CX - 1 : CX], out[0:1])
+        write_swap(parity[0], xb_out, xa_out, xa, xb)
+        y_faces(out, ya, yb, 1)
+        z_faces(out, za, zb)
+    else:
+        write_faces(parity, out, xa, xb, ya, yb, za, zb, yf, zf)
+
+
+def face_shapes(width):
+    shapes = [(width, CY, CZ)] * 2 + [(width, CX, CZ)] * 2 + [(8, ROWS)] * 2
+    return [jax.ShapeDtypeStruct(shape, F32) for shape in shapes]
+
+
 BLOCK = jax.ShapeDtypeStruct((CX, CY, CZ), F32)
+FACE_SCRATCH = [pltpu.VMEM((2, 3, CX, CZ), F32), pltpu.VMEM((2, 8, ROWS), F32)]
 
 
 def vmem_specs(count):
     return [pl.BlockSpec(memory_space=pltpu.VMEM)] * count
 
 
-def pack(phi):
+def parity_specs(count):
+    return [pl.BlockSpec(memory_space=pltpu.SMEM)] + vmem_specs(count)
+
+
+def pack(parity, phi):
     return pl.pallas_call(
         pack_kernel,
-        out_shape=[BLOCK] + FACES,
-        in_specs=vmem_specs(1),
-        out_specs=vmem_specs(7),
-        scratch_shapes=[pltpu.VMEM((3, CZ, 128), F32)],
+        out_shape=[BLOCK] * 3 + face_shapes(3),
+        in_specs=parity_specs(1),
+        out_specs=vmem_specs(9),
+        scratch_shapes=[pltpu.VMEM((3, CZ, 128), F32)] + FACE_SCRATCH,
         compiler_params=pltpu.CompilerParams(vmem_limit_bytes=VMEM_LIMIT),
         name="pack",
-    )(phi)
+    )(parity, phi)
 
 
 def unpack(mixed):
@@ -328,26 +415,34 @@
     )(mixed)
 
 
-def step(phi0, zlo0, zhi0, v, zlo_own, zhi_own, halos):
+def step(parity, sigma_in, pace, za0, zb0, v, za_own, zb_own, halos, last):
     return pl.pallas_call(
-        step_kernel,
-        out_shape=[BLOCK] + FACES,
-        in_specs=vmem_specs(12),
+        functools.partial(step_kernel, last),
+        out_shape=[BLOCK] + face_shapes(1 if last else 3),
+        in_specs=parity_specs(13),
         out_specs=vmem_specs(7),
         scratch_shapes=[
             pltpu.VMEM((2, CX, 64, 128), F32),
             pltpu.VMEM((2, CX, CY, 128), F32),
-            pltpu.VMEM((SUB, 2, 4, 64, 128), F32),
-            pltpu.VMEM((SUB, 2, 2, 64, 128), F32),
+            pltpu.VMEM((2, 4, 64, 128), F32),
+            pltpu.VMEM((2, 2, 64, 128), F32),
             pltpu.VMEM((24, ROWS), F32),
             pltpu.VMEM((4, 24, ROWS), F32),
             pltpu.VMEM((2, 24, ROWS), F32),
             pltpu.VMEM((2, 128, ROWS), F32),
             pltpu.VMEM((2, ROWS, 128), F32),
+        ]
+        + FACE_SCRATCH
+        + [
+            pltpu.VMEM((2, 3, CY, CZ), F32),
+            pltpu.VMEM((4, CY, 128), F32),
+            pltpu.VMEM((12, CY, 128), F32),
+            pltpu.VMEM((5, CY, 128), F32),
+            pltpu.VMEM((2, CY, 128), F32),
         ],
         compiler_params=pltpu.CompilerParams(vmem_limit_bytes=VMEM_LIMIT),
         name="step",
-    )(phi0, zlo0, zhi0, v, zlo_own, zhi_own, *halos)
+    )(parity, sigma_in, pace, za0, zb0, v, za_own, zb_own, *halos)
 
 
 HALF_COS = [
@@ -515,9 +610,12 @@
     )(v, x_low, x_high, y_low, y_high, z_window, places, z_places)
 
 
-def shift(value, axis, direction):
+def swap(value, axis, phase):
     count = lax.axis_size(axis)
-    pairs = [(i, (i + direction) % count) for i in range(count)]
+    if phase == 0:
+        pairs = [(i, i ^ 1) for i in range(count)]
+    else:
+        pairs = [(i, (i - 1 if i % 2 == 0 else i + 1) % count) for i in range(count)]
     return lax.ppermute(value, axis, pairs)
 
 
@@ -544,30 +642,45 @@
 
 
 def exchange(faces):
-    xlo, xhi, ylo, yhi, zlo, zhi = faces
-    return (
-        shift(xhi, "gx", 1), shift(xlo, "gx", -1),
-        shift(yhi, "gy", 1), shift(ylo, "gy", -1),
-        shift(zhi, "gz", 1), shift(zlo, "gz", -1),
-    )
+    xa, xb, ya, yb, za, zb = faces
+    yb = swap(yb, "gy", 1)
+    ya = swap(ya, "gy", 0)
+    zb = swap(zb, "gz", 1)
+    za = swap(za, "gz", 0)
+    xb = swap(xb, "gx", 1)
+    xa = swap(xa, "gx", 0)
+    return xa, xb, ya, yb, za, zb
+
+
+def exchange_pair(low, high, axis, odd):
+    part_b = swap(jnp.where(odd, high, low), axis, 1)
+    part_a = swap(jnp.where(odd, low, high), axis, 0)
+    return jnp.where(odd, part_a, part_b), jnp.where(odd, part_b, part_a)
 
 
 def per_device(phi_start, band_ids, band_count, owners):
+    parity = jnp.stack([lax.axis_index(name) % 2 for name in ("gx", "gy", "gz")])
+    parity = parity.astype(jnp.int32)
+    odd_x, odd_y, odd_z = [parity[k] == 1 for k in range(3)]
     places, z_places = place_tables(
         band_ids.reshape(-1), band_count.reshape(()), owners.reshape(-1)
     )
-    phi0, *faces = pack(phi_start)
-    zlo0, zhi0 = faces[4:]
-    v = phi0
-    for _ in range(STEPS):
-        v, *faces = step(phi0, zlo0, zhi0, v, faces[4], faces[5], exchange(faces))
+    v, sigma, pace, *faces = pack(parity, phi_start)
+    za0, zb0 = faces[4:]
+    for number in range(STEPS):
+        v, *faces = step(
+            parity, sigma, pace, za0, zb0, v, faces[4], faces[5], exchange(faces),
+            number == STEPS - 1,
+        )
     level_set = unpack(v)
 
-    xlo, xhi, ylo, yhi, zlo, zhi = faces
-    x_low, x_high = shift(xhi[2:3], "gx", 1), shift(xlo[0:1], "gx", -1)
+    xa, xb, ylo, yhi, zlo, zhi = faces
+    xb = swap(xb, "gx", 1)
+    xa = swap(xa, "gx", 0)
+    x_low, x_high = jnp.where(odd_x, xa, xb), jnp.where(odd_x, xb, xa)
     first = jnp.concatenate([x_low[:, 0], ylo[0], x_high[:, 0]], axis=0)
-    last = jnp.concatenate([x_low[:, CY - 1], yhi[2], x_high[:, CY - 1]], axis=0)
-    y_low, y_high = shift(last, "gy", 1), shift(first, "gy", -1)
+    last = jnp.concatenate([x_low[:, CY - 1], yhi[0], x_high[:, CY - 1]], axis=0)
+    y_low, y_high = exchange_pair(first, last, "gy", odd_y)
 
     def plane(body, lane):
         middle = jnp.concatenate(
@@ -577,7 +690,7 @@
 
     bottom, above = plane(zlo[0], 0), plane(zlo[1], 128)
     below, top = plane(zhi[6], 127), plane(zhi[7], 255)
-    under, over = shift(top, "gz", 1), shift(bottom, "gz", -1)
+    under, over = exchange_pair(bottom, top, "gz", odd_z)
     z_window = jnp.stack([under, bottom, above, below, top, over], axis=0)
     record = bricks(v, x_low, x_high, y_low, y_high, z_window, places, z_places)
     totals = lax.all_to_all(record[:5], ("gx", "gy"), split_axis=1, concat_axis=1, tiled=True)

time: 143 us -> 143 us (level)
  local copies, waits for them, and re-layouts: 13.4 us -> 21.3 us
  starting transfers between devices: 48.7 us -> 44.7 us
  waiting for transfers between devices: 27.3 us -> 24.1 us
  Pallas kernels: 49.6 us -> 47.5 us
    unnamed x38 -> x53, local copies, waits for them, and re-layouts: 10.2 us -> 17.6 us
    ppermute x24, starting transfers between devices: 42.8 us -> 38.6 us  [swap(): return lax.ppermute(value, axis, pairs)]
    ppermute x24, waiting for transfers between devices: 22.3 us -> 19 us  [swap(): return lax.ppermute(value, axis, pairs)]
    pallas_call x4, Pallas kernels: 42.8 us -> 40.6 us  [the longest x3 37.1 us: step(): pl.pallas_call(functools.partial(step_kernel, last), out_shape=[BLOCK] +...]
  transfers between devices with their start and end apart: 25 -> 25, of which waited for: 10 -> 11; matrix products, arithmetic and copies ran while one was open for 3% -> 4% of each run, Pallas kernels for 2% -> 2%
where the time goes in v1:
time: 143 us; the launch traced here: 142 us
  Pallas kernels  47.5 us (33%)
  starting transfers between devices  44.7 us (31%)
  waiting for transfers between devices  24.1 us (17%)
  local copies, waits for them, and re-layouts  21.3 us (15%)
  other arithmetic  2.83 us (2%)
  between operations  1.6 us (1%)
    ppermute x24, starting transfers between devices, swap(): return lax.ppermute(value, axis, pairs)  38.6 us
    pallas_call x3, Pallas kernels, step(): pl.pallas_call(functools.partial(step_kernel, last), out_shape=[BLOCK] +...  37.1 us
    ppermute x24, waiting for transfers between devices, swap(): return lax.ppermute(value, axis, pairs)  19 us
    unnamed x53, local copies, waits for them, and re-layouts  17.6 us
    all_to_all x1, starting transfers between devices, per_device(): lax.all_to_all(record[:5], ('gx', 'gy'), split_axis=1, concat_axis=1, til...  6.13 us
    all_to_all x1, waiting for transfers between devices, per_device(): lax.all_to_all(record[:5], ('gx', 'gy'), split_axis=1, concat_axis=1, til...  5.02 us
    pallas_call x1, Pallas kernels, bricks(): pl.pallas_call(brick_kernel, out_shape=jax.ShapeDtypeStruct((8, SLOTS), F...  4.66 us
    pallas_call x1, Pallas kernels, pack(): pl.pallas_call(pack_kernel, out_shape=[BLOCK] * 3 + face_shapes(3), in_sp...  3.52 us
  transfers between devices with their start and end apart: 25, of which 11 were waited for; matrix products, arithmetic and copies ran while one was open for 4% of the time, Pallas kernels for 2%

profile of v1, /device:TPU:1, one launch (start us, length us, event | category | flops | bytes accessed | tf_op | source)
XLA Modules:
  0.0 142.0 jit_solution(12240945809642421354)
XLA Ops:
  0.8 1.4 copy-done.2
  2.2 3.5 %pack.1 = (f32[32,48,256]{2,1,0:T(8,128)S(1)}, f32[32,48,256]{2,1,0:T(8,128)S(1)}, f32[32,48,256]{2,1,0:T(8,128)S(1)}, f32[3,48,256]{2,1,0:T(8,128)}, f32[3,48,2...) custom-call(s32[3]{0:T(128)S(1)} %pad_add_fusion.parity, ...), custom_call_target="tpu_custom_call" | custom-call | tf_op jit(solution)/shard_map/pack/pallas_call | solution.py:395
  6.8 3.2 %collective-permute-start = (f32[3,48,256]{2,1,0:T(8,128)}, f32[3,48,256]{2,1,0:T(8,128)S(1)}, u32[]{:S(2)}, u32[]{:S(2)}) collective-permute-start(f32[3,48,256]{2,1,0:T(8,128)} %get-tuple-element.37), channel_id=1, source_target_pairs={{0,64},{64,0},{128,192},{192,128},{1,65},{65,1},{129,193},{193,129... | collective-permute-start | bytes 442376 | tf_op jit(solution)/shard_map/ppermute | solution.py:619
  10.1 1.8 %collective-permute-start.2 = (f32[3,32,256]{2,1,0:T(8,128)}, f32[3,32,256]{2,1,0:T(8,128)}, u32[]{:S(2)}, u32[]{:S(2)}) collective-permute-start(f32[3,32,256]{2,1,0:T(8,128)} %get-tuple-element.39), channel_id=1, source_target_pairs={{0,8},{8,0},{16,24},{24,16},{32,40},{40,32},{48,56},{56,48},{1,9},... | collective-permute-start | bytes 294920 | tf_op jit(solution)/shard_map/ppermute | solution.py:619
  11.9 3.0 %collective-permute-start.3 = (f32[3,32,256]{2,1,0:T(8,128)}, f32[3,32,256]{2,1,0:T(8,128)}, u32[]{:S(2)}, u32[]{:S(2)}) collective-permute-start(f32[3,32,256]{2,1,0:T(8,128)} %get-tuple-element.40), channel_id=1, source_target_pairs={{0,56},{8,16},{16,8},{24,32},{32,24},{40,48},{48,40},{56,0},{1,57}... | collective-permute-start | bytes 294920 | tf_op jit(solution)/shard_map/ppermute | solution.py:619
  14.9 1.6 %collective-permute-start.4 = (f32[8,1536]{1,0:T(8,128)S(1)}, f32[8,1536]{1,0:T(8,128)S(1)}, u32[]{:S(2)}, u32[]{:S(2)}) collective-permute-start(f32[8,1536]{1,0:T(8,128)S(1)} %get-tuple-element.34.za0.za_own), channel_id=1, source_target_pairs={{0,1},{1,0},{2,3},{3,2},{4,5},{5,4},{6,7},{7,6},{8,9},{9,8},{10,11... | collective-permute-start | bytes 147464 | tf_op jit(solution)/shard_map/ppermute | solution.py:619
  19.0 5.4 %collective-permute-start.5 = (f32[8,1536]{1,0:T(8,128)S(1)}, f32[8,1536]{1,0:T(8,128)}, u32[]{:S(2)}, u32[]{:S(2)}) collective-permute-start(f32[8,1536]{1,0:T(8,128)S(1)} %get-tuple-element.35.zb0.zb_own), channel_id=1, source_target_pairs={{0,7},{1,2},{2,1},{3,4},{4,3},{5,6},{6,5},{7,0},{8,15},{9,10},{10,... | collective-permute-start | bytes 147464 | tf_op jit(solution)/shard_map/ppermute | solution.py:619
  25.7 1.5 %copy.12 = f32[96,64]{1,0:T(8,128)} copy(f32[96,64]{0,1:T(8,128)} %convert_element_type.21) | data formatting | bytes 49152 | tf_op jit(solution)/shard_map/convert_element_type | solution.py:635
  27.2 1.4 copy-done.6
  29.4 12.1 %step.3 = (f32[32,48,256]{2,1,0:T(8,128)S(1)}, f32[3,48,256]{2,1,0:T(8,128)S(1)}, f32[3,48,256]{2,1,0:T(8,128)S(1)}, f32[3,32,256]{2,1,0:T(8,128)S(1)}, f32[3,32...) custom-call(s32[3]{0:T(128)S(1)} %pad_add_fusion.parity, ...), custom_call_target="tpu_custom_call" | custom-call | tf_op jit(solution)/shard_map/step/pallas_call | solution.py:419
  41.7 2.2 %collective-permute-start.6 = (f32[3,48,256]{2,1,0:T(8,128)S(1)}, f32[3,48,256]{2,1,0:T(8,128)S(1)}, u32[]{:S(2)}, u32[]{:S(2)}) collective-permute-start(f32[3,48,256]{2,1,0:T(8,128)S(1)} %get-tuple-element.44), channel_id=1, source_target_pairs={{0,64},{64,0},{128,192},{192,128},{1,65},{65,1},{129,193},{193,129... | collective-permute-start | bytes 442376 | tf_op jit(solution)/shard_map/ppermute | solution.py:619
  45.4 1.8 %collective-permute-start.9 = (f32[3,32,256]{2,1,0:T(8,128)S(1)}, f32[3,32,256]{2,1,0:T(8,128)S(1)}, u32[]{:S(2)}, u32[]{:S(2)}) collective-permute-start(f32[3,32,256]{2,1,0:T(8,128)S(1)} %get-tuple-element.47), channel_id=1, source_target_pairs={{0,56},{8,16},{16,8},{24,32},{32,24},{40,48},{48,40},{56,0},{1,57}... | collective-permute-start | bytes 294920 | tf_op jit(solution)/shard_map/ppermute | solution.py:619
  47.2 2.3 %collective-permute-start.11 = (f32[8,1536]{1,0:T(8,128)S(1)}, f32[8,1536]{1,0:T(8,128)S(1)}, u32[]{:S(2)}, u32[]{:S(2)}) collective-permute-start(f32[8,1536]{1,0:T(8,128)S(1)} %get-tuple-element.43.zb_own), channel_id=1, source_target_pairs={{0,7},{1,2},{2,1},{3,4},{4,3},{5,6},{6,5},{7,0},{8,15},{9,10},{10,... | collective-permute-start | bytes 147464 | tf_op jit(solution)/shard_map/ppermute | solution.py:619
  49.6 2.1 %collective-permute-done.11.zb_in = f32[8,1536]{1,0:T(8,128)S(1)} collective-permute-done((f32[8,1536]{1,0:T(8,128)S(1)}, f32[8,1536]{1,0:T(8,128)S(1)}, u32[]{:S(2)}, u32[]{:S(2)}) %collective-permute-start.11) | collective-permute-done | bytes 49184 | tf_op jit(solution)/shard_map/ppermute | solution.py:619
  51.7 2.9 %collective-permute-done.9.yb_in = f32[3,32,256]{2,1,0:T(8,128)S(1)} collective-permute-done((f32[3,32,256]{2,1,0:T(8,128)S(1)}, f32[3,32,256]{2,1,0:T(8,128)S(1)}, u32[]{:S(2)}, u32[]{:S(2)}) %collective-permute-start.9) | collective-permute-done | bytes 98336 | tf_op jit(solution)/shard_map/ppermute | solution.py:619
  56.2 12.3 %step.4 = (f32[32,48,256]{2,1,0:T(8,128)S(1)}, f32[3,48,256]{2,1,0:T(8,128)}, f32[3,48,256]{2,1,0:T(8,128)}, f32[3,32,256]{2,1,0:T(8,128)}, f32[3,32,256]{2,1,0:...) custom-call(s32[3]{0:T(128)S(1)} %pad_add_fusion.parity, f32[32,48,256]{2,1,0:T(8,128)S(1)} %get-tuple-element.32.sigma_in, ...), custom_call_target="tpu_custom_call" | custom-call | tf_op jit(solution)/shard_map/step/pallas_call | solution.py:419
  69.6 1.7 %collective-permute-start.16 = (f32[8,1536]{1,0:T(8,128)S(1)}, f32[8,1536]{1,0:T(8,128)S(1)}, u32[]{:S(2)}, u32[]{:S(2)}) collective-permute-start(f32[8,1536]{1,0:T(8,128)S(1)} %get-tuple-element.49.za_own), channel_id=1, source_target_pairs={{0,1},{1,0},{2,3},{3,2},{4,5},{5,4},{6,7},{7,6},{8,9},{9,8},{10,11... | collective-permute-start | bytes 147464 | tf_op jit(solution)/shard_map/ppermute | solution.py:619
  74.2 3.4 %collective-permute-start.15 = (f32[3,32,256]{2,1,0:T(8,128)}, f32[3,32,256]{2,1,0:T(8,128)}, u32[]{:S(2)}, u32[]{:S(2)}) collective-permute-start(f32[3,32,256]{2,1,0:T(8,128)} %get-tuple-element.54), channel_id=1, source_target_pairs={{0,56},{8,16},{16,8},{24,32},{32,24},{40,48},{48,40},{56,0},{1,57}... | collective-permute-start | bytes 294920 | tf_op jit(solution)/shard_map/ppermute | solution.py:619
  78.2 2.3 %collective-permute-start.17 = (f32[8,1536]{1,0:T(8,128)}, f32[8,1536]{1,0:T(8,128)}, u32[]{:S(2)}, u32[]{:S(2)}) collective-permute-start(f32[8,1536]{1,0:T(8,128)} %get-tuple-element.50.zb_own), channel_id=1, source_target_pairs={{0,7},{1,2},{2,1},{3,4},{4,3},{5,6},{6,5},{7,0},{8,15},{9,10},{10,... | collective-permute-start | bytes 147464 | tf_op jit(solution)/shard_map/ppermute | solution.py:619
  81.2 1.5 %collective-permute-done.17.zb_in = f32[8,1536]{1,0:T(8,128)} collective-permute-done((f32[8,1536]{1,0:T(8,128)}, f32[8,1536]{1,0:T(8,128)}, u32[]{:S(2)}, u32[]{:S(2)}) %collective-permute-start.17) | collective-permute-done | bytes 49184 | tf_op jit(solution)/shard_map/ppermute | solution.py:619
  82.7 3.2 %collective-permute-done.15.yb_in = f32[3,32,256]{2,1,0:T(8,128)} collective-permute-done((f32[3,32,256]{2,1,0:T(8,128)}, f32[3,32,256]{2,1,0:T(8,128)}, u32[]{:S(2)}, u32[]{:S(2)}) %collective-permute-start.15) | collective-permute-done | bytes 98336 | tf_op jit(solution)/shard_map/ppermute | solution.py:619
  85.9 1.4 copy-done.4
  90.5 12.7 %step.5 = (f32[32,48,256]{2,1,0:T(8,128)S(1)}, f32[1,48,256]{2,1,0:T(8,128)}, f32[1,48,256]{2,1,0:T(8,128)}, f32[1,32,256]{2,1,0:T(8,128)S(1)}, f32[1,32,256]{2,...) custom-call(s32[3]{0:T(128)S(1)} %pad_add_fusion.parity, f32[32,48,256]{2,1,0:T(8,128)S(1)} %get-tuple-element.32.sigma_in, ...), custom_call_target="tpu_custom_call" | custom-call | tf_op jit(solution)/shard_map/step/pallas_call | solution.py:419
  107.7 2.6 %collective-permute-done.19 = f32[1,48,256]{2,1,0:T(8,128)S(1)} collective-permute-done((f32[1,48,256]{2,1,0:T(8,128)}, f32[1,48,256]{2,1,0:T(8,128)S(1)}, u32[]{:S(2)}, u32[]{:S(2)}) %collective-permute-start.19) | collective-permute-done | bytes 49184 | tf_op jit(solution)/shard_map/ppermute | solution.py:619
  111.3 1.9 %collective-permute-start.21 = (f32[34,256]{1,0:T(8,128)S(1)}, f32[34,256]{1,0:T(8,128)S(1)}, u32[]{:S(2)}, u32[]{:S(2)}) collective-permute-start(f32[34,256]{1,0:T(8,128)S(1)} %get-tuple-element.87), channel_id=1, source_target_pairs={{0,56},{8,16},{16,8},{24,32},{32,24},{40,48},{48,40},{56,0},{1,57}... | collective-permute-start | bytes 104456 | tf_op jit(solution)/shard_map/ppermute | solution.py:619
  113.5 2.1 %collective-permute-done.20 = f32[34,256]{1,0:T(8,128)S(1)} collective-permute-done((f32[34,256]{1,0:T(8,128)S(1)}, f32[34,256]{1,0:T(8,128)S(1)}, u32[]{:S(2)}, u32[]{:S(2)}) %collective-permute-start.20) | collective-permute-done | bytes 34848 | tf_op jit(solution)/shard_map/ppermute | solution.py:619
  115.6 2.2 %collective-permute-done.21 = f32[34,256]{1,0:T(8,128)S(1)} collective-permute-done((f32[34,256]{1,0:T(8,128)S(1)}, f32[34,256]{1,0:T(8,128)S(1)}, u32[]{:S(2)}, u32[]{:S(2)}) %collective-permute-start.21) | collective-permute-done | bytes 34848 | tf_op jit(solution)/shard_map/ppermute | solution.py:619
  118.2 2.6 %collective-permute-start.23 = (f32[34,50]{1,0:T(8,128)S(1)}, f32[34,50]{1,0:T(8,128)S(1)}, u32[]{:S(2)}, u32[]{:S(2)}) collective-permute-start(f32[34,50]{1,0:T(8,128)S(1)} %get-tuple-element.80), channel_id=1, source_target_pairs={{0,7},{1,2},{2,1},{3,4},{4,3},{5,6},{6,5},{7,0},{8,15},{9,10},{10,... | collective-permute-start | bytes 20408 | tf_op jit(solution)/shard_map/ppermute | solution.py:619
  122.6 4.7 %bricks.1 = f32[8,64]{1,0:T(8,128)S(1)} custom-call(f32[32,48,256]{2,1,0:T(8,128)S(1)} %copy-done.1, f32[1,48,256]{2,1,0:T(8,128)S(1)} %get-tuple-element.84.x_low, f32[1,48,256]{2,1,0:T(8,128)S(1)} %get-tuple-element.83.x_high, f32[34,256]{1,0:T(8,128)S(1)} %get-tuple-element.86.y_low, f32[34,256]{1,0:T(8,128)S(1)} %get-tuple-element.85.y_high, ...), custom_call_target="tpu_custom_call" | custom-call | tf_op jit(solution)/shard_map/bricks/pallas_call | solution.py:599
  128.0 6.1 %all-to-all-start = ((f32[5,32,2]{0,2,1:T(2,128)}), f32[5,32,2]{0,2,1:T(2,128)S(1)}, u32[]{:S(2)}, u32[]{:S(2)}) async-start(f32[5,32,2]{0,2,1:T(2,128)} %bitcast.25), calls=%async_computation | async-start | bytes 65536 | tf_op jit(solution)/shard_map/all_to_all | solution.py:696
  134.1 2.2 %unpack.1 = f32[32,48,256]{2,1,0:T(8,128)} custom-call(f32[32,48,256]{2,1,0:T(8,128)S(1)} %copy-done.1), custom_call_target="tpu_custom_call" | custom-call | tf_op jit(solution)/shard_map/unpack/pallas_call | solution.py:407
  136.3 5.0 %all-to-all-done = f32[5,32,2]{0,2,1:T(2,128)S(1)} async-done(((f32[5,32,2]{0,2,1:T(2,128)}), f32[5,32,2]{0,2,1:T(2,128)S(1)}, u32[]{:S(2)}, u32[]{:S(2)}) %all-to-all-start) | async-done | bytes 1312 | tf_op jit(solution)/shard_map/all_to_all | solution.py:696
  (112 shorter events, 25.9 us)
Async XLA Ops:
  0.6 16.5 %copy-start.22 = (s32[1,1,1,64]{3,2,1,0:T(1,128)S(1)}, s32[1,1,1,64]{3,2,1,0:T(1,128)}, u32[]{:S(2)}) copy-start(s32[1,1,1,64]{3,2,1,0:T(1,128)} %param.7) | copy-start | bytes 772
  0.6 16.8 %copy-start.23 = (s32[1,1,1,64]{3,2,1,0:T(1,128)S(1)}, s32[1,1,1,64]{3,2,1,0:T(1,128)}, u32[]{:S(2)}) copy-start(s32[1,1,1,64]{3,2,1,0:T(1,128)} %param.5) | copy-start | bytes 772
  6.8 34.7 %copy-start.7 = (f32[8,1536]{1,0:T(8,128)}, f32[8,1536]{1,0:T(8,128)S(1)}, u32[]{:S(2)}) copy-start(f32[8,1536]{1,0:T(8,128)S(1)} %get-tuple-element.34.za0.za_own) | copy-start | bytes 147460
  6.8 34.7 %copy-start.10 = (f32[8,1536]{1,0:T(8,128)}, f32[8,1536]{1,0:T(8,128)S(1)}, u32[]{:S(2)}) copy-start(f32[8,1536]{1,0:T(8,128)S(1)} %get-tuple-element.35.zb0.zb_own) | copy-start | bytes 147460
  6.8 20.3 %collective-permute-start = (f32[3,48,256]{2,1,0:T(8,128)}, f32[3,48,256]{2,1,0:T(8,128)S(1)}, u32[]{:S(2)}, u32[]{:S(2)}) collective-permute-start(f32[3,48,256]{2,1,0:T(8,128)} %get-tuple-element.37), channel_id=1, source_target_pairs={{0,64},{64,0},{128,192},{192,128},{1,65},{65,1},{129,193},{193,129... | collective-permute-start | bytes 442376 | tf_op jit(solution)/shard_map/ppermute | solution.py:619
  10.1 17.1 %collective-permute-start.1 = (f32[3,48,256]{2,1,0:T(8,128)}, f32[3,48,256]{2,1,0:T(8,128)S(1)}, u32[]{:S(2)}, u32[]{:S(2)}) collective-permute-start(f32[3,48,256]{2,1,0:T(8,128)} %get-tuple-element.38), channel_id=1, source_target_pairs={{0,192},{64,128},{128,64},{192,0},{1,193},{65,129},{129,65},{193,1... | collective-permute-start | bytes 442376 | tf_op jit(solution)/shard_map/ppermute | solution.py:619
  10.1 17.1 %collective-permute-start.2 = (f32[3,32,256]{2,1,0:T(8,128)}, f32[3,32,256]{2,1,0:T(8,128)}, u32[]{:S(2)}, u32[]{:S(2)}) collective-permute-start(f32[3,32,256]{2,1,0:T(8,128)} %get-tuple-element.39), channel_id=1, source_target_pairs={{0,8},{8,0},{16,24},{24,16},{32,40},{40,32},{48,56},{56,48},{1,9},... | collective-permute-start | bytes 294920 | tf_op jit(solution)/shard_map/ppermute | solution.py:619
  11.9 15.3 %collective-permute-start.3 = (f32[3,32,256]{2,1,0:T(8,128)}, f32[3,32,256]{2,1,0:T(8,128)}, u32[]{:S(2)}, u32[]{:S(2)}) collective-permute-start(f32[3,32,256]{2,1,0:T(8,128)} %get-tuple-element.40), channel_id=1, source_target_pairs={{0,56},{8,16},{16,8},{24,32},{32,24},{40,48},{48,40},{56,0},{1,57}... | collective-permute-start | bytes 294920 | tf_op jit(solution)/shard_map/ppermute | solution.py:619
  14.9 3.5 %collective-permute-start.4 = (f32[8,1536]{1,0:T(8,128)S(1)}, f32[8,1536]{1,0:T(8,128)S(1)}, u32[]{:S(2)}, u32[]{:S(2)}) collective-permute-start(f32[8,1536]{1,0:T(8,128)S(1)} %get-tuple-element.34.za0.za_own), channel_id=1, source_target_pairs={{0,1},{1,0},{2,3},{3,2},{4,5},{5,4},{6,7},{7,6},{8,9},{9,8},{10,11... | collective-permute-start | bytes 147464 | tf_op jit(solution)/shard_map/ppermute | solution.py:619
  19.0 8.2 %collective-permute-start.5 = (f32[8,1536]{1,0:T(8,128)S(1)}, f32[8,1536]{1,0:T(8,128)}, u32[]{:S(2)}, u32[]{:S(2)}) collective-permute-start(f32[8,1536]{1,0:T(8,128)S(1)} %get-tuple-element.35.zb0.zb_own), channel_id=1, source_target_pairs={{0,7},{1,2},{2,1},{3,4},{4,3},{5,6},{6,5},{7,0},{8,15},{9,10},{10,... | collective-permute-start | bytes 147464 | tf_op jit(solution)/shard_map/ppermute | solution.py:619
  27.2 1.4 copy-start.6
  29.4 12.2 %copy-start.21 = (f32[96,64]{1,0:T(8,128)S(1)}, f32[96,64]{1,0:T(8,128)}, u32[]{:S(2)}) copy-start(f32[96,64]{1,0:T(8,128)} %copy.12) | copy-start | bytes 73732
  41.5 5.7 %collective-permute-start.10 = (f32[8,1536]{1,0:T(8,128)S(1)}, f32[8,1536]{1,0:T(8,128)S(1)}, u32[]{:S(2)}, u32[]{:S(2)}) collective-permute-start(f32[8,1536]{1,0:T(8,128)S(1)} %get-tuple-element.42.za_own), channel_id=1, source_target_pairs={{0,1},{1,0},{2,3},{3,2},{4,5},{5,4},{6,7},{7,6},{8,9},{9,8},{10,11... | collective-permute-start | bytes 147464 | tf_op jit(solution)/shard_map/ppermute | solution.py:619
  41.7 12.9 %collective-permute-start.6 = (f32[3,48,256]{2,1,0:T(8,128)S(1)}, f32[3,48,256]{2,1,0:T(8,128)S(1)}, u32[]{:S(2)}, u32[]{:S(2)}) collective-permute-start(f32[3,48,256]{2,1,0:T(8,128)S(1)} %get-tuple-element.44), channel_id=1, source_target_pairs={{0,64},{64,0},{128,192},{192,128},{1,65},{65,1},{129,193},{193,129... | collective-permute-start | bytes 442376 | tf_op jit(solution)/shard_map/ppermute | solution.py:619
  43.8 10.7 %collective-permute-start.7 = (f32[3,48,256]{2,1,0:T(8,128)S(1)}, f32[3,48,256]{2,1,0:T(8,128)S(1)}, u32[]{:S(2)}, u32[]{:S(2)}) collective-permute-start(f32[3,48,256]{2,1,0:T(8,128)S(1)} %get-tuple-element.45), channel_id=1, source_target_pairs={{0,192},{64,128},{128,64},{192,0},{1,193},{65,129},{129,65},{193,1... | collective-permute-start | bytes 442376 | tf_op jit(solution)/shard_map/ppermute | solution.py:619
  44.1 7.6 %collective-permute-start.8 = (f32[3,32,256]{2,1,0:T(8,128)S(1)}, f32[3,32,256]{2,1,0:T(8,128)S(1)}, u32[]{:S(2)}, u32[]{:S(2)}) collective-permute-start(f32[3,32,256]{2,1,0:T(8,128)S(1)} %get-tuple-element.46), channel_id=1, source_target_pairs={{0,8},{8,0},{16,24},{24,16},{32,40},{40,32},{48,56},{56,48},{1,9},... | collective-permute-start | bytes 294920 | tf_op jit(solution)/shard_map/ppermute | solution.py:619
  45.4 9.2 %collective-permute-start.9 = (f32[3,32,256]{2,1,0:T(8,128)S(1)}, f32[3,32,256]{2,1,0:T(8,128)S(1)}, u32[]{:S(2)}, u32[]{:S(2)}) collective-permute-start(f32[3,32,256]{2,1,0:T(8,128)S(1)} %get-tuple-element.47), channel_id=1, source_target_pairs={{0,56},{8,16},{16,8},{24,32},{32,24},{40,48},{48,40},{56,0},{1,57}... | collective-permute-start | bytes 294920 | tf_op jit(solution)/shard_map/ppermute | solution.py:619
  47.2 4.4 %collective-permute-start.11 = (f32[8,1536]{1,0:T(8,128)S(1)}, f32[8,1536]{1,0:T(8,128)S(1)}, u32[]{:S(2)}, u32[]{:S(2)}) collective-permute-start(f32[8,1536]{1,0:T(8,128)S(1)} %get-tuple-element.43.zb_own), channel_id=1, source_target_pairs={{0,7},{1,2},{2,1},{3,4},{4,3},{5,6},{6,5},{7,0},{8,15},{9,10},{10,... | collective-permute-start | bytes 147464 | tf_op jit(solution)/shard_map/ppermute | solution.py:619
  69.6 8.0 %collective-permute-start.16 = (f32[8,1536]{1,0:T(8,128)S(1)}, f32[8,1536]{1,0:T(8,128)S(1)}, u32[]{:S(2)}, u32[]{:S(2)}) collective-permute-start(f32[8,1536]{1,0:T(8,128)S(1)} %get-tuple-element.49.za_own), channel_id=1, source_target_pairs={{0,1},{1,0},{2,3},{3,2},{4,5},{5,4},{6,7},{7,6},{8,9},{9,8},{10,11... | collective-permute-start | bytes 147464 | tf_op jit(solution)/shard_map/ppermute | solution.py:619
  72.0 13.9 %collective-permute-start.12 = (f32[3,48,256]{2,1,0:T(8,128)}, f32[3,48,256]{2,1,0:T(8,128)}, u32[]{:S(2)}, u32[]{:S(2)}) collective-permute-start(f32[3,48,256]{2,1,0:T(8,128)} %get-tuple-element.51), channel_id=1, source_target_pairs={{0,64},{64,0},{128,192},{192,128},{1,65},{65,1},{129,193},{193,129... | collective-permute-start | bytes 442376 | tf_op jit(solution)/shard_map/ppermute | solution.py:619
  73.2 12.7 %collective-permute-start.13 = (f32[3,48,256]{2,1,0:T(8,128)}, f32[3,48,256]{2,1,0:T(8,128)}, u32[]{:S(2)}, u32[]{:S(2)}) collective-permute-start(f32[3,48,256]{2,1,0:T(8,128)} %get-tuple-element.52), channel_id=1, source_target_pairs={{0,192},{64,128},{128,64},{192,0},{1,193},{65,129},{129,65},{193,1... | collective-permute-start | bytes 442376 | tf_op jit(solution)/shard_map/ppermute | solution.py:619
  73.4 9.3 %collective-permute-start.14 = (f32[3,32,256]{2,1,0:T(8,128)}, f32[3,32,256]{2,1,0:T(8,128)}, u32[]{:S(2)}, u32[]{:S(2)}) collective-permute-start(f32[3,32,256]{2,1,0:T(8,128)} %get-tuple-element.53), channel_id=1, source_target_pairs={{0,8},{8,0},{16,24},{24,16},{32,40},{40,32},{48,56},{56,48},{1,9},... | collective-permute-start | bytes 294920 | tf_op jit(solution)/shard_map/ppermute | solution.py:619
  74.2 11.7 %collective-permute-start.15 = (f32[3,32,256]{2,1,0:T(8,128)}, f32[3,32,256]{2,1,0:T(8,128)}, u32[]{:S(2)}, u32[]{:S(2)}) collective-permute-start(f32[3,32,256]{2,1,0:T(8,128)} %get-tuple-element.54), channel_id=1, source_target_pairs={{0,56},{8,16},{16,8},{24,32},{32,24},{40,48},{48,40},{56,0},{1,57}... | collective-permute-start | bytes 294920 | tf_op jit(solution)/shard_map/ppermute | solution.py:619
  78.2 4.5 %collective-permute-start.17 = (f32[8,1536]{1,0:T(8,128)}, f32[8,1536]{1,0:T(8,128)}, u32[]{:S(2)}, u32[]{:S(2)}) collective-permute-start(f32[8,1536]{1,0:T(8,128)} %get-tuple-element.50.zb_own), channel_id=1, source_target_pairs={{0,7},{1,2},{2,1},{3,4},{4,3},{5,6},{6,5},{7,0},{8,15},{9,10},{10,... | collective-permute-start | bytes 147464 | tf_op jit(solution)/shard_map/ppermute | solution.py:619
  105.6 17.0 %copy-start.1 = (f32[32,48,256]{2,1,0:T(8,128)S(1)}, f32[32,48,256]{2,1,0:T(8,128)}, u32[]{:S(2)}) copy-start(f32[32,48,256]{2,1,0:T(8,128)} %copy-done) | copy-start | bytes 4718596
  105.6 2.1 %collective-permute-start.18 = (f32[1,48,256]{2,1,0:T(8,128)}, f32[1,48,256]{2,1,0:T(8,128)S(1)}, u32[]{:S(2)}, u32[]{:S(2)}) collective-permute-start(f32[1,48,256]{2,1,0:T(8,128)} %get-tuple-element.56), channel_id=1, source_target_pairs={{0,64},{64,0},{128,192},{192,128},{1,65},{65,1},{129,193},{193,129... | collective-permute-start | bytes 147464 | tf_op jit(solution)/shard_map/ppermute | solution.py:619
  106.6 3.7 %collective-permute-start.19 = (f32[1,48,256]{2,1,0:T(8,128)}, f32[1,48,256]{2,1,0:T(8,128)S(1)}, u32[]{:S(2)}, u32[]{:S(2)}) collective-permute-start(f32[1,48,256]{2,1,0:T(8,128)} %get-tuple-element.57), channel_id=1, source_target_pairs={{0,192},{64,128},{128,64},{192,0},{1,193},{65,129},{129,65},{193,1... | collective-permute-start | bytes 147464 | tf_op jit(solution)/shard_map/ppermute | solution.py:619
  111.2 4.4 %collective-permute-start.20 = (f32[34,256]{1,0:T(8,128)S(1)}, f32[34,256]{1,0:T(8,128)S(1)}, u32[]{:S(2)}, u32[]{:S(2)}) collective-permute-start(f32[34,256]{1,0:T(8,128)S(1)} %get-tuple-element.88), channel_id=1, source_target_pairs={{0,8},{8,0},{16,24},{24,16},{32,40},{40,32},{48,56},{56,48},{1,9},... | collective-permute-start | bytes 104456 | tf_op jit(solution)/shard_map/ppermute | solution.py:619
  111.3 6.6 %collective-permute-start.21 = (f32[34,256]{1,0:T(8,128)S(1)}, f32[34,256]{1,0:T(8,128)S(1)}, u32[]{:S(2)}, u32[]{:S(2)}) collective-permute-start(f32[34,256]{1,0:T(8,128)S(1)} %get-tuple-element.87), channel_id=1, source_target_pairs={{0,56},{8,16},{16,8},{24,32},{32,24},{40,48},{48,40},{56,0},{1,57}... | collective-permute-start | bytes 104456 | tf_op jit(solution)/shard_map/ppermute | solution.py:619
  118.1 3.6 %collective-permute-start.22 = (f32[34,50]{1,0:T(8,128)S(1)}, f32[34,50]{1,0:T(8,128)S(1)}, u32[]{:S(2)}, u32[]{:S(2)}) collective-permute-start(f32[34,50]{1,0:T(8,128)S(1)} %broadcast_select_fusion.5), channel_id=1, source_target_pairs={{0,1},{1,0},{2,3},{3,2},{4,5},{5,4},{6,7},{7,6},{8,9},{9,8},{10,11... | collective-permute-start | bytes 20408 | tf_op jit(solution)/shard_map/ppermute | solution.py:619
  118.2 4.2 %collective-permute-start.23 = (f32[34,50]{1,0:T(8,128)S(1)}, f32[34,50]{1,0:T(8,128)S(1)}, u32[]{:S(2)}, u32[]{:S(2)}) collective-permute-start(f32[34,50]{1,0:T(8,128)S(1)} %get-tuple-element.80), channel_id=1, source_target_pairs={{0,7},{1,2},{2,1},{3,4},{4,3},{5,6},{6,5},{7,0},{8,15},{9,10},{10,... | collective-permute-start | bytes 20408 | tf_op jit(solution)/shard_map/ppermute | solution.py:619
  128.0 13.4 %all-to-all-start = ((f32[5,32,2]{0,2,1:T(2,128)}), f32[5,32,2]{0,2,1:T(2,128)S(1)}, u32[]{:S(2)}, u32[]{:S(2)}) async-start(f32[5,32,2]{0,2,1:T(2,128)} %bitcast.25), calls=%async_computation | async-start | bytes 65536 | tf_op jit(solution)/shard_map/all_to_all | solution.py:696
  (17 other events, 14.9 us)

commit v2 on v1

--- a/solution.py
+++ b/solution.py
@@ -15,7 +15,7 @@
 YT = CY // 8
 WENO_EPS = 1e-06
 F32 = jnp.float32
-VMEM_LIMIT = 24 * 1024 * 1024
+VMEM_LIMIT = 16 * 1024 * 1024
 
 
 def rcp(value):
@@ -190,10 +190,22 @@
 def step_kernel(
     last,
     parity, sigma_in, pace, za0, zb0, v, za_own, zb_own, xa_in, xb_in, ya_in, yb_in, za_in, zb_in,
-    out, xa, xb, ya, yb, za, zb,
+    *refs,
+):
+    faces = 6 if last else 7
+    step_body(last, parity, sigma_in, pace, za0, zb0, v, za_own, zb_own, xa_in, xb_in, ya_in,
+              yb_in, za_in, zb_in, refs[:faces], *refs[faces:])
+
+
+def step_body(
+    last,
+    parity, sigma_in, pace, za0, zb0, v, za_own, zb_own, xa_in, xb_in, ya_in, yb_in, za_in, zb_in,
+    outs,
     vs, summed, u_ref, p_ref, window, zu_ref, zp_ref, edges, fixes, yf, zf, xh,
     rolled, zs, zp, tots,
 ):
+    out = outs[0]
+
     def fill(x, carry):
         for zt in range(2):
             vs[zt, x, 8 : 8 + CY, :] = v[x, :, pl.ds(128 * zt, 128)]
@@ -366,17 +378,85 @@
     for at in range(3):
         run(CX + at, at + 1, 3)
     if last:
-        xa_out, xb_out = (out[CX - 1 : CX], out[0:1])
-        write_swap(parity[0], xb_out, xa_out, xa, xb)
-        y_faces(out, ya, yb, 1)
-        z_faces(out, za, zb)
+        xa, xb, ylo, yhi, planes = outs[1:]
+        write_swap(parity[0], out[0:1], out[CX - 1 : CX], xa, xb)
+        y_faces(out, ylo, yhi, 1)
+        planes[...] = jnp.zeros((4, CX, 128), F32)
+        for chunk in range(CX // 8):
+            for half in range(2):
+                part = out[8 * chunk : 8 * chunk + 8, :, 128 * half : 128 * half + 128]
+                part = part.reshape(8 * CY, 128).T
+                for x in range(8):
+                    lanes = slice(CY * x, CY * x + CY)
+                    at = slice(8 * chunk + x, 8 * chunk + x + 1)
+                    planes[half, at, 0:CY] = part[0:1, lanes]
+                    planes[2 + half, at, 0:CY] = part[127:128, lanes]
     else:
-        write_faces(parity, out, xa, xb, ya, yb, za, zb, yf, zf)
+        write_faces(parity, out, *outs[1:], yf, zf)
+
+
+def rows_kernel(parity, xa, xb, ylo, yhi, ya, yb, ext):
+    x_low, x_high = low_high(parity[0], xa[0], xb[0])
+    for side, (source, row) in enumerate(((ylo, 0), (yhi, CY - 1))):
+        ext[side, 0:1, :] = x_low[row : row + 1]
+        ext[side, 1 : CX + 1, :] = source[0]
+        ext[side, CX + 1 : CX + 2, :] = x_high[row : row + 1]
+    write_swap(parity[1], ext[0], ext[1], ya, yb)
+
+
+def planes_kernel(parity, xa, xb, ya, yb, own, planes, za, zb):
+    x_sides = low_high(parity[0], xa[0], xb[0])
+    y_low, y_high = low_high(parity[1], ya[...], yb[...])
+    planes[...] = jnp.zeros((4, 40, 128), F32)
+    for q in range(4):
+        planes[q, 1 : CX + 1, :] = own[q]
+    for side in range(2):
+        row = (CX + 1) * side
+        for half in range(2):
+            turned = x_sides[side][:, 128 * half : 128 * half + 128].T
+            planes[half, row : row + 1, 0:CY] = turned[0:1]
+            planes[2 + half, row : row + 1, 0:CY] = turned[127:128]
+    lane = lax.broadcasted_iota(jnp.int32, (CX + 2, 128), 1)
+    for q in range(4):
+        lanes = slice(128 * (q % 2), 128 * (q % 2) + 128)
+        start = 0 if q < 2 else 127
+        low = y_low[:, lanes]
+        if start != 127:
+            low = pltpu.roll(low, 127 - start, 1)
+        high = pltpu.roll(y_high[:, lanes], (CY - start) % 128, 1)
+        planes[q, 0 : CX + 2, :] = jnp.where(
+            lane == 127, low, jnp.where(lane == CY, high, planes[q, 0 : CX + 2, :])
+        )
+    write_swap(parity[2], planes[0], planes[3], za, zb)
 
 
 def face_shapes(width):
-    shapes = [(width, CY, CZ)] * 2 + [(width, CX, CZ)] * 2 + [(8, ROWS)] * 2
+    shapes = [(width, CY, CZ)] * 2 + [(width, CX, CZ)] * 2
+    shapes += [(8, ROWS)] * 2 if width == 3 else [(4, CX, 128)]
     return [jax.ShapeDtypeStruct(shape, F32) for shape in shapes]
+
+
+def row_faces(parity, xa, xb, ylo, yhi):
+    return pl.pallas_call(
+        rows_kernel,
+        out_shape=[jax.ShapeDtypeStruct((CX + 2, CZ), F32)] * 2,
+        in_specs=parity_specs(4),
+        out_specs=vmem_specs(2),
+        scratch_shapes=[pltpu.VMEM((2, CX + 2, CZ), F32)],
+        compiler_params=pltpu.CompilerParams(vmem_limit_bytes=VMEM_LIMIT),
+        name="row_faces",
+    )(parity, xa, xb, ylo, yhi)
+
+
+def plane_faces(parity, xa, xb, ya, yb, own):
+    return pl.pallas_call(
+        planes_kernel,
+        out_shape=[jax.ShapeDtypeStruct(shape, F32) for shape in ((4, 40, 128), (40, 128), (40, 128))],
+        in_specs=parity_specs(5),
+        out_specs=vmem_specs(3),
+        compiler_params=pltpu.CompilerParams(vmem_limit_bytes=VMEM_LIMIT),
+        name="plane_faces",
+    )(parity, xa, xb, ya, yb, own)
 
 
 BLOCK = jax.ShapeDtypeStruct((CX, CY, CZ), F32)
@@ -420,7 +500,7 @@
         functools.partial(step_kernel, last),
         out_shape=[BLOCK] + face_shapes(1 if last else 3),
         in_specs=parity_specs(13),
-        out_specs=vmem_specs(7),
+        out_specs=vmem_specs(6 if last else 7),
         scratch_shapes=[
             pltpu.VMEM((2, CX, 64, 128), F32),
             pltpu.VMEM((2, CX, CY, 128), F32),
@@ -480,7 +560,37 @@
     )
 
 
-def brick_kernel(v, x_low, x_high, y_low, y_high, z_window, places, z_places, record, vs, stack):
+def brick_tables(ids, targets, live_count):
+    entry = lax.broadcasted_iota(jnp.int32, (1, SLOTS), 1)
+    live = entry < live_count
+    row = lax.broadcasted_iota(jnp.int32, (SLOTS, SLOTS), 0)
+    column = lax.broadcasted_iota(jnp.int32, (SLOTS, SLOTS), 1)
+    owner = targets.astype(F32)
+    down = jnp.sum(jnp.where(row == column, owner, 0.0), axis=1, keepdims=True)
+    earlier = (row < column) & (row < live_count) & (down == owner)
+    rank = jnp.sum(earlier.astype(F32), axis=0, keepdims=True)
+    slot = jnp.where(live, 2.0 * owner + rank, F32(SLOTS))
+    to_slot = (slot == row.astype(F32)).astype(F32)
+
+    def finder(count, brick_of):
+        at = lax.broadcasted_iota(jnp.int32, (count, SLOTS), 0)
+        return (ids == brick_of(at)).astype(F32)
+
+    return to_slot, finder
+
+
+def exact_dot(left, right, dims=(((1,), (0,)), ((), ()))):
+    return lax.dot_general(
+        left, right, dims, precision=lax.Precision.HIGHEST, preferred_element_type=F32
+    )
+
+
+def brick_kernel(
+    parity, count, v, xa, xb, ya, yb, za, zb, planes, ids, targets, record, vs, stack
+):
+    x_low, x_high = low_high(parity[0], xa[...], xb[...])
+    y_low, y_high = low_high(parity[1], ya[...], yb[...])
+    under, over = low_high(parity[2], za[...], zb[...])
     def fill(x, carry):
         for zt in range(2):
             vs[zt, x + 1, 8 : 8 + CY, :] = v[x, :, pl.ds(128 * zt, 128)]
@@ -561,45 +671,50 @@
             row = 8 * (3 * bx + by)
             stack[row + 5 : row + 8, :] = jnp.zeros((3, 128), F32)
 
-    total = jnp.zeros((8, SLOTS), F32)
+    to_slot, finder = brick_tables(ids[...], targets[...], count[0])
+    found = jnp.zeros((8, SLOTS), F32)
     for b in range(6):
-        total = total + jnp.dot(
-            stack[8 * b : 8 * b + 8, :], places[b],
-            precision=lax.Precision.HIGHEST, preferred_element_type=F32,
+        found = found + exact_dot(
+            stack[8 * b : 8 * b + 8, :], finder(128, lambda at: 16 * b + at // 8)
         )
     for side in range(2):
-        planes = [z_window[3 * side + k] for k in range(3)]
+        window = (under, planes[0], planes[1]) if side == 0 else (planes[2], planes[3], over)
 
         def cut(plane, step_x, step_y):
-            return planes[plane][1 + step_x : 33 + step_x, 1 + step_y : 49 + step_y]
+            part = window[plane][1 + step_x : 33 + step_x]
+            return pltpu.roll(part, (-step_y) % 128, 1) if step_y else part
 
         high, low = cut(1, 1, 0), cut(1, -1, 0)
         right, left = cut(1, 0, 1), cut(1, 0, -1)
-        over, under = cut(2, 0, 0), cut(0, 0, 0)
+        above, below = cut(2, 0, 0), cut(0, 0, 0)
         terms = five_terms(
             cut(1, 0, 0), None,
-            high - low, high + low, right - left, right + left, over - under, over + under,
+            high - low, high + low, right - left, right + left, above - below, above + below,
             (cut(1, 1, 1) - cut(1, -1, 1)) - (cut(1, 1, -1) - cut(1, -1, -1)),
             (cut(2, 1, 0) - cut(2, -1, 0)) - (cut(0, 1, 0) - cut(0, -1, 0)),
             (cut(2, 0, 1) - cut(2, 0, -1)) - (cut(0, 0, 1) - cut(0, 0, -1)),
         )
         for bx in range(2):
             rows = [jnp.sum(term[16 * bx : 16 * bx + 16], axis=0, keepdims=True) for term in terms]
-            rows = jnp.concatenate(rows + [jnp.zeros((3, CY), F32)], axis=0)
-            total = total + jnp.dot(
-                rows, z_places[2 * side + bx],
-                precision=lax.Precision.HIGHEST, preferred_element_type=F32,
+            rows = jnp.concatenate(rows + [jnp.zeros((3, 128), F32)], axis=0)
+            found = found + exact_dot(
+                rows,
+                finder(
+                    128,
+                    lambda at: jnp.where(at < CY, 48 * bx + 16 * (at // 16) + 15 * side, -1),
+                ),
             )
+    total = exact_dot(found, to_slot, (((1,), (1,)), ((), ())))
     scale = 2.0 / 3.0 / (BRICK * BRICK)
     row = lax.broadcasted_iota(jnp.int32, (8, SLOTS), 0)
     record[...] = total * jnp.where(row == 1, F32(scale), F32(0.5 * scale))
 
 
-def bricks(v, x_low, x_high, y_low, y_high, z_window, places, z_places):
+def bricks(parity, count, v, halos, planes, ids, targets):
     return pl.pallas_call(
         brick_kernel,
         out_shape=jax.ShapeDtypeStruct((8, SLOTS), F32),
-        in_specs=vmem_specs(8),
+        in_specs=[pl.BlockSpec(memory_space=pltpu.SMEM)] * 2 + vmem_specs(10),
         out_specs=vmem_specs(1)[0],
         scratch_shapes=[
             pltpu.VMEM((2, CX + 2, 64, 128), F32),
@@ -607,7 +722,7 @@
         ],
         compiler_params=pltpu.CompilerParams(vmem_limit_bytes=VMEM_LIMIT),
         name="bricks",
-    )(v, x_low, x_high, y_low, y_high, z_window, places, z_places)
+    )(parity, count, v, *halos, planes, ids, targets)
 
 
 def swap(value, axis, phase):
@@ -617,28 +732,6 @@
     else:
         pairs = [(i, (i - 1 if i % 2 == 0 else i + 1) % count) for i in range(count)]
     return lax.ppermute(value, axis, pairs)
-
-
-def place_tables(device_ids, live_count, targets):
-    entries = jnp.arange(device_ids.shape[0], dtype=jnp.int32)
-    is_live = entries < live_count
-    earlier = entries[None, :] < entries[:, None]
-    same_owner = targets[None, :] == targets[:, None]
-    rank = jnp.sum((earlier & same_owner & is_live[None, :]).astype(jnp.int32), axis=1)
-    columns = jnp.where(is_live, targets * 2 + rank, SLOTS)
-    count = (CX // BRICK) * (CY // BRICK) * (CZ // BRICK)
-    brick = jnp.arange(count, dtype=jnp.int32)
-    slot = jnp.arange(SLOTS, dtype=jnp.int32)
-    hits = (device_ids[:, None, None] == brick[None, :, None]) & (
-        columns[:, None, None] == slot[None, None, :]
-    )
-    table = jnp.any(hits, axis=0).astype(F32)
-    table = table.reshape(2, 3, 16, SLOTS)
-    places = jnp.repeat(table.reshape(6, 16, SLOTS), 8, axis=1)
-    z_places = [
-        jnp.repeat(table[bx, :, end], BRICK, axis=0) for end in (0, 15) for bx in range(2)
-    ]
-    return places, jnp.stack(z_places, axis=0)
 
 
 def exchange(faces):
@@ -652,19 +745,9 @@
     return xa, xb, ya, yb, za, zb
 
 
-def exchange_pair(low, high, axis, odd):
-    part_b = swap(jnp.where(odd, high, low), axis, 1)
-    part_a = swap(jnp.where(odd, low, high), axis, 0)
-    return jnp.where(odd, part_a, part_b), jnp.where(odd, part_b, part_a)
-
-
 def per_device(phi_start, band_ids, band_count, owners):
     parity = jnp.stack([lax.axis_index(name) % 2 for name in ("gx", "gy", "gz")])
     parity = parity.astype(jnp.int32)
-    odd_x, odd_y, odd_z = [parity[k] == 1 for k in range(3)]
-    places, z_places = place_tables(
-        band_ids.reshape(-1), band_count.reshape(()), owners.reshape(-1)
-    )
     v, sigma, pace, *faces = pack(parity, phi_start)
     za0, zb0 = faces[4:]
     for number in range(STEPS):
@@ -674,25 +757,19 @@
         )
     level_set = unpack(v)
 
-    xa, xb, ylo, yhi, zlo, zhi = faces
+    xa, xb, ylo, yhi, own = faces
     xb = swap(xb, "gx", 1)
     xa = swap(xa, "gx", 0)
-    x_low, x_high = jnp.where(odd_x, xa, xb), jnp.where(odd_x, xb, xa)
-    first = jnp.concatenate([x_low[:, 0], ylo[0], x_high[:, 0]], axis=0)
-    last = jnp.concatenate([x_low[:, CY - 1], yhi[0], x_high[:, CY - 1]], axis=0)
-    y_low, y_high = exchange_pair(first, last, "gy", odd_y)
-
-    def plane(body, lane):
-        middle = jnp.concatenate(
-            [x_low[:, :, lane], body.reshape(CX, CY), x_high[:, :, lane]], axis=0
-        )
-        return jnp.concatenate([y_low[:, lane, None], middle, y_high[:, lane, None]], axis=1)
-
-    bottom, above = plane(zlo[0], 0), plane(zlo[1], 128)
-    below, top = plane(zhi[6], 127), plane(zhi[7], 255)
-    under, over = exchange_pair(bottom, top, "gz", odd_z)
-    z_window = jnp.stack([under, bottom, above, below, top, over], axis=0)
-    record = bricks(v, x_low, x_high, y_low, y_high, z_window, places, z_places)
+    ya, yb = row_faces(parity, xa, xb, ylo, yhi)
+    yb = swap(yb, "gy", 1)
+    ya = swap(ya, "gy", 0)
+    planes, za, zb = plane_faces(parity, xa, xb, ya, yb, own)
+    zb = swap(zb, "gz", 1)
+    za = swap(za, "gz", 0)
+    record = bricks(
+        parity, band_count.reshape(1), v, (xa, xb, ya, yb, za, zb), planes,
+        band_ids.reshape(1, SLOTS), owners.reshape(1, SLOTS),
+    )
     totals = lax.all_to_all(record[:5], ("gx", "gy"), split_axis=1, concat_axis=1, tiled=True)
     return level_set, totals.reshape(1, 1, 1, 5, SLOTS)
 

time: 143 us -> 123 us (0.86)
  local copies, waits for them, and re-layouts: 21.3 us -> 2.82 us
  starting transfers between devices: 44.7 us -> 49.5 us
  other arithmetic: 2.83 us -> 0.08 us
  waiting for transfers between devices: 24.1 us -> 21.7 us
    unnamed x53 -> x7, local copies, waits for them, and re-layouts: 17.6 us -> 2.07 us
    ppermute x24, starting transfers between devices: 38.6 us -> 42.5 us  [swap(): return lax.ppermute(value, axis, pairs)]
    ppermute x24, waiting for transfers between devices: 19 us -> 16.7 us  [swap(): return lax.ppermute(value, axis, pairs)]
    convert_element_type x1 -> x0, local copies, waits for them, and re-layouts: 1.47 us -> none  [place_tables(): table = jnp.any(hits, axis=0).astype(F32)]
    pallas_call x3, Pallas kernels: 37.1 us -> 35.7 us  [step(): pl.pallas_call(functools.partial(step_kernel, last), out_shape=[BLOCK] +...]
  transfers between devices with their start and end apart: 25 -> 25, of which waited for: 11 -> 12; matrix products, arithmetic and copies ran while one was open for 4% -> 0% of each run, Pallas kernels for 2% -> 2%
where the time goes in v2:
time: 123 us
  starting transfers between devices  49.5 us (40%)
  Pallas kernels  47.5 us (39%)
  waiting for transfers between devices  21.7 us (18%)
  local copies, waits for them, and re-layouts  2.82 us (2%)
  between operations  1.41 us (1%)
    ppermute x24, starting transfers between devices, swap(): return lax.ppermute(value, axis, pairs)  42.5 us
    pallas_call x3, Pallas kernels, step(): pl.pallas_call(functools.partial(step_kernel, last), out_shape=[BLOCK] +...  35.7 us
    ppermute x24, waiting for transfers between devices, swap(): return lax.ppermute(value, axis, pairs)  16.7 us
    all_to_all x1, starting transfers between devices, per_device(): lax.all_to_all(record[:5], ('gx', 'gy'), split_axis=1, concat_axis=1, til...  6.96 us
    pallas_call x1, Pallas kernels, bricks(): pl.pallas_call(brick_kernel, out_shape=jax.ShapeDtypeStruct((8, SLOTS), F...  5.5 us
    all_to_all x1, waiting for transfers between devices, per_device(): lax.all_to_all(record[:5], ('gx', 'gy'), split_axis=1, concat_axis=1, til...  5.02 us
    pallas_call x1, Pallas kernels, pack(): pl.pallas_call(pack_kernel, out_shape=[BLOCK] * 3 + face_shapes(3), in_sp...  2.8 us
  transfers between devices with their start and end apart: 25, of which 12 were waited for; matrix products, arithmetic and copies ran while one was open for 0% of the time, Pallas kernels for 2%

profile of v2, /device:TPU:1, one launch (start us, length us, event | category | flops | bytes accessed | tf_op | source)
XLA Modules:
  0.0 122.9 jit_solution(5542066655799652465)
XLA Ops:
  0.7 1.4 %copy-done = f32[32,48,256]{2,1,0:T(8,128)S(1)} copy-done((f32[32,48,256]{2,1,0:T(8,128)S(1)}, f32[32,48,256]{2,1,0:T(8,128)}, u32[]{:S(2)}) %copy-start) | copy-done | bytes 1572888
  2.1 2.8 %pack.1 = (f32[32,48,256]{2,1,0:T(8,128)S(1)}, f32[32,48,256]{2,1,0:T(8,128)S(1)}, f32[32,48,256]{2,1,0:T(8,128)S(1)}, f32[3,48,256]{2,1,0:T(8,128)S(1)}, f32[3,...) custom-call(s32[3]{0:T(128)S(1)} %pad_add_fusion.parity, ...), custom_call_target="tpu_custom_call" | custom-call | tf_op jit(solution)/shard_map/pack/pallas_call | solution.py:475
  4.9 3.3 %collective-permute-start = (f32[3,48,256]{2,1,0:T(8,128)S(1)}, f32[3,48,256]{2,1,0:T(8,128)S(1)}, u32[]{:S(2)}, u32[]{:S(2)}) collective-permute-start(f32[3,48,256]{2,1,0:T(8,128)S(1)} %get-tuple-element.41), channel_id=1, source_target_pairs={{0,64},{64,0},{128,192},{192,128},{1,65},{65,1},{129,193},{193,129... | collective-permute-start | bytes 442376 | tf_op jit(solution)/shard_map/ppermute | solution.py:734
  8.3 1.1 collective-permute-start.4
  9.4 2.5 %collective-permute-start.2 = (f32[3,32,256]{2,1,0:T(8,128)S(1)}, f32[3,32,256]{2,1,0:T(8,128)S(1)}, u32[]{:S(2)}, u32[]{:S(2)}) collective-permute-start(f32[3,32,256]{2,1,0:T(8,128)S(1)} %get-tuple-element.43), channel_id=1, source_target_pairs={{0,8},{8,0},{16,24},{24,16},{32,40},{40,32},{48,56},{56,48},{1,9},... | collective-permute-start | bytes 294920 | tf_op jit(solution)/shard_map/ppermute | solution.py:734
  11.8 3.0 %collective-permute-start.3 = (f32[3,32,256]{2,1,0:T(8,128)S(1)}, f32[3,32,256]{2,1,0:T(8,128)S(1)}, u32[]{:S(2)}, u32[]{:S(2)}) collective-permute-start(f32[3,32,256]{2,1,0:T(8,128)S(1)} %get-tuple-element.44), channel_id=1, source_target_pairs={{0,56},{8,16},{16,8},{24,32},{32,24},{40,48},{48,40},{56,0},{1,57}... | collective-permute-start | bytes 294920 | tf_op jit(solution)/shard_map/ppermute | solution.py:734
  14.8 4.7 %collective-permute-start.5 = (f32[8,1536]{1,0:T(8,128)S(1)}, f32[8,1536]{1,0:T(8,128)S(1)}, u32[]{:S(2)}, u32[]{:S(2)}) collective-permute-start(f32[8,1536]{1,0:T(8,128)S(1)} %get-tuple-element.39.zb0.zb_own), channel_id=1, source_target_pairs={{0,7},{1,2},{2,1},{3,4},{4,3},{5,6},{6,5},{7,0},{8,15},{9,10},{10,... | collective-permute-start | bytes 147464 | tf_op jit(solution)/shard_map/ppermute | solution.py:734
  19.5 1.8 %collective-permute-done.5.zb_in = f32[8,1536]{1,0:T(8,128)S(1)} collective-permute-done((f32[8,1536]{1,0:T(8,128)S(1)}, f32[8,1536]{1,0:T(8,128)S(1)}, u32[]{:S(2)}, u32[]{:S(2)}) %collective-permute-start.5) | collective-permute-done | bytes 49184 | tf_op jit(solution)/shard_map/ppermute | solution.py:734
  21.3 11.8 %step.3 = (f32[32,48,256]{2,1,0:T(8,128)S(1)}, f32[3,48,256]{2,1,0:T(8,128)S(1)}, f32[3,48,256]{2,1,0:T(8,128)S(1)}, f32[3,32,256]{2,1,0:T(8,128)S(1)}, f32[3,32...) custom-call(s32[3]{0:T(128)S(1)} %pad_add_fusion.parity, ...), custom_call_target="tpu_custom_call" | custom-call | tf_op jit(solution)/shard_map/step/pallas_call | solution.py:499
  33.1 1.9 %collective-permute-start.6 = (f32[3,48,256]{2,1,0:T(8,128)S(1)}, f32[3,48,256]{2,1,0:T(8,128)S(1)}, u32[]{:S(2)}, u32[]{:S(2)}) collective-permute-start(f32[3,48,256]{2,1,0:T(8,128)S(1)} %get-tuple-element.48), channel_id=1, source_target_pairs={{0,64},{64,0},{128,192},{192,128},{1,65},{65,1},{129,193},{193,129... | collective-permute-start | bytes 442376 | tf_op jit(solution)/shard_map/ppermute | solution.py:734
  35.3 1.3 %collective-permute-start.8 = (f32[3,32,256]{2,1,0:T(8,128)S(1)}, f32[3,32,256]{2,1,0:T(8,128)S(1)}, u32[]{:S(2)}, u32[]{:S(2)}) collective-permute-start(f32[3,32,256]{2,1,0:T(8,128)S(1)} %get-tuple-element.50), channel_id=1, source_target_pairs={{0,8},{8,0},{16,24},{24,16},{32,40},{40,32},{48,56},{56,48},{1,9},... | collective-permute-start | bytes 294920 | tf_op jit(solution)/shard_map/ppermute | solution.py:734
  36.6 1.8 %collective-permute-start.9 = (f32[3,32,256]{2,1,0:T(8,128)S(1)}, f32[3,32,256]{2,1,0:T(8,128)S(1)}, u32[]{:S(2)}, u32[]{:S(2)}) collective-permute-start(f32[3,32,256]{2,1,0:T(8,128)S(1)} %get-tuple-element.51), channel_id=1, source_target_pairs={{0,56},{8,16},{16,8},{24,32},{32,24},{40,48},{48,40},{56,0},{1,57}... | collective-permute-start | bytes 294920 | tf_op jit(solution)/shard_map/ppermute | solution.py:734
  38.5 4.5 %collective-permute-start.11 = (f32[8,1536]{1,0:T(8,128)S(1)}, f32[8,1536]{1,0:T(8,128)S(1)}, u32[]{:S(2)}, u32[]{:S(2)}) collective-permute-start(f32[8,1536]{1,0:T(8,128)S(1)} %get-tuple-element.47.zb_own), channel_id=1, source_target_pairs={{0,7},{1,2},{2,1},{3,4},{4,3},{5,6},{6,5},{7,0},{8,15},{9,10},{10,... | collective-permute-start | bytes 147464 | tf_op jit(solution)/shard_map/ppermute | solution.py:734
  43.0 1.8 %collective-permute-done.11.zb_in = f32[8,1536]{1,0:T(8,128)S(1)} collective-permute-done((f32[8,1536]{1,0:T(8,128)S(1)}, f32[8,1536]{1,0:T(8,128)S(1)}, u32[]{:S(2)}, u32[]{:S(2)}) %collective-permute-start.11) | collective-permute-done | bytes 49184 | tf_op jit(solution)/shard_map/ppermute | solution.py:734
  45.8 11.8 %step.4 = (f32[32,48,256]{2,1,0:T(8,128)S(1)}, f32[3,48,256]{2,1,0:T(8,128)S(1)}, f32[3,48,256]{2,1,0:T(8,128)S(1)}, f32[3,32,256]{2,1,0:T(8,128)S(1)}, f32[3,32...) custom-call(s32[3]{0:T(128)S(1)} %pad_add_fusion.parity, ...), custom_call_target="tpu_custom_call" | custom-call | tf_op jit(solution)/shard_map/step/pallas_call | solution.py:499
  57.6 1.0 collective-permute-start.12
  58.6 1.4 %collective-permute-start.13 = (f32[3,48,256]{2,1,0:T(8,128)S(1)}, f32[3,48,256]{2,1,0:T(8,128)S(1)}, u32[]{:S(2)}, u32[]{:S(2)}) collective-permute-start(f32[3,48,256]{2,1,0:T(8,128)S(1)} %get-tuple-element.56), channel_id=1, source_target_pairs={{0,192},{64,128},{128,64},{192,0},{1,193},{65,129},{129,65},{193,1... | collective-permute-start | bytes 442376 | tf_op jit(solution)/shard_map/ppermute | solution.py:734
  60.1 1.4 %collective-permute-start.14 = (f32[3,32,256]{2,1,0:T(8,128)S(1)}, f32[3,32,256]{2,1,0:T(8,128)S(1)}, u32[]{:S(2)}, u32[]{:S(2)}) collective-permute-start(f32[3,32,256]{2,1,0:T(8,128)S(1)} %get-tuple-element.57), channel_id=1, source_target_pairs={{0,8},{8,0},{16,24},{24,16},{32,40},{40,32},{48,56},{56,48},{1,9},... | collective-permute-start | bytes 294920 | tf_op jit(solution)/shard_map/ppermute | solution.py:734
  61.5 1.8 %collective-permute-start.15 = (f32[3,32,256]{2,1,0:T(8,128)S(1)}, f32[3,32,256]{2,1,0:T(8,128)S(1)}, u32[]{:S(2)}, u32[]{:S(2)}) collective-permute-start(f32[3,32,256]{2,1,0:T(8,128)S(1)} %get-tuple-element.58), channel_id=1, source_target_pairs={{0,56},{8,16},{16,8},{24,32},{32,24},{40,48},{48,40},{56,0},{1,57}... | collective-permute-start | bytes 294920 | tf_op jit(solution)/shard_map/ppermute | solution.py:734
  63.3 4.7 %collective-permute-start.17 = (f32[8,1536]{1,0:T(8,128)S(1)}, f32[8,1536]{1,0:T(8,128)S(1)}, u32[]{:S(2)}, u32[]{:S(2)}) collective-permute-start(f32[8,1536]{1,0:T(8,128)S(1)} %get-tuple-element.54.zb_own), channel_id=1, source_target_pairs={{0,7},{1,2},{2,1},{3,4},{4,3},{5,6},{6,5},{7,0},{8,15},{9,10},{10,... | collective-permute-start | bytes 147464 | tf_op jit(solution)/shard_map/ppermute | solution.py:734
  68.0 1.5 %collective-permute-done.17.zb_in = f32[8,1536]{1,0:T(8,128)S(1)} collective-permute-done((f32[8,1536]{1,0:T(8,128)S(1)}, f32[8,1536]{1,0:T(8,128)S(1)}, u32[]{:S(2)}, u32[]{:S(2)}) %collective-permute-start.17) | collective-permute-done | bytes 49184 | tf_op jit(solution)/shard_map/ppermute | solution.py:734
  69.4 1.7 %collective-permute-done.15.yb_in = f32[3,32,256]{2,1,0:T(8,128)S(1)} collective-permute-done((f32[3,32,256]{2,1,0:T(8,128)S(1)}, f32[3,32,256]{2,1,0:T(8,128)S(1)}, u32[]{:S(2)}, u32[]{:S(2)}) %collective-permute-start.15) | collective-permute-done | bytes 98336 | tf_op jit(solution)/shard_map/ppermute | solution.py:734
  71.2 12.0 %step.5 = (f32[32,48,256]{2,1,0:T(8,128)S(1)}, f32[1,48,256]{2,1,0:T(8,128)S(1)}, f32[1,48,256]{2,1,0:T(8,128)S(1)}, f32[1,32,256]{2,1,0:T(8,128)S(1)}, f32[1,32...) custom-call(s32[3]{0:T(128)S(1)} %pad_add_fusion.parity, f32[32,48,256]{2,1,0:T(8,128)S(1)} %get-tuple-element.36.sigma_in, ...), custom_call_target="tpu_custom_call" | custom-call | tf_op jit(solution)/shard_map/step/pallas_call | solution.py:499
  85.1 2.7 %collective-permute-done.19.xb = f32[1,48,256]{2,1,0:T(8,128)S(1)} collective-permute-done((f32[1,48,256]{2,1,0:T(8,128)S(1)}, f32[1,48,256]{2,1,0:T(8,128)S(1)}, u32[]{:S(2)}, u32[]{:S(2)}) %collective-permute-start.19) | collective-permute-done | bytes 49184 | tf_op jit(solution)/shard_map/ppermute | solution.py:734
  89.1 1.6 %collective-permute-start.21 = (f32[34,256]{1,0:T(8,128)S(1)}, f32[34,256]{1,0:T(8,128)S(1)}, u32[]{:S(2)}, u32[]{:S(2)}) collective-permute-start(f32[34,256]{1,0:T(8,128)S(1)} %get-tuple-element.65), channel_id=1, source_target_pairs={{0,56},{8,16},{16,8},{24,32},{32,24},{40,48},{48,40},{56,0},{1,57}... | collective-permute-start | bytes 104456 | tf_op jit(solution)/shard_map/ppermute | solution.py:734
  90.7 2.1 %collective-permute-done.20.ya = f32[34,256]{1,0:T(8,128)S(1)} collective-permute-done((f32[34,256]{1,0:T(8,128)S(1)}, f32[34,256]{1,0:T(8,128)S(1)}, u32[]{:S(2)}, u32[]{:S(2)}) %collective-permute-start.20) | collective-permute-done | bytes 34848 | tf_op jit(solution)/shard_map/ppermute | solution.py:734
  92.8 2.7 %collective-permute-done.21.yb = f32[34,256]{1,0:T(8,128)S(1)} collective-permute-done((f32[34,256]{1,0:T(8,128)S(1)}, f32[34,256]{1,0:T(8,128)S(1)}, u32[]{:S(2)}, u32[]{:S(2)}) %collective-permute-start.21) | collective-permute-done | bytes 34848 | tf_op jit(solution)/shard_map/ppermute | solution.py:734
  96.4 4.3 %collective-permute-start.23 = (f32[40,128]{1,0:T(8,128)S(1)}, f32[40,128]{1,0:T(8,128)S(1)}, u32[]{:S(2)}, u32[]{:S(2)}) collective-permute-start(f32[40,128]{1,0:T(8,128)S(1)} %get-tuple-element.68), channel_id=1, source_target_pairs={{0,7},{1,2},{2,1},{3,4},{4,3},{5,6},{6,5},{7,0},{8,15},{9,10},{10,... | collective-permute-start | bytes 61448 | tf_op jit(solution)/shard_map/ppermute | solution.py:734
  101.8 5.5 %bricks.1 = f32[8,64]{1,0:T(8,128)S(1)} custom-call(s32[3]{0:T(128)S(1)} %pad_add_fusion.parity, s32[1]{0:T(128)} %bitcast.9.count, f32[32,48,256]{2,1,0:T(8,128)S(1)} %get-tuple-element.59.mixed.v, f32[1,48,256]{2,1,0:T(8,128)S(1)} %collective-permute-done.18.xa, f32[1,48,256]{2,1,0:T(8,128)S(1)} %collective-permute-done.19.xb, ...), custom_call_target="tpu_custom_call" | custom-call | tf_op jit(solution)/shard_map/bricks/pallas_call | solution.py:714
  108.1 7.0 %all-to-all-start = ((f32[5,32,2]{0,2,1:T(2,128)}), f32[5,32,2]{0,2,1:T(2,128)S(1)}, u32[]{:S(2)}, u32[]{:S(2)}) async-start(f32[5,32,2]{0,2,1:T(2,128)} %bitcast.6), calls=%async_computation | async-start | bytes 65536 | tf_op jit(solution)/shard_map/all_to_all | solution.py:773
  115.0 2.2 %unpack.1 = f32[32,48,256]{2,1,0:T(8,128)} custom-call(f32[32,48,256]{2,1,0:T(8,128)S(1)} %get-tuple-element.59.mixed.v), custom_call_target="tpu_custom_call" | custom-call | tf_op jit(solution)/shard_map/unpack/pallas_call | solution.py:487
  117.2 5.0 %all-to-all-done = f32[5,32,2]{0,2,1:T(2,128)S(1)} async-done(((f32[5,32,2]{0,2,1:T(2,128)}), f32[5,32,2]{0,2,1:T(2,128)S(1)}, u32[]{:S(2)}, u32[]{:S(2)}) %all-to-all-start) | async-done | bytes 1312 | tf_op jit(solution)/shard_map/all_to_all | solution.py:773
  (35 shorter events, 7.3 us)
Async XLA Ops:
  0.7 1.4 %copy-start = (f32[32,48,256]{2,1,0:T(8,128)S(1)}, f32[32,48,256]{2,1,0:T(8,128)}, u32[]{:S(2)}) copy-start(f32[32,48,256]{2,1,0:T(8,128)} %phi.1) | copy-start | bytes 4718596
  4.9 16.3 %collective-permute-start = (f32[3,48,256]{2,1,0:T(8,128)S(1)}, f32[3,48,256]{2,1,0:T(8,128)S(1)}, u32[]{:S(2)}, u32[]{:S(2)}) collective-permute-start(f32[3,48,256]{2,1,0:T(8,128)S(1)} %get-tuple-element.41), channel_id=1, source_target_pairs={{0,64},{64,0},{128,192},{192,128},{1,65},{65,1},{129,193},{193,129... | collective-permute-start | bytes 442376 | tf_op jit(solution)/shard_map/ppermute | solution.py:734
  8.3 13.0 %collective-permute-start.1 = (f32[3,48,256]{2,1,0:T(8,128)S(1)}, f32[3,48,256]{2,1,0:T(8,128)S(1)}, u32[]{:S(2)}, u32[]{:S(2)}) collective-permute-start(f32[3,48,256]{2,1,0:T(8,128)S(1)} %get-tuple-element.42), channel_id=1, source_target_pairs={{0,192},{64,128},{128,64},{192,0},{1,193},{65,129},{129,65},{193,1... | collective-permute-start | bytes 442376 | tf_op jit(solution)/shard_map/ppermute | solution.py:734
  8.3 6.5 %collective-permute-start.4 = (f32[8,1536]{1,0:T(8,128)S(1)}, f32[8,1536]{1,0:T(8,128)S(1)}, u32[]{:S(2)}, u32[]{:S(2)}) collective-permute-start(f32[8,1536]{1,0:T(8,128)S(1)} %get-tuple-element.38.za0.za_own), channel_id=1, source_target_pairs={{0,1},{1,0},{2,3},{3,2},{4,5},{5,4},{6,7},{7,6},{8,9},{9,8},{10,11... | collective-permute-start | bytes 147464 | tf_op jit(solution)/shard_map/ppermute | solution.py:734
  9.4 11.9 %collective-permute-start.2 = (f32[3,32,256]{2,1,0:T(8,128)S(1)}, f32[3,32,256]{2,1,0:T(8,128)S(1)}, u32[]{:S(2)}, u32[]{:S(2)}) collective-permute-start(f32[3,32,256]{2,1,0:T(8,128)S(1)} %get-tuple-element.43), channel_id=1, source_target_pairs={{0,8},{8,0},{16,24},{24,16},{32,40},{40,32},{48,56},{56,48},{1,9},... | collective-permute-start | bytes 294920 | tf_op jit(solution)/shard_map/ppermute | solution.py:734
  11.8 9.4 %collective-permute-start.3 = (f32[3,32,256]{2,1,0:T(8,128)S(1)}, f32[3,32,256]{2,1,0:T(8,128)S(1)}, u32[]{:S(2)}, u32[]{:S(2)}) collective-permute-start(f32[3,32,256]{2,1,0:T(8,128)S(1)} %get-tuple-element.44), channel_id=1, source_target_pairs={{0,56},{8,16},{16,8},{24,32},{32,24},{40,48},{48,40},{56,0},{1,57}... | collective-permute-start | bytes 294920 | tf_op jit(solution)/shard_map/ppermute | solution.py:734
  14.8 6.4 %collective-permute-start.5 = (f32[8,1536]{1,0:T(8,128)S(1)}, f32[8,1536]{1,0:T(8,128)S(1)}, u32[]{:S(2)}, u32[]{:S(2)}) collective-permute-start(f32[8,1536]{1,0:T(8,128)S(1)} %get-tuple-element.39.zb0.zb_own), channel_id=1, source_target_pairs={{0,7},{1,2},{2,1},{3,4},{4,3},{5,6},{6,5},{7,0},{8,15},{9,10},{10,... | collective-permute-start | bytes 147464 | tf_op jit(solution)/shard_map/ppermute | solution.py:734
  33.1 12.6 %collective-permute-start.6 = (f32[3,48,256]{2,1,0:T(8,128)S(1)}, f32[3,48,256]{2,1,0:T(8,128)S(1)}, u32[]{:S(2)}, u32[]{:S(2)}) collective-permute-start(f32[3,48,256]{2,1,0:T(8,128)S(1)} %get-tuple-element.48), channel_id=1, source_target_pairs={{0,64},{64,0},{128,192},{192,128},{1,65},{65,1},{129,193},{193,129... | collective-permute-start | bytes 442376 | tf_op jit(solution)/shard_map/ppermute | solution.py:734
  35.0 10.7 %collective-permute-start.7 = (f32[3,48,256]{2,1,0:T(8,128)S(1)}, f32[3,48,256]{2,1,0:T(8,128)S(1)}, u32[]{:S(2)}, u32[]{:S(2)}) collective-permute-start(f32[3,48,256]{2,1,0:T(8,128)S(1)} %get-tuple-element.49), channel_id=1, source_target_pairs={{0,192},{64,128},{128,64},{192,0},{1,193},{65,129},{129,65},{193,1... | collective-permute-start | bytes 442376 | tf_op jit(solution)/shard_map/ppermute | solution.py:734
  35.3 3.2 %collective-permute-start.10 = (f32[8,1536]{1,0:T(8,128)S(1)}, f32[8,1536]{1,0:T(8,128)S(1)}, u32[]{:S(2)}, u32[]{:S(2)}) collective-permute-start(f32[8,1536]{1,0:T(8,128)S(1)} %get-tuple-element.46.za_own), channel_id=1, source_target_pairs={{0,1},{1,0},{2,3},{3,2},{4,5},{5,4},{6,7},{7,6},{8,9},{9,8},{10,11... | collective-permute-start | bytes 147464 | tf_op jit(solution)/shard_map/ppermute | solution.py:734
  35.3 9.5 %collective-permute-start.8 = (f32[3,32,256]{2,1,0:T(8,128)S(1)}, f32[3,32,256]{2,1,0:T(8,128)S(1)}, u32[]{:S(2)}, u32[]{:S(2)}) collective-permute-start(f32[3,32,256]{2,1,0:T(8,128)S(1)} %get-tuple-element.50), channel_id=1, source_target_pairs={{0,8},{8,0},{16,24},{24,16},{32,40},{40,32},{48,56},{56,48},{1,9},... | collective-permute-start | bytes 294920 | tf_op jit(solution)/shard_map/ppermute | solution.py:734
  36.6 9.2 %collective-permute-start.9 = (f32[3,32,256]{2,1,0:T(8,128)S(1)}, f32[3,32,256]{2,1,0:T(8,128)S(1)}, u32[]{:S(2)}, u32[]{:S(2)}) collective-permute-start(f32[3,32,256]{2,1,0:T(8,128)S(1)} %get-tuple-element.51), channel_id=1, source_target_pairs={{0,56},{8,16},{16,8},{24,32},{32,24},{40,48},{48,40},{56,0},{1,57}... | collective-permute-start | bytes 294920 | tf_op jit(solution)/shard_map/ppermute | solution.py:734
  38.5 6.3 %collective-permute-start.11 = (f32[8,1536]{1,0:T(8,128)S(1)}, f32[8,1536]{1,0:T(8,128)S(1)}, u32[]{:S(2)}, u32[]{:S(2)}) collective-permute-start(f32[8,1536]{1,0:T(8,128)S(1)} %get-tuple-element.47.zb_own), channel_id=1, source_target_pairs={{0,7},{1,2},{2,1},{3,4},{4,3},{5,6},{6,5},{7,0},{8,15},{9,10},{10,... | collective-permute-start | bytes 147464 | tf_op jit(solution)/shard_map/ppermute | solution.py:734
  57.6 13.6 %collective-permute-start.12 = (f32[3,48,256]{2,1,0:T(8,128)S(1)}, f32[3,48,256]{2,1,0:T(8,128)S(1)}, u32[]{:S(2)}, u32[]{:S(2)}) collective-permute-start(f32[3,48,256]{2,1,0:T(8,128)S(1)} %get-tuple-element.55), channel_id=1, source_target_pairs={{0,64},{64,0},{128,192},{192,128},{1,65},{65,1},{129,193},{193,129... | collective-permute-start | bytes 442376 | tf_op jit(solution)/shard_map/ppermute | solution.py:734
  58.6 12.5 %collective-permute-start.13 = (f32[3,48,256]{2,1,0:T(8,128)S(1)}, f32[3,48,256]{2,1,0:T(8,128)S(1)}, u32[]{:S(2)}, u32[]{:S(2)}) collective-permute-start(f32[3,48,256]{2,1,0:T(8,128)S(1)} %get-tuple-element.56), channel_id=1, source_target_pairs={{0,192},{64,128},{128,64},{192,0},{1,193},{65,129},{129,65},{193,1... | collective-permute-start | bytes 442376 | tf_op jit(solution)/shard_map/ppermute | solution.py:734
  60.1 3.2 %collective-permute-start.16 = (f32[8,1536]{1,0:T(8,128)S(1)}, f32[8,1536]{1,0:T(8,128)S(1)}, u32[]{:S(2)}, u32[]{:S(2)}) collective-permute-start(f32[8,1536]{1,0:T(8,128)S(1)} %get-tuple-element.53.za_own), channel_id=1, source_target_pairs={{0,1},{1,0},{2,3},{3,2},{4,5},{5,4},{6,7},{7,6},{8,9},{9,8},{10,11... | collective-permute-start | bytes 147464 | tf_op jit(solution)/shard_map/ppermute | solution.py:734
  60.1 9.4 %collective-permute-start.14 = (f32[3,32,256]{2,1,0:T(8,128)S(1)}, f32[3,32,256]{2,1,0:T(8,128)S(1)}, u32[]{:S(2)}, u32[]{:S(2)}) collective-permute-start(f32[3,32,256]{2,1,0:T(8,128)S(1)} %get-tuple-element.57), channel_id=1, source_target_pairs={{0,8},{8,0},{16,24},{24,16},{32,40},{40,32},{48,56},{56,48},{1,9},... | collective-permute-start | bytes 294920 | tf_op jit(solution)/shard_map/ppermute | solution.py:734
  61.5 9.7 %collective-permute-start.15 = (f32[3,32,256]{2,1,0:T(8,128)S(1)}, f32[3,32,256]{2,1,0:T(8,128)S(1)}, u32[]{:S(2)}, u32[]{:S(2)}) collective-permute-start(f32[3,32,256]{2,1,0:T(8,128)S(1)} %get-tuple-element.58), channel_id=1, source_target_pairs={{0,56},{8,16},{16,8},{24,32},{32,24},{40,48},{48,40},{56,0},{1,57}... | collective-permute-start | bytes 294920 | tf_op jit(solution)/shard_map/ppermute | solution.py:734
  63.3 6.1 %collective-permute-start.17 = (f32[8,1536]{1,0:T(8,128)S(1)}, f32[8,1536]{1,0:T(8,128)S(1)}, u32[]{:S(2)}, u32[]{:S(2)}) collective-permute-start(f32[8,1536]{1,0:T(8,128)S(1)} %get-tuple-element.54.zb_own), channel_id=1, source_target_pairs={{0,7},{1,2},{2,1},{3,4},{4,3},{5,6},{6,5},{7,0},{8,15},{9,10},{10,... | collective-permute-start | bytes 147464 | tf_op jit(solution)/shard_map/ppermute | solution.py:734
  71.2 30.7 %copy-start.1 = (s32[1,1,1,64]{3,2,1,0:T(1,128)S(1)}, s32[1,1,1,64]{3,2,1,0:T(1,128)}, u32[]{:S(2)}) copy-start(s32[1,1,1,64]{3,2,1,0:T(1,128)} %param.5) | copy-start | bytes 772
  71.2 30.7 %copy-start.2 = (s32[1,1,1,64]{3,2,1,0:T(1,128)S(1)}, s32[1,1,1,64]{3,2,1,0:T(1,128)}, u32[]{:S(2)}) copy-start(s32[1,1,1,64]{3,2,1,0:T(1,128)} %param.7) | copy-start | bytes 772
  83.2 1.9 %collective-permute-start.18 = (f32[1,48,256]{2,1,0:T(8,128)S(1)}, f32[1,48,256]{2,1,0:T(8,128)S(1)}, u32[]{:S(2)}, u32[]{:S(2)}) collective-permute-start(f32[1,48,256]{2,1,0:T(8,128)S(1)} %get-tuple-element.60), channel_id=1, source_target_pairs={{0,64},{64,0},{128,192},{192,128},{1,65},{65,1},{129,193},{193,129... | collective-permute-start | bytes 147464 | tf_op jit(solution)/shard_map/ppermute | solution.py:734
  84.2 3.5 %collective-permute-start.19 = (f32[1,48,256]{2,1,0:T(8,128)S(1)}, f32[1,48,256]{2,1,0:T(8,128)S(1)}, u32[]{:S(2)}, u32[]{:S(2)}) collective-permute-start(f32[1,48,256]{2,1,0:T(8,128)S(1)} %get-tuple-element.61), channel_id=1, source_target_pairs={{0,192},{64,128},{128,64},{192,0},{1,193},{65,129},{129,65},{193,1... | collective-permute-start | bytes 147464 | tf_op jit(solution)/shard_map/ppermute | solution.py:734
  88.3 4.5 %collective-permute-start.20 = (f32[34,256]{1,0:T(8,128)S(1)}, f32[34,256]{1,0:T(8,128)S(1)}, u32[]{:S(2)}, u32[]{:S(2)}) collective-permute-start(f32[34,256]{1,0:T(8,128)S(1)} %get-tuple-element.64), channel_id=1, source_target_pairs={{0,8},{8,0},{16,24},{24,16},{32,40},{40,32},{48,56},{56,48},{1,9},... | collective-permute-start | bytes 104456 | tf_op jit(solution)/shard_map/ppermute | solution.py:734
  89.1 6.5 %collective-permute-start.21 = (f32[34,256]{1,0:T(8,128)S(1)}, f32[34,256]{1,0:T(8,128)S(1)}, u32[]{:S(2)}, u32[]{:S(2)}) collective-permute-start(f32[34,256]{1,0:T(8,128)S(1)} %get-tuple-element.65), channel_id=1, source_target_pairs={{0,56},{8,16},{16,8},{24,32},{32,24},{40,48},{48,40},{56,0},{1,57}... | collective-permute-start | bytes 104456 | tf_op jit(solution)/shard_map/ppermute | solution.py:734
  96.3 5.0 %collective-permute-start.22 = (f32[40,128]{1,0:T(8,128)S(1)}, f32[40,128]{1,0:T(8,128)S(1)}, u32[]{:S(2)}, u32[]{:S(2)}) collective-permute-start(f32[40,128]{1,0:T(8,128)S(1)} %get-tuple-element.67), channel_id=1, source_target_pairs={{0,1},{1,0},{2,3},{3,2},{4,5},{5,4},{6,7},{7,6},{8,9},{9,8},{10,11... | collective-permute-start | bytes 61448 | tf_op jit(solution)/shard_map/ppermute | solution.py:734
  96.4 5.5 %collective-permute-start.23 = (f32[40,128]{1,0:T(8,128)S(1)}, f32[40,128]{1,0:T(8,128)S(1)}, u32[]{:S(2)}, u32[]{:S(2)}) collective-permute-start(f32[40,128]{1,0:T(8,128)S(1)} %get-tuple-element.68), channel_id=1, source_target_pairs={{0,7},{1,2},{2,1},{3,4},{4,3},{5,6},{6,5},{7,0},{8,15},{9,10},{10,... | collective-permute-start | bytes 61448 | tf_op jit(solution)/shard_map/ppermute | solution.py:734
  108.1 14.2 %all-to-all-start = ((f32[5,32,2]{0,2,1:T(2,128)}), f32[5,32,2]{0,2,1:T(2,128)S(1)}, u32[]{:S(2)}, u32[]{:S(2)}) async-start(f32[5,32,2]{0,2,1:T(2,128)} %bitcast.6), calls=%async_computation | async-start | bytes 65536 | tf_op jit(solution)/shard_map/all_to_all | solution.py:773

commit v3 on v2

--- a/solution.py
+++ b/solution.py
@@ -380,7 +380,7 @@
     if last:
         xa, xb, ylo, yhi, planes = outs[1:]
         write_swap(parity[0], out[0:1], out[CX - 1 : CX], xa, xb)
-        y_faces(out, ylo, yhi, 1)
+        y_faces(out, ylo, yhi, 2)
         planes[...] = jnp.zeros((4, CX, 128), F32)
         for chunk in range(CX // 8):
             for half in range(2):
@@ -395,13 +395,15 @@
         write_faces(parity, out, *outs[1:], yf, zf)
 
 
-def rows_kernel(parity, xa, xb, ylo, yhi, ya, yb, ext):
+def rows_kernel(parity, xa, xb, ylo, yhi, ya, yb, y_rows):
     x_low, x_high = low_high(parity[0], xa[0], xb[0])
-    for side, (source, row) in enumerate(((ylo, 0), (yhi, CY - 1))):
-        ext[side, 0:1, :] = x_low[row : row + 1]
-        ext[side, 1 : CX + 1, :] = source[0]
-        ext[side, CX + 1 : CX + 2, :] = x_high[row : row + 1]
-    write_swap(parity[1], ext[0], ext[1], ya, yb)
+    for at, (source, layer, row) in enumerate(
+        ((ylo, 0, 0), (ylo, 1, 1), (yhi, 0, CY - 2), (yhi, 1, CY - 1))
+    ):
+        y_rows[at, 0:1, :] = x_low[row : row + 1]
+        y_rows[at, 1 : CX + 1, :] = source[layer]
+        y_rows[at, CX + 1 : CX + 2, :] = x_high[row : row + 1]
+    write_swap(parity[1], y_rows[0], y_rows[3], ya, yb)
 
 
 def planes_kernel(parity, xa, xb, ya, yb, own, planes, za, zb):
@@ -431,7 +433,7 @@
 
 
 def face_shapes(width):
-    shapes = [(width, CY, CZ)] * 2 + [(width, CX, CZ)] * 2
+    shapes = [(width, CY, CZ)] * 2 + [(max(width, 2), CX, CZ)] * 2
     shapes += [(8, ROWS)] * 2 if width == 3 else [(4, CX, 128)]
     return [jax.ShapeDtypeStruct(shape, F32) for shape in shapes]
 
@@ -439,10 +441,10 @@
 def row_faces(parity, xa, xb, ylo, yhi):
     return pl.pallas_call(
         rows_kernel,
-        out_shape=[jax.ShapeDtypeStruct((CX + 2, CZ), F32)] * 2,
+        out_shape=[jax.ShapeDtypeStruct((CX + 2, CZ), F32)] * 2
+        + [jax.ShapeDtypeStruct((4, CX + 2, CZ), F32)],
         in_specs=parity_specs(4),
-        out_specs=vmem_specs(2),
-        scratch_shapes=[pltpu.VMEM((2, CX + 2, CZ), F32)],
+        out_specs=vmem_specs(3),
         compiler_params=pltpu.CompilerParams(vmem_limit_bytes=VMEM_LIMIT),
         name="row_faces",
     )(parity, xa, xb, ylo, yhi)
@@ -585,91 +587,137 @@
     )
 
 
-def brick_kernel(
-    parity, count, v, xa, xb, ya, yb, za, zb, planes, ids, targets, record, vs, stack
-):
-    x_low, x_high = low_high(parity[0], xa[...], xb[...])
-    y_low, y_high = low_high(parity[1], ya[...], yb[...])
-    under, over = low_high(parity[2], za[...], zb[...])
+def neighbours(pair):
+    return ((lane_down(pair[1]), pair[1]), (pair[0], lane_up(pair[0])))
+
+
+def pair_terms(grid, keeps):
+    two = range(2)
+
+    def diff(first, second):
+        return [grid[first][half] - grid[second][half] for half in two]
+
+    def summed(first, second):
+        return [grid[first][half] + grid[second][half] for half in two]
+
+    dx, sx = diff((1, 0), (-1, 0)), summed((1, 0), (-1, 0))
+    dy, sy = diff((0, 1), (0, -1)), summed((0, 1), (0, -1))
+    over, under = diff((1, 1), (-1, 1)), diff((1, -1), (-1, -1))
+    around, dx_around, dy_around = neighbours(grid[0, 0]), neighbours(dx), neighbours(dy)
+    results = []
+    for half in two:
+        results.append(
+            five_terms(
+                grid[0, 0][half], keeps[half], dx[half], sx[half], dy[half], sy[half],
+                around[half][1] - around[half][0], around[half][1] + around[half][0],
+                over[half] - under[half],
+                dx_around[half][1] - dx_around[half][0],
+                dy_around[half][1] - dy_around[half][0],
+            )
+        )
+    return [results[0][n] + results[1][n] for n in range(5)]
+
+
+STAR = [(0, 0), (1, 0), (-1, 0), (0, 1), (0, -1), (1, 1), (1, -1), (-1, 1), (-1, -1)]
+
+
+def tile_terms(vs, plane, k, keeps):
+    grid = {
+        (sx, sy): [vs[half, plane + sx, pl.ds(8 + 8 * k + sy, 8), :] for half in range(2)]
+        for sx, sy in STAR
+    }
+    return pair_terms(grid, keeps)
+
+
+def z_keeps(rows):
+    lane = lax.broadcasted_iota(jnp.int32, (rows, 128), 1)
+    return [lane != 0, lane != 127]
+
+
+def inner_kernel(v, stack, vs):
     def fill(x, carry):
-        for zt in range(2):
-            vs[zt, x + 1, 8 : 8 + CY, :] = v[x, :, pl.ds(128 * zt, 128)]
+        for half in range(2):
+            vs[half, x, 8 : 8 + CY, :] = v[x, :, pl.ds(128 * half, 128)]
+            vs[half, x, 7:8, :] = jnp.zeros((1, 128), F32)
+            vs[half, x, 8 + CY : 9 + CY, :] = jnp.zeros((1, 128), F32)
         return carry
 
     lax.fori_loop(0, CX, fill, 0)
-    for zt in range(2):
-        lanes = slice(128 * zt, 128 * zt + 128)
-        vs[zt, 0, 8 : 8 + CY, :] = x_low[0, :, lanes]
-        vs[zt, CX + 1, 8 : 8 + CY, :] = x_high[0, :, lanes]
-        for x in range(CX + 2):
-            vs[zt, x, 7:8, :] = y_low[x : x + 1, lanes]
-            vs[zt, x, 8 + CY : 9 + CY, :] = y_high[x : x + 1, lanes]
-
-    lane = lax.broadcasted_iota(jnp.int32, (8, 128), 1)
-    keeps = (lane != 0, lane != 127)
-
-    def down(part):
-        return pltpu.roll(part, 1, 1)
-
-    def up(part):
-        return pltpu.roll(part, 127, 1)
-
-    def neighbours(pair):
-        return ((down(pair[1]), pair[1]), (pair[0], up(pair[0])))
-
-    def tile_terms(x, k):
-        def read(zt, plane, shift):
-            return vs[zt, plane, pl.ds(8 + 8 * k + shift, 8), :]
-
-        two = range(2)
-        centre = [read(zt, x + 1, 0) for zt in two]
-        high = [read(zt, x + 2, 0) for zt in two]
-        low = [read(zt, x, 0) for zt in two]
-        dx = [high[zt] - low[zt] for zt in two]
-        sx = [high[zt] + low[zt] for zt in two]
-        right = [read(zt, x + 1, 1) for zt in two]
-        left = [read(zt, x + 1, -1) for zt in two]
-        dy = [right[zt] - left[zt] for zt in two]
-        sy = [right[zt] + left[zt] for zt in two]
-        dxy = [
-            (read(zt, x + 2, 1) - read(zt, x, 1)) - (read(zt, x + 2, -1) - read(zt, x, -1))
-            for zt in two
-        ]
-        around, dx_around, dy_around = neighbours(centre), neighbours(dx), neighbours(dy)
-        results = []
-        for zt in two:
-            results.append(
-                five_terms(
-                    centre[zt], keeps[zt], dx[zt], sx[zt], dy[zt], sy[zt],
-                    around[zt][1] - around[zt][0], around[zt][1] + around[zt][0],
-                    dxy[zt],
-                    dx_around[zt][1] - dx_around[zt][0],
-                    dy_around[zt][1] - dy_around[zt][0],
-                )
-            )
-        return [results[0][n] + results[1][n] for n in range(5)]
-
+    keeps = z_keeps(8)
+    row = lax.broadcasted_iota(jnp.int32, (8, 128), 0)
+    first = [keep & (row != 0) for keep in keeps]
+    last = [keep & (row != 7) for keep in keeps]
     zeros = jnp.zeros((8, 128), F32)
     for bx in range(2):
 
         def body(step_at, sums):
             sums = list(sums)
-            for sub in range(2):
-                x = BRICK * bx + 2 * step_at + sub
+            for sub in range(3):
+                x = BRICK * bx + (1 - bx) + 3 * step_at + sub
                 for k in range(YT):
-                    parts = tile_terms(x, k)
+                    parts = tile_terms(vs, x, k, first if k == 0 else last if k == 5 else keeps)
                     for n in range(5):
                         slot = 5 * (k // 2) + n
                         sums[slot] = sums[slot] + parts[n]
             return tuple(sums)
 
-        sums = lax.fori_loop(0, BRICK // 2, body, (zeros,) * 15)
+        sums = lax.fori_loop(0, 5, body, (zeros,) * 15)
         for by in range(3):
+            row_at = 8 * (3 * bx + by)
             for n in range(5):
-                row = 8 * (3 * bx + by) + n
-                stack[row : row + 1, :] = jnp.sum(sums[5 * by + n], axis=0, keepdims=True)
-            row = 8 * (3 * bx + by)
-            stack[row + 5 : row + 8, :] = jnp.zeros((3, 128), F32)
+                total = jnp.sum(sums[5 * by + n], axis=0, keepdims=True)
+                stack[row_at + n : row_at + n + 1, :] = total
+            stack[row_at + 5 : row_at + 8, :] = jnp.zeros((3, 128), F32)
+
+
+def edge_kernel(
+    parity, count, inner, v, xa, xb, ya, yb, za, zb, y_rows, planes, ids, targets, record,
+    vs, stack,
+):
+    x_sides = low_high(parity[0], xa[0], xb[0])
+    y_sides = low_high(parity[1], ya[...], yb[...])
+    under, over = low_high(parity[2], za[...], zb[...])
+    stack[...] = inner[...]
+
+    def add(b, n, row):
+        stack[8 * b + n : 8 * b + n + 1, :] += row
+
+    keeps = z_keeps(8)
+    for side in range(2):
+        for half in range(2):
+            lanes = slice(128 * half, 128 * half + 128)
+            for at in range(3):
+                x = at - 1 if side == 0 else CX - 2 + at
+                if 0 <= x < CX:
+                    vs[half, at, 8 : 8 + CY, :] = v[x, :, lanes]
+                else:
+                    vs[half, at, 8 : 8 + CY, :] = x_sides[side][:, lanes]
+                vs[half, at, 7:8, :] = y_sides[0][x + 1 : x + 2, lanes]
+                vs[half, at, 8 + CY : 9 + CY, :] = y_sides[1][x + 1 : x + 2, lanes]
+        for by in range(3):
+            parts = [tile_terms(vs, 1, 2 * by + sub, keeps) for sub in range(2)]
+            for n in range(5):
+                add(3 * side + by, n, jnp.sum(parts[0][n] + parts[1][n], axis=0, keepdims=True))
+
+    keeps = z_keeps(16)
+    row = lax.broadcasted_iota(jnp.int32, (16, 128), 0)
+    for side in range(2):
+        if side == 0:
+            rows = (y_sides[0], y_rows[0], y_rows[1])
+        else:
+            rows = (y_rows[2], y_rows[3], y_sides[1])
+        for bx in range(2):
+            grid = {
+                (sx, sy): [
+                    rows[1 + sy][1 + 16 * bx + sx : 17 + 16 * bx + sx, 128 * half : 128 * half + 128]
+                    for half in range(2)
+                ]
+                for sx, sy in STAR
+            }
+            inside = row != (0 if bx == 0 else 15)
+            parts = pair_terms(grid, [keep & inside for keep in keeps])
+            for n in range(5):
+                add(3 * bx + 2 * side, n, jnp.sum(parts[n], axis=0, keepdims=True))
 
     to_slot, finder = brick_tables(ids[...], targets[...], count[0])
     found = jnp.zeros((8, SLOTS), F32)
@@ -710,19 +758,32 @@
     record[...] = total * jnp.where(row == 1, F32(scale), F32(0.5 * scale))
 
 
-def bricks(parity, count, v, halos, planes, ids, targets):
+def inner_bricks(v):
     return pl.pallas_call(
-        brick_kernel,
+        inner_kernel,
+        out_shape=jax.ShapeDtypeStruct((48, 128), F32),
+        in_specs=vmem_specs(1),
+        out_specs=vmem_specs(1)[0],
+        scratch_shapes=[pltpu.VMEM((2, CX, 64, 128), F32)],
+        compiler_params=pltpu.CompilerParams(vmem_limit_bytes=VMEM_LIMIT),
+        cost_estimate=pl.CostEstimate(flops=20000000, bytes_accessed=6000000, transcendentals=400000),
+        name="inner_bricks",
+    )(v)
+
+
+def edge_bricks(parity, count, inner, v, halos, y_rows, planes, ids, targets):
+    return pl.pallas_call(
+        edge_kernel,
         out_shape=jax.ShapeDtypeStruct((8, SLOTS), F32),
-        in_specs=[pl.BlockSpec(memory_space=pltpu.SMEM)] * 2 + vmem_specs(10),
+        in_specs=[pl.BlockSpec(memory_space=pltpu.SMEM)] * 2 + vmem_specs(12),
         out_specs=vmem_specs(1)[0],
         scratch_shapes=[
-            pltpu.VMEM((2, CX + 2, 64, 128), F32),
+            pltpu.VMEM((2, 3, 64, 128), F32),
             pltpu.VMEM((48, 128), F32),
         ],
         compiler_params=pltpu.CompilerParams(vmem_limit_bytes=VMEM_LIMIT),
-        name="bricks",
-    )(parity, count, v, *halos, planes, ids, targets)
+        name="edge_bricks",
+    )(parity, count, inner, v, *halos, y_rows, planes, ids, targets)
 
 
 def swap(value, axis, phase):
@@ -736,9 +797,9 @@
 
 def exchange(faces):
     xa, xb, ya, yb, za, zb = faces
+    zb = swap(zb, "gz", 1)
     yb = swap(yb, "gy", 1)
     ya = swap(ya, "gy", 0)
-    zb = swap(zb, "gz", 1)
     za = swap(za, "gz", 0)
     xb = swap(xb, "gx", 1)
     xa = swap(xa, "gx", 0)
@@ -760,14 +821,16 @@
     xa, xb, ylo, yhi, own = faces
     xb = swap(xb, "gx", 1)
     xa = swap(xa, "gx", 0)
-    ya, yb = row_faces(parity, xa, xb, ylo, yhi)
+    ya, yb, y_rows = row_faces(parity, xa, xb, ylo, yhi)
+    inner = inner_bricks(v)
     yb = swap(yb, "gy", 1)
     ya = swap(ya, "gy", 0)
+    ya, yb, inner = lax.optimization_barrier((ya, yb, inner))
     planes, za, zb = plane_faces(parity, xa, xb, ya, yb, own)
     zb = swap(zb, "gz", 1)
     za = swap(za, "gz", 0)
-    record = bricks(
-        parity, band_count.reshape(1), v, (xa, xb, ya, yb, za, zb), planes,
+    record = edge_bricks(
+        parity, band_count.reshape(1), inner, v, (xa, xb, ya, yb, za, zb), y_rows, planes,
         band_ids.reshape(1, SLOTS), owners.reshape(1, SLOTS),
     )
     totals = lax.all_to_all(record[:5], ("gx", "gy"), split_axis=1, concat_axis=1, tiled=True)

time: 123 us -> 120 us (0.976)
  waiting for transfers between devices: 21.7 us -> 18 us
    ppermute x24, waiting for transfers between devices: 16.7 us -> 13 us  [swap(): return lax.ppermute(value, axis, pairs)]
    pallas_call x1 -> x2, Pallas kernels: 5.5 us -> 5.7 us  [the longest x1 3.66 us: inner_bricks(): pl.pallas_call(inner_kernel, out_shape=jax.ShapeDtypeStruct((48, 128), F3...]
  transfers between devices with their start and end apart: 25 -> 25, of which waited for: 12 -> 11; matrix products, arithmetic and copies ran while one was open for 0% -> 0% of each run, Pallas kernels for 2% -> 5%
where the time goes in v3:
time: 120 us
  starting transfers between devices  49.7 us (41%)
  Pallas kernels  47.7 us (40%)
  waiting for transfers between devices  18 us (15%)
  local copies, waits for them, and re-layouts  2.82 us (2%)
  between operations  1.42 us (1%)
    ppermute x24, starting transfers between devices, swap(): return lax.ppermute(value, axis, pairs)  42.7 us
    pallas_call x3, Pallas kernels, step(): pl.pallas_call(functools.partial(step_kernel, last), out_shape=[BLOCK] +...  35.7 us
    ppermute x24, waiting for transfers between devices, swap(): return lax.ppermute(value, axis, pairs)  13 us
    all_to_all x1, starting transfers between devices, per_device(): lax.all_to_all(record[:5], ('gx', 'gy'), split_axis=1, concat_axis=1, til...  6.96 us
    all_to_all x1, waiting for transfers between devices, per_device(): lax.all_to_all(record[:5], ('gx', 'gy'), split_axis=1, concat_axis=1, til...  5.02 us
    pallas_call x1, Pallas kernels, inner_bricks(): pl.pallas_call(inner_kernel, out_shape=jax.ShapeDtypeStruct((48, 128), F3...  3.66 us
    pallas_call x1, Pallas kernels, pack(): pl.pallas_call(pack_kernel, out_shape=[BLOCK] * 3 + face_shapes(3), in_sp...  2.8 us
  transfers between devices with their start and end apart: 25, of which 11 were waited for; matrix products, arithmetic and copies ran while one was open for 0% of the time, Pallas kernels for 5%

profile of v3, /device:TPU:1, one launch (start us, length us, event | category | flops | bytes accessed | tf_op | source)
XLA Modules:
  0.0 119.7 jit_solution(6113103658902706472)
XLA Ops:
  0.7 1.4 %copy-done = f32[32,48,256]{2,1,0:T(8,128)S(1)} copy-done((f32[32,48,256]{2,1,0:T(8,128)S(1)}, f32[32,48,256]{2,1,0:T(8,128)}, u32[]{:S(2)}) %copy-start) | copy-done | bytes 1572888
  2.1 2.8 %pack.1 = (f32[32,48,256]{2,1,0:T(8,128)S(1)}, f32[32,48,256]{2,1,0:T(8,128)S(1)}, f32[32,48,256]{2,1,0:T(8,128)S(1)}, f32[3,48,256]{2,1,0:T(8,128)S(1)}, f32[3,...) custom-call(s32[3]{0:T(128)S(1)} %pad_add_fusion.parity, ...), custom_call_target="tpu_custom_call" | custom-call | tf_op jit(solution)/shard_map/pack/pallas_call | solution.py:477
  4.9 3.3 %collective-permute-start = (f32[3,48,256]{2,1,0:T(8,128)S(1)}, f32[3,48,256]{2,1,0:T(8,128)S(1)}, u32[]{:S(2)}, u32[]{:S(2)}) collective-permute-start(f32[3,48,256]{2,1,0:T(8,128)S(1)} %get-tuple-element.45), channel_id=1, source_target_pairs={{0,64},{64,0},{128,192},{192,128},{1,65},{65,1},{129,193},{193,129... | collective-permute-start | bytes 442376 | tf_op jit(solution)/shard_map/ppermute | solution.py:795
  8.3 1.1 collective-permute-start.4
  9.4 2.5 %collective-permute-start.2 = (f32[3,32,256]{2,1,0:T(8,128)S(1)}, f32[3,32,256]{2,1,0:T(8,128)S(1)}, u32[]{:S(2)}, u32[]{:S(2)}) collective-permute-start(f32[3,32,256]{2,1,0:T(8,128)S(1)} %get-tuple-element.47), channel_id=1, source_target_pairs={{0,8},{8,0},{16,24},{24,16},{32,40},{40,32},{48,56},{56,48},{1,9},... | collective-permute-start | bytes 294920 | tf_op jit(solution)/shard_map/ppermute | solution.py:795
  11.8 3.0 %collective-permute-start.3 = (f32[3,32,256]{2,1,0:T(8,128)S(1)}, f32[3,32,256]{2,1,0:T(8,128)S(1)}, u32[]{:S(2)}, u32[]{:S(2)}) collective-permute-start(f32[3,32,256]{2,1,0:T(8,128)S(1)} %get-tuple-element.48), channel_id=1, source_target_pairs={{0,56},{8,16},{16,8},{24,32},{32,24},{40,48},{48,40},{56,0},{1,57}... | collective-permute-start | bytes 294920 | tf_op jit(solution)/shard_map/ppermute | solution.py:795
  14.8 4.7 %collective-permute-start.5 = (f32[8,1536]{1,0:T(8,128)S(1)}, f32[8,1536]{1,0:T(8,128)S(1)}, u32[]{:S(2)}, u32[]{:S(2)}) collective-permute-start(f32[8,1536]{1,0:T(8,128)S(1)} %get-tuple-element.43.zb0.zb_own), channel_id=1, source_target_pairs={{0,7},{1,2},{2,1},{3,4},{4,3},{5,6},{6,5},{7,0},{8,15},{9,10},{10,... | collective-permute-start | bytes 147464 | tf_op jit(solution)/shard_map/ppermute | solution.py:795
  19.5 1.8 %collective-permute-done.5.zb_in = f32[8,1536]{1,0:T(8,128)S(1)} collective-permute-done((f32[8,1536]{1,0:T(8,128)S(1)}, f32[8,1536]{1,0:T(8,128)S(1)}, u32[]{:S(2)}, u32[]{:S(2)}) %collective-permute-start.5) | collective-permute-done | bytes 49184 | tf_op jit(solution)/shard_map/ppermute | solution.py:795
  21.3 11.8 %step.3 = (f32[32,48,256]{2,1,0:T(8,128)S(1)}, f32[3,48,256]{2,1,0:T(8,128)S(1)}, f32[3,48,256]{2,1,0:T(8,128)S(1)}, f32[3,32,256]{2,1,0:T(8,128)S(1)}, f32[3,32...) custom-call(s32[3]{0:T(128)S(1)} %pad_add_fusion.parity, ...), custom_call_target="tpu_custom_call" | custom-call | tf_op jit(solution)/shard_map/step/pallas_call | solution.py:501
  33.1 1.9 %collective-permute-start.6 = (f32[3,48,256]{2,1,0:T(8,128)S(1)}, f32[3,48,256]{2,1,0:T(8,128)S(1)}, u32[]{:S(2)}, u32[]{:S(2)}) collective-permute-start(f32[3,48,256]{2,1,0:T(8,128)S(1)} %get-tuple-element.52), channel_id=1, source_target_pairs={{0,64},{64,0},{128,192},{192,128},{1,65},{65,1},{129,193},{193,129... | collective-permute-start | bytes 442376 | tf_op jit(solution)/shard_map/ppermute | solution.py:795
  35.3 1.3 %collective-permute-start.8 = (f32[3,32,256]{2,1,0:T(8,128)S(1)}, f32[3,32,256]{2,1,0:T(8,128)S(1)}, u32[]{:S(2)}, u32[]{:S(2)}) collective-permute-start(f32[3,32,256]{2,1,0:T(8,128)S(1)} %get-tuple-element.54), channel_id=1, source_target_pairs={{0,8},{8,0},{16,24},{24,16},{32,40},{40,32},{48,56},{56,48},{1,9},... | collective-permute-start | bytes 294920 | tf_op jit(solution)/shard_map/ppermute | solution.py:795
  36.6 1.8 %collective-permute-start.9 = (f32[3,32,256]{2,1,0:T(8,128)S(1)}, f32[3,32,256]{2,1,0:T(8,128)S(1)}, u32[]{:S(2)}, u32[]{:S(2)}) collective-permute-start(f32[3,32,256]{2,1,0:T(8,128)S(1)} %get-tuple-element.55), channel_id=1, source_target_pairs={{0,56},{8,16},{16,8},{24,32},{32,24},{40,48},{48,40},{56,0},{1,57}... | collective-permute-start | bytes 294920 | tf_op jit(solution)/shard_map/ppermute | solution.py:795
  38.5 4.5 %collective-permute-start.11 = (f32[8,1536]{1,0:T(8,128)S(1)}, f32[8,1536]{1,0:T(8,128)S(1)}, u32[]{:S(2)}, u32[]{:S(2)}) collective-permute-start(f32[8,1536]{1,0:T(8,128)S(1)} %get-tuple-element.51.zb_own), channel_id=1, source_target_pairs={{0,7},{1,2},{2,1},{3,4},{4,3},{5,6},{6,5},{7,0},{8,15},{9,10},{10,... | collective-permute-start | bytes 147464 | tf_op jit(solution)/shard_map/ppermute | solution.py:795
  43.0 1.8 %collective-permute-done.11.zb_in = f32[8,1536]{1,0:T(8,128)S(1)} collective-permute-done((f32[8,1536]{1,0:T(8,128)S(1)}, f32[8,1536]{1,0:T(8,128)S(1)}, u32[]{:S(2)}, u32[]{:S(2)}) %collective-permute-start.11) | collective-permute-done | bytes 49184 | tf_op jit(solution)/shard_map/ppermute | solution.py:795
  45.8 11.8 %step.4 = (f32[32,48,256]{2,1,0:T(8,128)S(1)}, f32[3,48,256]{2,1,0:T(8,128)S(1)}, f32[3,48,256]{2,1,0:T(8,128)S(1)}, f32[3,32,256]{2,1,0:T(8,128)S(1)}, f32[3,32...) custom-call(s32[3]{0:T(128)S(1)} %pad_add_fusion.parity, ...), custom_call_target="tpu_custom_call" | custom-call | tf_op jit(solution)/shard_map/step/pallas_call | solution.py:501
  57.6 1.0 collective-permute-start.12
  58.6 1.4 %collective-permute-start.13 = (f32[3,48,256]{2,1,0:T(8,128)S(1)}, f32[3,48,256]{2,1,0:T(8,128)S(1)}, u32[]{:S(2)}, u32[]{:S(2)}) collective-permute-start(f32[3,48,256]{2,1,0:T(8,128)S(1)} %get-tuple-element.60), channel_id=1, source_target_pairs={{0,192},{64,128},{128,64},{192,0},{1,193},{65,129},{129,65},{193,1... | collective-permute-start | bytes 442376 | tf_op jit(solution)/shard_map/ppermute | solution.py:795
  60.1 1.4 %collective-permute-start.14 = (f32[3,32,256]{2,1,0:T(8,128)S(1)}, f32[3,32,256]{2,1,0:T(8,128)S(1)}, u32[]{:S(2)}, u32[]{:S(2)}) collective-permute-start(f32[3,32,256]{2,1,0:T(8,128)S(1)} %get-tuple-element.61), channel_id=1, source_target_pairs={{0,8},{8,0},{16,24},{24,16},{32,40},{40,32},{48,56},{56,48},{1,9},... | collective-permute-start | bytes 294920 | tf_op jit(solution)/shard_map/ppermute | solution.py:795
  61.5 1.8 %collective-permute-start.15 = (f32[3,32,256]{2,1,0:T(8,128)S(1)}, f32[3,32,256]{2,1,0:T(8,128)S(1)}, u32[]{:S(2)}, u32[]{:S(2)}) collective-permute-start(f32[3,32,256]{2,1,0:T(8,128)S(1)} %get-tuple-element.62), channel_id=1, source_target_pairs={{0,56},{8,16},{16,8},{24,32},{32,24},{40,48},{48,40},{56,0},{1,57}... | collective-permute-start | bytes 294920 | tf_op jit(solution)/shard_map/ppermute | solution.py:795
  63.3 4.7 %collective-permute-start.17 = (f32[8,1536]{1,0:T(8,128)S(1)}, f32[8,1536]{1,0:T(8,128)S(1)}, u32[]{:S(2)}, u32[]{:S(2)}) collective-permute-start(f32[8,1536]{1,0:T(8,128)S(1)} %get-tuple-element.58.zb_own), channel_id=1, source_target_pairs={{0,7},{1,2},{2,1},{3,4},{4,3},{5,6},{6,5},{7,0},{8,15},{9,10},{10,... | collective-permute-start | bytes 147464 | tf_op jit(solution)/shard_map/ppermute | solution.py:795
  68.0 1.5 %collective-permute-done.17.zb_in = f32[8,1536]{1,0:T(8,128)S(1)} collective-permute-done((f32[8,1536]{1,0:T(8,128)S(1)}, f32[8,1536]{1,0:T(8,128)S(1)}, u32[]{:S(2)}, u32[]{:S(2)}) %collective-permute-start.17) | collective-permute-done | bytes 49184 | tf_op jit(solution)/shard_map/ppermute | solution.py:795
  69.4 1.7 %collective-permute-done.15.yb_in = f32[3,32,256]{2,1,0:T(8,128)S(1)} collective-permute-done((f32[3,32,256]{2,1,0:T(8,128)S(1)}, f32[3,32,256]{2,1,0:T(8,128)S(1)}, u32[]{:S(2)}, u32[]{:S(2)}) %collective-permute-start.15) | collective-permute-done | bytes 98336 | tf_op jit(solution)/shard_map/ppermute | solution.py:795
  71.2 12.0 %step.5 = (f32[32,48,256]{2,1,0:T(8,128)S(1)}, f32[1,48,256]{2,1,0:T(8,128)S(1)}, f32[1,48,256]{2,1,0:T(8,128)S(1)}, f32[2,32,256]{2,1,0:T(8,128)S(1)}, f32[2,32...) custom-call(s32[3]{0:T(128)S(1)} %pad_add_fusion.parity, f32[32,48,256]{2,1,0:T(8,128)S(1)} %get-tuple-element.40.sigma_in, ...), custom_call_target="tpu_custom_call" | custom-call | tf_op jit(solution)/shard_map/step/pallas_call | solution.py:501
  85.1 2.7 %collective-permute-done.19.xb = f32[1,48,256]{2,1,0:T(8,128)S(1)} collective-permute-done((f32[1,48,256]{2,1,0:T(8,128)S(1)}, f32[1,48,256]{2,1,0:T(8,128)S(1)}, u32[]{:S(2)}, u32[]{:S(2)}) %collective-permute-start.19) | collective-permute-done | bytes 49184 | tf_op jit(solution)/shard_map/ppermute | solution.py:795
  89.1 1.6 %collective-permute-start.21 = (f32[34,256]{1,0:T(8,128)S(1)}, f32[34,256]{1,0:T(8,128)S(1)}, u32[]{:S(2)}, u32[]{:S(2)}) collective-permute-start(f32[34,256]{1,0:T(8,128)S(1)} %get-tuple-element.69), channel_id=1, source_target_pairs={{0,56},{8,16},{16,8},{24,32},{32,24},{40,48},{48,40},{56,0},{1,57}... | collective-permute-start | bytes 104456 | tf_op jit(solution)/shard_map/ppermute | solution.py:795
  90.7 3.7 %inner_bricks.1.inner = f32[48,128]{1,0:T(8,128)S(1)} custom-call(f32[32,48,256]{2,1,0:T(8,128)S(1)} %get-tuple-element.63.mixed.v), custom_call_target="tpu_custom_call" | custom-call | flops 20000000 | bytes 6000000 | tf_op jit(solution)/shard_map/inner_bricks/pallas_call | solution.py:762
  94.4 1.2 collective-permute-done.21.yb
  96.6 4.3 %collective-permute-start.23 = (f32[40,128]{1,0:T(8,128)S(1)}, f32[40,128]{1,0:T(8,128)S(1)}, u32[]{:S(2)}, u32[]{:S(2)}) collective-permute-start(f32[40,128]{1,0:T(8,128)S(1)} %get-tuple-element.75), channel_id=1, source_target_pairs={{0,7},{1,2},{2,1},{3,4},{4,3},{5,6},{6,5},{7,0},{8,15},{9,10},{10,... | collective-permute-start | bytes 61448 | tf_op jit(solution)/shard_map/ppermute | solution.py:795
  102.1 2.0 %edge_bricks.1 = f32[8,64]{1,0:T(8,128)S(1)} custom-call(s32[3]{0:T(128)S(1)} %pad_add_fusion.parity, s32[1]{0:T(128)} %bitcast.9.count, f32[48,128]{1,0:T(8,128)S(1)} %inner_bricks.1.inner, f32[32,48,256]{2,1,0:T(8,128)S(1)} %get-tuple-element.63.mixed.v, f32[1,48,256]{2,1,0:T(8,128)S(1)} %collective-permute-done.18.xa, ...), custom_call_target="tpu_custom_call" | custom-call | tf_op jit(solution)/shard_map/edge_bricks/pallas_call | solution.py:775
  104.9 7.0 %all-to-all-start = ((f32[5,32,2]{0,2,1:T(2,128)}), f32[5,32,2]{0,2,1:T(2,128)S(1)}, u32[]{:S(2)}, u32[]{:S(2)}) async-start(f32[5,32,2]{0,2,1:T(2,128)} %bitcast.6), calls=%async_computation | async-start | bytes 65536 | tf_op jit(solution)/shard_map/all_to_all | solution.py:836
  111.8 2.2 %unpack.1 = f32[32,48,256]{2,1,0:T(8,128)} custom-call(f32[32,48,256]{2,1,0:T(8,128)S(1)} %get-tuple-element.63.mixed.v), custom_call_target="tpu_custom_call" | custom-call | tf_op jit(solution)/shard_map/unpack/pallas_call | solution.py:489
  114.0 5.0 %all-to-all-done = f32[5,32,2]{0,2,1:T(2,128)S(1)} async-done(((f32[5,32,2]{0,2,1:T(2,128)}), f32[5,32,2]{0,2,1:T(2,128)S(1)}, u32[]{:S(2)}, u32[]{:S(2)}) %all-to-all-start) | async-done | bytes 1312 | tf_op jit(solution)/shard_map/all_to_all | solution.py:836
  (36 shorter events, 7.6 us)
Async XLA Ops:
  0.7 1.4 %copy-start = (f32[32,48,256]{2,1,0:T(8,128)S(1)}, f32[32,48,256]{2,1,0:T(8,128)}, u32[]{:S(2)}) copy-start(f32[32,48,256]{2,1,0:T(8,128)} %phi.1) | copy-start | bytes 4718596
  4.9 16.3 %collective-permute-start = (f32[3,48,256]{2,1,0:T(8,128)S(1)}, f32[3,48,256]{2,1,0:T(8,128)S(1)}, u32[]{:S(2)}, u32[]{:S(2)}) collective-permute-start(f32[3,48,256]{2,1,0:T(8,128)S(1)} %get-tuple-element.45), channel_id=1, source_target_pairs={{0,64},{64,0},{128,192},{192,128},{1,65},{65,1},{129,193},{193,129... | collective-permute-start | bytes 442376 | tf_op jit(solution)/shard_map/ppermute | solution.py:795
  8.3 13.0 %collective-permute-start.1 = (f32[3,48,256]{2,1,0:T(8,128)S(1)}, f32[3,48,256]{2,1,0:T(8,128)S(1)}, u32[]{:S(2)}, u32[]{:S(2)}) collective-permute-start(f32[3,48,256]{2,1,0:T(8,128)S(1)} %get-tuple-element.46), channel_id=1, source_target_pairs={{0,192},{64,128},{128,64},{192,0},{1,193},{65,129},{129,65},{193,1... | collective-permute-start | bytes 442376 | tf_op jit(solution)/shard_map/ppermute | solution.py:795
  8.3 6.5 %collective-permute-start.4 = (f32[8,1536]{1,0:T(8,128)S(1)}, f32[8,1536]{1,0:T(8,128)S(1)}, u32[]{:S(2)}, u32[]{:S(2)}) collective-permute-start(f32[8,1536]{1,0:T(8,128)S(1)} %get-tuple-element.42.za0.za_own), channel_id=1, source_target_pairs={{0,1},{1,0},{2,3},{3,2},{4,5},{5,4},{6,7},{7,6},{8,9},{9,8},{10,11... | collective-permute-start | bytes 147464 | tf_op jit(solution)/shard_map/ppermute | solution.py:795
  9.4 11.9 %collective-permute-start.2 = (f32[3,32,256]{2,1,0:T(8,128)S(1)}, f32[3,32,256]{2,1,0:T(8,128)S(1)}, u32[]{:S(2)}, u32[]{:S(2)}) collective-permute-start(f32[3,32,256]{2,1,0:T(8,128)S(1)} %get-tuple-element.47), channel_id=1, source_target_pairs={{0,8},{8,0},{16,24},{24,16},{32,40},{40,32},{48,56},{56,48},{1,9},... | collective-permute-start | bytes 294920 | tf_op jit(solution)/shard_map/ppermute | solution.py:795
  11.8 9.4 %collective-permute-start.3 = (f32[3,32,256]{2,1,0:T(8,128)S(1)}, f32[3,32,256]{2,1,0:T(8,128)S(1)}, u32[]{:S(2)}, u32[]{:S(2)}) collective-permute-start(f32[3,32,256]{2,1,0:T(8,128)S(1)} %get-tuple-element.48), channel_id=1, source_target_pairs={{0,56},{8,16},{16,8},{24,32},{32,24},{40,48},{48,40},{56,0},{1,57}... | collective-permute-start | bytes 294920 | tf_op jit(solution)/shard_map/ppermute | solution.py:795
  14.8 6.4 %collective-permute-start.5 = (f32[8,1536]{1,0:T(8,128)S(1)}, f32[8,1536]{1,0:T(8,128)S(1)}, u32[]{:S(2)}, u32[]{:S(2)}) collective-permute-start(f32[8,1536]{1,0:T(8,128)S(1)} %get-tuple-element.43.zb0.zb_own), channel_id=1, source_target_pairs={{0,7},{1,2},{2,1},{3,4},{4,3},{5,6},{6,5},{7,0},{8,15},{9,10},{10,... | collective-permute-start | bytes 147464 | tf_op jit(solution)/shard_map/ppermute | solution.py:795
  33.1 12.6 %collective-permute-start.6 = (f32[3,48,256]{2,1,0:T(8,128)S(1)}, f32[3,48,256]{2,1,0:T(8,128)S(1)}, u32[]{:S(2)}, u32[]{:S(2)}) collective-permute-start(f32[3,48,256]{2,1,0:T(8,128)S(1)} %get-tuple-element.52), channel_id=1, source_target_pairs={{0,64},{64,0},{128,192},{192,128},{1,65},{65,1},{129,193},{193,129... | collective-permute-start | bytes 442376 | tf_op jit(solution)/shard_map/ppermute | solution.py:795
  35.0 10.7 %collective-permute-start.7 = (f32[3,48,256]{2,1,0:T(8,128)S(1)}, f32[3,48,256]{2,1,0:T(8,128)S(1)}, u32[]{:S(2)}, u32[]{:S(2)}) collective-permute-start(f32[3,48,256]{2,1,0:T(8,128)S(1)} %get-tuple-element.53), channel_id=1, source_target_pairs={{0,192},{64,128},{128,64},{192,0},{1,193},{65,129},{129,65},{193,1... | collective-permute-start | bytes 442376 | tf_op jit(solution)/shard_map/ppermute | solution.py:795
  35.3 3.2 %collective-permute-start.10 = (f32[8,1536]{1,0:T(8,128)S(1)}, f32[8,1536]{1,0:T(8,128)S(1)}, u32[]{:S(2)}, u32[]{:S(2)}) collective-permute-start(f32[8,1536]{1,0:T(8,128)S(1)} %get-tuple-element.50.za_own), channel_id=1, source_target_pairs={{0,1},{1,0},{2,3},{3,2},{4,5},{5,4},{6,7},{7,6},{8,9},{9,8},{10,11... | collective-permute-start | bytes 147464 | tf_op jit(solution)/shard_map/ppermute | solution.py:795
  35.3 9.5 %collective-permute-start.8 = (f32[3,32,256]{2,1,0:T(8,128)S(1)}, f32[3,32,256]{2,1,0:T(8,128)S(1)}, u32[]{:S(2)}, u32[]{:S(2)}) collective-permute-start(f32[3,32,256]{2,1,0:T(8,128)S(1)} %get-tuple-element.54), channel_id=1, source_target_pairs={{0,8},{8,0},{16,24},{24,16},{32,40},{40,32},{48,56},{56,48},{1,9},... | collective-permute-start | bytes 294920 | tf_op jit(solution)/shard_map/ppermute | solution.py:795
  36.6 9.2 %collective-permute-start.9 = (f32[3,32,256]{2,1,0:T(8,128)S(1)}, f32[3,32,256]{2,1,0:T(8,128)S(1)}, u32[]{:S(2)}, u32[]{:S(2)}) collective-permute-start(f32[3,32,256]{2,1,0:T(8,128)S(1)} %get-tuple-element.55), channel_id=1, source_target_pairs={{0,56},{8,16},{16,8},{24,32},{32,24},{40,48},{48,40},{56,0},{1,57}... | collective-permute-start | bytes 294920 | tf_op jit(solution)/shard_map/ppermute | solution.py:795
  38.5 6.3 %collective-permute-start.11 = (f32[8,1536]{1,0:T(8,128)S(1)}, f32[8,1536]{1,0:T(8,128)S(1)}, u32[]{:S(2)}, u32[]{:S(2)}) collective-permute-start(f32[8,1536]{1,0:T(8,128)S(1)} %get-tuple-element.51.zb_own), channel_id=1, source_target_pairs={{0,7},{1,2},{2,1},{3,4},{4,3},{5,6},{6,5},{7,0},{8,15},{9,10},{10,... | collective-permute-start | bytes 147464 | tf_op jit(solution)/shard_map/ppermute | solution.py:795
  57.6 13.6 %collective-permute-start.12 = (f32[3,48,256]{2,1,0:T(8,128)S(1)}, f32[3,48,256]{2,1,0:T(8,128)S(1)}, u32[]{:S(2)}, u32[]{:S(2)}) collective-permute-start(f32[3,48,256]{2,1,0:T(8,128)S(1)} %get-tuple-element.59), channel_id=1, source_target_pairs={{0,64},{64,0},{128,192},{192,128},{1,65},{65,1},{129,193},{193,129... | collective-permute-start | bytes 442376 | tf_op jit(solution)/shard_map/ppermute | solution.py:795
  58.6 12.5 %collective-permute-start.13 = (f32[3,48,256]{2,1,0:T(8,128)S(1)}, f32[3,48,256]{2,1,0:T(8,128)S(1)}, u32[]{:S(2)}, u32[]{:S(2)}) collective-permute-start(f32[3,48,256]{2,1,0:T(8,128)S(1)} %get-tuple-element.60), channel_id=1, source_target_pairs={{0,192},{64,128},{128,64},{192,0},{1,193},{65,129},{129,65},{193,1... | collective-permute-start | bytes 442376 | tf_op jit(solution)/shard_map/ppermute | solution.py:795
  60.1 3.2 %collective-permute-start.16 = (f32[8,1536]{1,0:T(8,128)S(1)}, f32[8,1536]{1,0:T(8,128)S(1)}, u32[]{:S(2)}, u32[]{:S(2)}) collective-permute-start(f32[8,1536]{1,0:T(8,128)S(1)} %get-tuple-element.57.za_own), channel_id=1, source_target_pairs={{0,1},{1,0},{2,3},{3,2},{4,5},{5,4},{6,7},{7,6},{8,9},{9,8},{10,11... | collective-permute-start | bytes 147464 | tf_op jit(solution)/shard_map/ppermute | solution.py:795
  60.1 9.4 %collective-permute-start.14 = (f32[3,32,256]{2,1,0:T(8,128)S(1)}, f32[3,32,256]{2,1,0:T(8,128)S(1)}, u32[]{:S(2)}, u32[]{:S(2)}) collective-permute-start(f32[3,32,256]{2,1,0:T(8,128)S(1)} %get-tuple-element.61), channel_id=1, source_target_pairs={{0,8},{8,0},{16,24},{24,16},{32,40},{40,32},{48,56},{56,48},{1,9},... | collective-permute-start | bytes 294920 | tf_op jit(solution)/shard_map/ppermute | solution.py:795
  61.5 9.7 %collective-permute-start.15 = (f32[3,32,256]{2,1,0:T(8,128)S(1)}, f32[3,32,256]{2,1,0:T(8,128)S(1)}, u32[]{:S(2)}, u32[]{:S(2)}) collective-permute-start(f32[3,32,256]{2,1,0:T(8,128)S(1)} %get-tuple-element.62), channel_id=1, source_target_pairs={{0,56},{8,16},{16,8},{24,32},{32,24},{40,48},{48,40},{56,0},{1,57}... | collective-permute-start | bytes 294920 | tf_op jit(solution)/shard_map/ppermute | solution.py:795
  63.3 6.1 %collective-permute-start.17 = (f32[8,1536]{1,0:T(8,128)S(1)}, f32[8,1536]{1,0:T(8,128)S(1)}, u32[]{:S(2)}, u32[]{:S(2)}) collective-permute-start(f32[8,1536]{1,0:T(8,128)S(1)} %get-tuple-element.58.zb_own), channel_id=1, source_target_pairs={{0,7},{1,2},{2,1},{3,4},{4,3},{5,6},{6,5},{7,0},{8,15},{9,10},{10,... | collective-permute-start | bytes 147464 | tf_op jit(solution)/shard_map/ppermute | solution.py:795
  83.2 18.9 %copy-start.1 = (s32[1,1,1,64]{3,2,1,0:T(1,128)S(1)}, s32[1,1,1,64]{3,2,1,0:T(1,128)}, u32[]{:S(2)}) copy-start(s32[1,1,1,64]{3,2,1,0:T(1,128)} %param.5) | copy-start | bytes 772
  83.2 18.9 %copy-start.2 = (s32[1,1,1,64]{3,2,1,0:T(1,128)S(1)}, s32[1,1,1,64]{3,2,1,0:T(1,128)}, u32[]{:S(2)}) copy-start(s32[1,1,1,64]{3,2,1,0:T(1,128)} %param.7) | copy-start | bytes 772
  83.2 1.9 %collective-permute-start.18 = (f32[1,48,256]{2,1,0:T(8,128)S(1)}, f32[1,48,256]{2,1,0:T(8,128)S(1)}, u32[]{:S(2)}, u32[]{:S(2)}) collective-permute-start(f32[1,48,256]{2,1,0:T(8,128)S(1)} %get-tuple-element.64), channel_id=1, source_target_pairs={{0,64},{64,0},{128,192},{192,128},{1,65},{65,1},{129,193},{193,129... | collective-permute-start | bytes 147464 | tf_op jit(solution)/shard_map/ppermute | solution.py:795
  84.2 3.5 %collective-permute-start.19 = (f32[1,48,256]{2,1,0:T(8,128)S(1)}, f32[1,48,256]{2,1,0:T(8,128)S(1)}, u32[]{:S(2)}, u32[]{:S(2)}) collective-permute-start(f32[1,48,256]{2,1,0:T(8,128)S(1)} %get-tuple-element.65), channel_id=1, source_target_pairs={{0,192},{64,128},{128,64},{192,0},{1,193},{65,129},{129,65},{193,1... | collective-permute-start | bytes 147464 | tf_op jit(solution)/shard_map/ppermute | solution.py:795
  88.3 6.0 %collective-permute-start.20 = (f32[34,256]{1,0:T(8,128)S(1)}, f32[34,256]{1,0:T(8,128)S(1)}, u32[]{:S(2)}, u32[]{:S(2)}) collective-permute-start(f32[34,256]{1,0:T(8,128)S(1)} %get-tuple-element.68), channel_id=1, source_target_pairs={{0,8},{8,0},{16,24},{24,16},{32,40},{40,32},{48,56},{56,48},{1,9},... | collective-permute-start | bytes 104456 | tf_op jit(solution)/shard_map/ppermute | solution.py:795
  89.1 6.5 %collective-permute-start.21 = (f32[34,256]{1,0:T(8,128)S(1)}, f32[34,256]{1,0:T(8,128)S(1)}, u32[]{:S(2)}, u32[]{:S(2)}) collective-permute-start(f32[34,256]{1,0:T(8,128)S(1)} %get-tuple-element.69), channel_id=1, source_target_pairs={{0,56},{8,16},{16,8},{24,32},{32,24},{40,48},{48,40},{56,0},{1,57}... | collective-permute-start | bytes 104456 | tf_op jit(solution)/shard_map/ppermute | solution.py:795
  96.3 5.3 %collective-permute-start.22 = (f32[40,128]{1,0:T(8,128)S(1)}, f32[40,128]{1,0:T(8,128)S(1)}, u32[]{:S(2)}, u32[]{:S(2)}) collective-permute-start(f32[40,128]{1,0:T(8,128)S(1)} %get-tuple-element.74), channel_id=1, source_target_pairs={{0,1},{1,0},{2,3},{3,2},{4,5},{5,4},{6,7},{7,6},{8,9},{9,8},{10,11... | collective-permute-start | bytes 61448 | tf_op jit(solution)/shard_map/ppermute | solution.py:795
  96.6 5.5 %collective-permute-start.23 = (f32[40,128]{1,0:T(8,128)S(1)}, f32[40,128]{1,0:T(8,128)S(1)}, u32[]{:S(2)}, u32[]{:S(2)}) collective-permute-start(f32[40,128]{1,0:T(8,128)S(1)} %get-tuple-element.75), channel_id=1, source_target_pairs={{0,7},{1,2},{2,1},{3,4},{4,3},{5,6},{6,5},{7,0},{8,15},{9,10},{10,... | collective-permute-start | bytes 61448 | tf_op jit(solution)/shard_map/ppermute | solution.py:795
  104.9 14.2 %all-to-all-start = ((f32[5,32,2]{0,2,1:T(2,128)}), f32[5,32,2]{0,2,1:T(2,128)S(1)}, u32[]{:S(2)}, u32[]{:S(2)}) async-start(f32[5,32,2]{0,2,1:T(2,128)} %bitcast.6), calls=%async_computation | async-start | bytes 65536 | tf_op jit(solution)/shard_map/all_to_all | solution.py:836

commit v4 on v3

--- a/solution.py
+++ b/solution.py
@@ -10,6 +10,8 @@
 STEPS = 3
 BRICK = 16
 SLOTS = 64
+Z_SENT = 32
+PEERS = 32
 CX, CY, CZ = 32, 48, 256
 ROWS = CX * CY
 YT = CY // 8
@@ -135,13 +137,32 @@
 def write_swap(parity, low, high, out_a, out_b):
     odd = parity == 1
     out_a[...] = jnp.where(odd, low, high)
-    out_b[...] = jnp.where(odd, high, low)
-
-
-def write_faces(parity, source, xa, xb, ya, yb, za, zb, yf, zf):
+    if out_b.shape == out_a.shape:
+        out_b[...] = jnp.where(odd, high, low)
+    else:
+        out_b[...] = jnp.zeros(out_b.shape, F32)
+        out_b[0:8] = jnp.where(odd, high, low)
+
+
+def side_faces_kernel(with_signs, parity, source, *refs):
+    xa, xb, ya, yb = refs[:4]
+    yf = refs[-1]
     y_faces(source, yf.at[0], yf.at[1], 3)
     write_swap(parity[1], yf[0], yf[1], ya, yb)
     write_swap(parity[0], source[0:3], source[CX - 3 : CX], xa, xb)
+    if with_signs:
+        sigma, pace = refs[4:6]
+
+        def signs(x, carry):
+            value = source[x]
+            sigma[x] = sigma_of(value)
+            pace[x] = (0.05 * value) * lax.rsqrt(value * value + 1.0)
+            return carry
+
+        lax.fori_loop(0, CX, signs, 0)
+
+
+def write_z_faces(parity, source, za, zb, zf):
     z_faces(source, zf.at[0], zf.at[1])
     write_swap(parity[2], zf[0], zf[1], za, zb)
 
@@ -151,7 +172,7 @@
     return jnp.where(odd, part_a, part_b), jnp.where(odd, part_b, part_a)
 
 
-def pack_kernel(parity, phi, mixed, sigma, pace, xa, xb, ya, yb, za, zb, turned, yf, zf):
+def pack_kernel(parity, phi, mixed, za, zb, turned, zf):
     for chunk in range(CX // 8):
         planes = slice(8 * chunk, 8 * chunk + 8)
         for half in range(2):
@@ -163,14 +184,7 @@
             part = [turned[c, pl.ds(which, 128, stride=2), :].T for c in range(3)]
             part = jnp.concatenate(part, axis=0)
             mixed[planes, :, 128 * which : 128 * which + 128] = part.reshape(8, CY, 128)
-    def signs(x, carry):
-        value = mixed[x]
-        sigma[x] = sigma_of(value)
-        pace[x] = (0.05 * value) * lax.rsqrt(value * value + 1.0)
-        return carry
-
-    lax.fori_loop(0, CX, signs, 0)
-    write_faces(parity, mixed, xa, xb, ya, yb, za, zb, yf, zf)
+    write_z_faces(parity, mixed, za, zb, zf)
 
 
 def unpack_kernel(mixed, out, turned):
@@ -192,7 +206,7 @@
     parity, sigma_in, pace, za0, zb0, v, za_own, zb_own, xa_in, xb_in, ya_in, yb_in, za_in, zb_in,
     *refs,
 ):
-    faces = 6 if last else 7
+    faces = 6 if last else 3
     step_body(last, parity, sigma_in, pace, za0, zb0, v, za_own, zb_own, xa_in, xb_in, ya_in,
               yb_in, za_in, zb_in, refs[:faces], *refs[faces:])
 
@@ -221,9 +235,9 @@
                 vs[zt, x, 8 + CY + k : 9 + CY + k, :] = yf[1, k, x : x + 1, lanes]
     xh[0], xh[1] = low_high(parity[0], xa_in[...], xb_in[...])
 
-    z_low, z_high = low_high(parity[2], za_in[...], zb_in[...])
-    zlo0, zhi0 = low_high(parity[2], za0[...], zb0[...])
-    zlo_own, zhi_own = low_high(parity[2], za_own[...], zb_own[...])
+    z_low, z_high = low_high(parity[2], za_in[...], zb_in[0:8])
+    zlo0, zhi0 = low_high(parity[2], za0[...], zb0[0:8])
+    zlo_own, zhi_own = low_high(parity[2], za_own[...], zb_own[0:8])
     window[5:8, :] = z_low[5:8]
     window[8:16, :] = zlo_own
     fixed = edge_column(window, zu_ref, zp_ref, 6, 7, sigma_of(zlo0))
@@ -392,7 +406,7 @@
                     planes[half, at, 0:CY] = part[0:1, lanes]
                     planes[2 + half, at, 0:CY] = part[127:128, lanes]
     else:
-        write_faces(parity, out, *outs[1:], yf, zf)
+        write_z_faces(parity, out, *outs[1:], zf)
 
 
 def rows_kernel(parity, xa, xb, ylo, yhi, ya, yb, y_rows):
@@ -473,16 +487,34 @@
     return [pl.BlockSpec(memory_space=pltpu.SMEM)] + vmem_specs(count)
 
 
+Z_FACE = jax.ShapeDtypeStruct((8, ROWS), F32)
+Z_LONG = jax.ShapeDtypeStruct((Z_SENT, ROWS), F32)
+
+
 def pack(parity, phi):
     return pl.pallas_call(
         pack_kernel,
-        out_shape=[BLOCK] * 3 + face_shapes(3),
+        out_shape=[BLOCK, Z_FACE, Z_LONG],
         in_specs=parity_specs(1),
-        out_specs=vmem_specs(9),
-        scratch_shapes=[pltpu.VMEM((3, CZ, 128), F32)] + FACE_SCRATCH,
+        out_specs=vmem_specs(3),
+        scratch_shapes=[pltpu.VMEM((3, CZ, 128), F32), pltpu.VMEM((2, 8, ROWS), F32)],
         compiler_params=pltpu.CompilerParams(vmem_limit_bytes=VMEM_LIMIT),
         name="pack",
     )(parity, phi)
+
+
+def side_faces(parity, source, with_signs):
+    shapes = face_shapes(3)[:4] + [BLOCK] * (2 if with_signs else 0)
+    return pl.pallas_call(
+        functools.partial(side_faces_kernel, with_signs),
+        out_shape=shapes,
+        in_specs=parity_specs(1),
+        out_specs=vmem_specs(len(shapes)),
+        scratch_shapes=[pltpu.VMEM((2, 3, CX, CZ), F32)],
+        compiler_params=pltpu.CompilerParams(vmem_limit_bytes=VMEM_LIMIT),
+        cost_estimate=pl.CostEstimate(flops=20000000, bytes_accessed=6000000, transcendentals=400000),
+        name="side_faces",
+    )(parity, source)
 
 
 def unpack(mixed):
@@ -500,9 +532,9 @@
 def step(parity, sigma_in, pace, za0, zb0, v, za_own, zb_own, halos, last):
     return pl.pallas_call(
         functools.partial(step_kernel, last),
-        out_shape=[BLOCK] + face_shapes(1 if last else 3),
+        out_shape=[BLOCK] + (face_shapes(1) if last else [Z_FACE, Z_LONG]),
         in_specs=parity_specs(13),
-        out_specs=vmem_specs(6 if last else 7),
+        out_specs=vmem_specs(6 if last else 3),
         scratch_shapes=[
             pltpu.VMEM((2, CX, 64, 128), F32),
             pltpu.VMEM((2, CX, CY, 128), F32),
@@ -571,8 +603,9 @@
     down = jnp.sum(jnp.where(row == column, owner, 0.0), axis=1, keepdims=True)
     earlier = (row < column) & (row < live_count) & (down == owner)
     rank = jnp.sum(earlier.astype(F32), axis=0, keepdims=True)
-    slot = jnp.where(live, 2.0 * owner + rank, F32(SLOTS))
-    to_slot = (slot == row.astype(F32)).astype(F32)
+    owner_at = jnp.where(live, owner, F32(SLOTS))
+    peers = lax.broadcasted_iota(jnp.int32, (PEERS, SLOTS), 0).astype(F32)
+    to_slot = [((owner_at == peers) & (rank == F32(c))).astype(F32) for c in range(2)]
 
     def finder(count, brick_of):
         at = lax.broadcasted_iota(jnp.int32, (count, SLOTS), 0)
@@ -752,10 +785,34 @@
                     lambda at: jnp.where(at < CY, 48 * bx + 16 * (at // 16) + 15 * side, -1),
                 ),
             )
-    total = exact_dot(found, to_slot, (((1,), (1,)), ((), ())))
     scale = 2.0 / 3.0 / (BRICK * BRICK)
     row = lax.broadcasted_iota(jnp.int32, (8, SLOTS), 0)
-    record[...] = total * jnp.where(row == 1, F32(scale), F32(0.5 * scale))
+    found = found * jnp.where(row == 1, F32(scale), F32(0.5 * scale))
+    for c in range(2):
+        record[:, 8 * c : 8 * c + 8] = exact_dot(to_slot[c], found, (((1,), (1,)), ((), ())))
+
+
+def arrange_kernel(received, out):
+    source = lax.broadcasted_iota(jnp.int32, (PEERS, SLOTS), 0)
+    slot = lax.broadcasted_iota(jnp.int32, (PEERS, SLOTS), 1)
+    total = jnp.zeros((8, SLOTS), F32)
+    for c in range(2):
+        total = total + exact_dot(
+            received[:, 8 * c : 8 * c + 8], (slot == 2 * source + c).astype(F32),
+            (((0,), (0,)), ((), ())),
+        )
+    out[...] = total[0:5]
+
+
+def arrange(received):
+    return pl.pallas_call(
+        arrange_kernel,
+        out_shape=jax.ShapeDtypeStruct((5, SLOTS), F32),
+        in_specs=vmem_specs(1),
+        out_specs=vmem_specs(1)[0],
+        compiler_params=pltpu.CompilerParams(vmem_limit_bytes=VMEM_LIMIT),
+        name="arrange",
+    )(received)
 
 
 def inner_bricks(v):
@@ -774,7 +831,7 @@
 def edge_bricks(parity, count, inner, v, halos, y_rows, planes, ids, targets):
     return pl.pallas_call(
         edge_kernel,
-        out_shape=jax.ShapeDtypeStruct((8, SLOTS), F32),
+        out_shape=jax.ShapeDtypeStruct((PEERS, 16), F32),
         in_specs=[pl.BlockSpec(memory_space=pltpu.SMEM)] * 2 + vmem_specs(12),
         out_specs=vmem_specs(1)[0],
         scratch_shapes=[
@@ -795,27 +852,27 @@
     return lax.ppermute(value, axis, pairs)
 
 
-def exchange(faces):
-    xa, xb, ya, yb, za, zb = faces
+def exchange(v, za, zb, parity, with_signs):
     zb = swap(zb, "gz", 1)
+    za = swap(za, "gz", 0)
+    xa, xb, ya, yb, *signs = side_faces(parity, v, with_signs)
     yb = swap(yb, "gy", 1)
     ya = swap(ya, "gy", 0)
-    za = swap(za, "gz", 0)
     xb = swap(xb, "gx", 1)
     xa = swap(xa, "gx", 0)
-    return xa, xb, ya, yb, za, zb
+    return (xa, xb, ya, yb, za, zb), signs
 
 
 def per_device(phi_start, band_ids, band_count, owners):
     parity = jnp.stack([lax.axis_index(name) % 2 for name in ("gx", "gy", "gz")])
     parity = parity.astype(jnp.int32)
-    v, sigma, pace, *faces = pack(parity, phi_start)
-    za0, zb0 = faces[4:]
-    for number in range(STEPS):
-        v, *faces = step(
-            parity, sigma, pace, za0, zb0, v, faces[4], faces[5], exchange(faces),
-            number == STEPS - 1,
-        )
+    v, za0, zb0 = pack(parity, phi_start)
+    halos, (sigma, pace) = exchange(v, za0, zb0, parity, True)
+    za, zb = za0, zb0
+    for number in range(STEPS - 1):
+        v, za, zb = step(parity, sigma, pace, za0, zb0, v, za, zb, halos, False)
+        halos, _ = exchange(v, za, zb, parity, False)
+    v, *faces = step(parity, sigma, pace, za0, zb0, v, za, zb, halos, True)
     level_set = unpack(v)
 
     xa, xb, ylo, yhi, own = faces
@@ -833,8 +890,8 @@
         parity, band_count.reshape(1), inner, v, (xa, xb, ya, yb, za, zb), y_rows, planes,
         band_ids.reshape(1, SLOTS), owners.reshape(1, SLOTS),
     )
-    totals = lax.all_to_all(record[:5], ("gx", "gy"), split_axis=1, concat_axis=1, tiled=True)
-    return level_set, totals.reshape(1, 1, 1, 5, SLOTS)
+    received = lax.all_to_all(record, ("gx", "gy"), split_axis=0, concat_axis=0, tiled=True)
+    return level_set, arrange(received).reshape(1, 1, 1, 5, SLOTS)
 
 
 def solution(mesh):

time: 120 us -> 129 us (1.075)
  waiting for transfers between devices: 18 us -> 30.8 us
  starting transfers between devices: 49.7 us -> 43.9 us
  Pallas kernels: 47.7 us -> 50.4 us
    ppermute x24, waiting for transfers between devices: 13 us -> 26 us  [swap(): return lax.ppermute(value, axis, pairs)]
    ppermute x24, starting transfers between devices: 42.7 us -> 37.3 us  [swap(): return lax.ppermute(value, axis, pairs)]
    pallas_call x2 -> x6, Pallas kernels: 4.84 us -> 7.67 us  [the longest x1 2.73 us: edge_bricks(): pl.pallas_call(edge_kernel, out_shape=jax.ShapeDtypeStruct((PEERS, 16), F...]
  transfers between devices with their start and end apart: 25 -> 25, of which waited for: 11 -> 11; matrix products, arithmetic and copies ran while one was open for 0% -> 0% of each run, Pallas kernels for 5% -> 7%
where the time goes in v4:
time: 129 us
  Pallas kernels  50.4 us (39%)
  starting transfers between devices  43.9 us (34%)
  waiting for transfers between devices  30.8 us (24%)
  local copies, waits for them, and re-layouts  2.07 us (2%)
  between operations  1.46 us (1%)
    ppermute x24, starting transfers between devices, swap(): return lax.ppermute(value, axis, pairs)  37.3 us
    pallas_call x3, Pallas kernels, step(): pl.pallas_call(functools.partial(step_kernel, last), out_shape=[BLOCK] +...  35.6 us
    ppermute x24, waiting for transfers between devices, swap(): return lax.ppermute(value, axis, pairs)  26 us
    all_to_all x1, starting transfers between devices, per_device(): lax.all_to_all(record, ('gx', 'gy'), split_axis=0, concat_axis=0, tiled=T...  6.62 us
    all_to_all x1, waiting for transfers between devices, per_device(): lax.all_to_all(record, ('gx', 'gy'), split_axis=0, concat_axis=0, tiled=T...  4.75 us
    pallas_call x1, Pallas kernels, inner_bricks(): pl.pallas_call(inner_kernel, out_shape=jax.ShapeDtypeStruct((48, 128), F3...  3.66 us
    pallas_call x1, Pallas kernels, edge_bricks(): pl.pallas_call(edge_kernel, out_shape=jax.ShapeDtypeStruct((PEERS, 16), F...  2.73 us
    pallas_call x3, Pallas kernels, side_faces(): pl.pallas_call(functools.partial(side_faces_kernel, with_signs), out_shap...  2.63 us
  transfers between devices with their start and end apart: 25, of which 11 were waited for; matrix products, arithmetic and copies ran while one was open for 0% of the time, Pallas kernels for 7%

profile of v4, /device:TPU:1, one launch (start us, length us, event | category | flops | bytes accessed | tf_op | source)
XLA Modules:
  0.0 128.7 jit_solution(5404260507633421556)
XLA Ops:
  0.7 1.4 %copy-done = f32[32,48,256]{2,1,0:T(8,128)S(1)} copy-done((f32[32,48,256]{2,1,0:T(8,128)S(1)}, f32[32,48,256]{2,1,0:T(8,128)}, u32[]{:S(2)}) %copy-start) | copy-done | bytes 1572888
  2.1 2.1 %pack.1 = (f32[32,48,256]{2,1,0:T(8,128)S(1)}, f32[8,1536]{1,0:T(8,128)S(1)}, f32[32,1536]{1,0:T(8,128)S(1)}) custom-call(s32[3]{0:T(128)S(1)} %pad_add_fusion.parity, f32[32,48,256]{2,1,0:T(8,128)S(1)} %copy-done), custom_call_target="tpu_custom_call" | custom-call | tf_op jit(solution)/shard_map/pack/pallas_call | solution.py:495
  4.2 6.5 %collective-permute-start.5 = (f32[32,1536]{1,0:T(8,128)S(1)}, f32[32,1536]{1,0:T(8,128)S(1)}, u32[]{:S(2)}, u32[]{:S(2)}) collective-permute-start(f32[32,1536]{1,0:T(8,128)S(1)} %get-tuple-element.44.zb0.zb_own), channel_id=1, source_target_pairs={{0,7},{1,2},{2,1},{3,4},{4,3},{5,6},{6,5},{7,0},{8,15},{9,10},{10,... | collective-permute-start | bytes 589832 | tf_op jit(solution)/shard_map/ppermute | solution.py:852
  10.7 1.3 side_faces.3
  12.0 1.0 collective-permute-start
  13.1 1.2 collective-permute-start.1
  14.2 2.5 %collective-permute-start.2 = (f32[3,32,256]{2,1,0:T(8,128)S(1)}, f32[3,32,256]{2,1,0:T(8,128)S(1)}, u32[]{:S(2)}, u32[]{:S(2)}) collective-permute-start(f32[3,32,256]{2,1,0:T(8,128)S(1)} %get-tuple-element.47), channel_id=1, source_target_pairs={{0,8},{8,0},{16,24},{24,16},{32,40},{40,32},{48,56},{56,48},{1,9},... | collective-permute-start | bytes 294920 | tf_op jit(solution)/shard_map/ppermute | solution.py:852
  16.7 3.0 %collective-permute-start.3 = (f32[3,32,256]{2,1,0:T(8,128)S(1)}, f32[3,32,256]{2,1,0:T(8,128)S(1)}, u32[]{:S(2)}, u32[]{:S(2)}) collective-permute-start(f32[3,32,256]{2,1,0:T(8,128)S(1)} %get-tuple-element.48), channel_id=1, source_target_pairs={{0,56},{8,16},{16,8},{24,32},{32,24},{40,48},{48,40},{56,0},{1,57}... | collective-permute-start | bytes 294920 | tf_op jit(solution)/shard_map/ppermute | solution.py:852
  19.7 3.0 %collective-permute-done.2.ya_in = f32[3,32,256]{2,1,0:T(8,128)S(1)} collective-permute-done((f32[3,32,256]{2,1,0:T(8,128)S(1)}, f32[3,32,256]{2,1,0:T(8,128)S(1)}, u32[]{:S(2)}, u32[]{:S(2)}) %collective-permute-start.2) | collective-permute-done | bytes 98336 | tf_op jit(solution)/shard_map/ppermute | solution.py:852
  22.7 4.6 %collective-permute-done.3.yb_in = f32[3,32,256]{2,1,0:T(8,128)S(1)} collective-permute-done((f32[3,32,256]{2,1,0:T(8,128)S(1)}, f32[3,32,256]{2,1,0:T(8,128)S(1)}, u32[]{:S(2)}, u32[]{:S(2)}) %collective-permute-start.3) | collective-permute-done | bytes 98336 | tf_op jit(solution)/shard_map/ppermute | solution.py:852
  27.2 11.8 %step.3 = (f32[32,48,256]{2,1,0:T(8,128)S(1)}, f32[8,1536]{1,0:T(8,128)S(1)}, f32[32,1536]{1,0:T(8,128)S(1)}) custom-call(s32[3]{0:T(128)S(1)} %pad_add_fusion.parity, f32[32,48,256]{2,1,0:T(8,128)S(1)} %get-tuple-element.41.sigma_in, f32[32,48,256]{2,1,0:T(8,128)S(1)} %get-tuple-element.42.pace, f32[8,1536]{1,0:T(8,128)S(1)} %get-tuple-element.43.za0.za_own, ...), custom_call_target="tpu_custom_call" | custom-call | tf_op jit(solution)/shard_map/step/pallas_call | solution.py:533
  39.0 1.8 %collective-permute-start.11 = (f32[32,1536]{1,0:T(8,128)S(1)}, f32[32,1536]{1,0:T(8,128)S(1)}, u32[]{:S(2)}, u32[]{:S(2)}) collective-permute-start(f32[32,1536]{1,0:T(8,128)S(1)} %get-tuple-element.51.zb_own), channel_id=1, source_target_pairs={{0,7},{1,2},{2,1},{3,4},{4,3},{5,6},{6,5},{7,0},{8,15},{9,10},{10,... | collective-permute-start | bytes 589832 | tf_op jit(solution)/shard_map/ppermute | solution.py:852
  42.2 1.6 %collective-permute-start.6 = (f32[3,48,256]{2,1,0:T(8,128)S(1)}, f32[3,48,256]{2,1,0:T(8,128)S(1)}, u32[]{:S(2)}, u32[]{:S(2)}) collective-permute-start(f32[3,48,256]{2,1,0:T(8,128)S(1)} %get-tuple-element.52), channel_id=1, source_target_pairs={{0,64},{64,0},{128,192},{192,128},{1,65},{65,1},{129,193},{193,129... | collective-permute-start | bytes 442376 | tf_op jit(solution)/shard_map/ppermute | solution.py:852
  43.9 3.1 %collective-permute-start.9 = (f32[3,32,256]{2,1,0:T(8,128)S(1)}, f32[3,32,256]{2,1,0:T(8,128)S(1)}, u32[]{:S(2)}, u32[]{:S(2)}) collective-permute-start(f32[3,32,256]{2,1,0:T(8,128)S(1)} %get-tuple-element.55), channel_id=1, source_target_pairs={{0,56},{8,16},{16,8},{24,32},{32,24},{40,48},{48,40},{56,0},{1,57}... | collective-permute-start | bytes 294920 | tf_op jit(solution)/shard_map/ppermute | solution.py:852
  47.0 2.6 %collective-permute-done.8.ya_in = f32[3,32,256]{2,1,0:T(8,128)S(1)} collective-permute-done((f32[3,32,256]{2,1,0:T(8,128)S(1)}, f32[3,32,256]{2,1,0:T(8,128)S(1)}, u32[]{:S(2)}, u32[]{:S(2)}) %collective-permute-start.8) | collective-permute-done | bytes 98336 | tf_op jit(solution)/shard_map/ppermute | solution.py:852
  49.6 2.8 %collective-permute-done.9.yb_in = f32[3,32,256]{2,1,0:T(8,128)S(1)} collective-permute-done((f32[3,32,256]{2,1,0:T(8,128)S(1)}, f32[3,32,256]{2,1,0:T(8,128)S(1)}, u32[]{:S(2)}, u32[]{:S(2)}) %collective-permute-start.9) | collective-permute-done | bytes 98336 | tf_op jit(solution)/shard_map/ppermute | solution.py:852
  52.4 11.8 %step.4 = (f32[32,48,256]{2,1,0:T(8,128)S(1)}, f32[8,1536]{1,0:T(8,128)S(1)}, f32[32,1536]{1,0:T(8,128)S(1)}) custom-call(s32[3]{0:T(128)S(1)} %pad_add_fusion.parity, f32[32,48,256]{2,1,0:T(8,128)S(1)} %get-tuple-element.41.sigma_in, f32[32,48,256]{2,1,0:T(8,128)S(1)} %get-tuple-element.42.pace, f32[8,1536]{1,0:T(8,128)S(1)} %get-tuple-element.43.za0.za_own, ...), custom_call_target="tpu_custom_call" | custom-call | tf_op jit(solution)/shard_map/step/pallas_call | solution.py:533
  66.5 2.5 %collective-permute-start.12 = (f32[3,48,256]{2,1,0:T(8,128)S(1)}, f32[3,48,256]{2,1,0:T(8,128)S(1)}, u32[]{:S(2)}, u32[]{:S(2)}) collective-permute-start(f32[3,48,256]{2,1,0:T(8,128)S(1)} %get-tuple-element.59), channel_id=1, source_target_pairs={{0,64},{64,0},{128,192},{192,128},{1,65},{65,1},{129,193},{193,129... | collective-permute-start | bytes 442376 | tf_op jit(solution)/shard_map/ppermute | solution.py:852
  69.1 2.1 %collective-permute-start.14 = (f32[3,32,256]{2,1,0:T(8,128)S(1)}, f32[3,32,256]{2,1,0:T(8,128)S(1)}, u32[]{:S(2)}, u32[]{:S(2)}) collective-permute-start(f32[3,32,256]{2,1,0:T(8,128)S(1)} %get-tuple-element.61), channel_id=1, source_target_pairs={{0,8},{8,0},{16,24},{24,16},{32,40},{40,32},{48,56},{56,48},{1,9},... | collective-permute-start | bytes 294920 | tf_op jit(solution)/shard_map/ppermute | solution.py:852
  71.2 3.4 %collective-permute-start.15 = (f32[3,32,256]{2,1,0:T(8,128)S(1)}, f32[3,32,256]{2,1,0:T(8,128)S(1)}, u32[]{:S(2)}, u32[]{:S(2)}) collective-permute-start(f32[3,32,256]{2,1,0:T(8,128)S(1)} %get-tuple-element.62), channel_id=1, source_target_pairs={{0,56},{8,16},{16,8},{24,32},{32,24},{40,48},{48,40},{56,0},{1,57}... | collective-permute-start | bytes 294920 | tf_op jit(solution)/shard_map/ppermute | solution.py:852
  74.6 2.5 %collective-permute-done.14.ya_in = f32[3,32,256]{2,1,0:T(8,128)S(1)} collective-permute-done((f32[3,32,256]{2,1,0:T(8,128)S(1)}, f32[3,32,256]{2,1,0:T(8,128)S(1)}, u32[]{:S(2)}, u32[]{:S(2)}) %collective-permute-start.14) | collective-permute-done | bytes 98336 | tf_op jit(solution)/shard_map/ppermute | solution.py:852
  77.0 5.5 %collective-permute-done.15.yb_in = f32[3,32,256]{2,1,0:T(8,128)S(1)} collective-permute-done((f32[3,32,256]{2,1,0:T(8,128)S(1)}, f32[3,32,256]{2,1,0:T(8,128)S(1)}, u32[]{:S(2)}, u32[]{:S(2)}) %collective-permute-start.15) | collective-permute-done | bytes 98336 | tf_op jit(solution)/shard_map/ppermute | solution.py:852
  82.6 12.0 %step.5 = (f32[32,48,256]{2,1,0:T(8,128)S(1)}, f32[1,48,256]{2,1,0:T(8,128)S(1)}, f32[1,48,256]{2,1,0:T(8,128)S(1)}, f32[2,32,256]{2,1,0:T(8,128)S(1)}, f32[2,32...) custom-call(s32[3]{0:T(128)S(1)} %pad_add_fusion.parity, f32[32,48,256]{2,1,0:T(8,128)S(1)} %get-tuple-element.41.sigma_in, ...), custom_call_target="tpu_custom_call" | custom-call | tf_op jit(solution)/shard_map/step/pallas_call | solution.py:533
  94.6 1.1 collective-permute-start.18
  96.6 2.7 %collective-permute-done.19.xb = f32[1,48,256]{2,1,0:T(8,128)S(1)} collective-permute-done((f32[1,48,256]{2,1,0:T(8,128)S(1)}, f32[1,48,256]{2,1,0:T(8,128)S(1)}, u32[]{:S(2)}, u32[]{:S(2)}) %collective-permute-start.19) | collective-permute-done | bytes 49184 | tf_op jit(solution)/shard_map/ppermute | solution.py:852
  99.9 1.9 %collective-permute-start.21 = (f32[34,256]{1,0:T(8,128)S(1)}, f32[34,256]{1,0:T(8,128)S(1)}, u32[]{:S(2)}, u32[]{:S(2)}) collective-permute-start(f32[34,256]{1,0:T(8,128)S(1)} %get-tuple-element.69), channel_id=1, source_target_pairs={{0,56},{8,16},{16,8},{24,32},{32,24},{40,48},{48,40},{56,0},{1,57}... | collective-permute-start | bytes 104456 | tf_op jit(solution)/shard_map/ppermute | solution.py:852
  101.9 3.7 %inner_bricks.1.inner = f32[48,128]{1,0:T(8,128)S(1)} custom-call(f32[32,48,256]{2,1,0:T(8,128)S(1)} %get-tuple-element.63.mixed.v), custom_call_target="tpu_custom_call" | custom-call | flops 20000000 | bytes 6000000 | tf_op jit(solution)/shard_map/inner_bricks/pallas_call | solution.py:819
  107.6 2.7 %collective-permute-start.23 = (f32[40,128]{1,0:T(8,128)S(1)}, f32[40,128]{1,0:T(8,128)S(1)}, u32[]{:S(2)}, u32[]{:S(2)}) collective-permute-start(f32[40,128]{1,0:T(8,128)S(1)} %get-tuple-element.75), channel_id=1, source_target_pairs={{0,7},{1,2},{2,1},{3,4},{4,3},{5,6},{6,5},{7,0},{8,15},{9,10},{10,... | collective-permute-start | bytes 61448 | tf_op jit(solution)/shard_map/ppermute | solution.py:852
  111.5 2.7 %edge_bricks.1 = f32[32,16]{1,0:T(8,128)} custom-call(s32[3]{0:T(128)S(1)} %pad_add_fusion.parity, s32[1]{0:T(128)} %bitcast.11.count, f32[48,128]{1,0:T(8,128)S(1)} %inner_bricks.1.inner, f32[32,48,256]{2,1,0:T(8,128)S(1)} %get-tuple-element.63.mixed.v, f32[1,48,256]{2,1,0:T(8,128)S(1)} %collective-permute-done.18.xa, ...), custom_call_target="tpu_custom_call" | custom-call | tf_op jit(solution)/shard_map/edge_bricks/pallas_call | solution.py:832
  114.2 6.6 %all-to-all-start = ((f32[32,1,16]{2,1,0:T(1,128)}), f32[32,1,16]{2,1,0:T(1,128)S(1)}, u32[]{:S(2)}, u32[]{:S(2)}) async-start(f32[32,1,16]{2,1,0:T(1,128)} %bitcast.7), calls=%async_computation | async-start | bytes 32768 | tf_op jit(solution)/shard_map/all_to_all | solution.py:893
  120.8 2.2 %unpack.1 = f32[32,48,256]{2,1,0:T(8,128)} custom-call(f32[32,48,256]{2,1,0:T(8,128)S(1)} %get-tuple-element.63.mixed.v), custom_call_target="tpu_custom_call" | custom-call | tf_op jit(solution)/shard_map/unpack/pallas_call | solution.py:521
  123.0 4.8 %all-to-all-done = f32[32,1,16]{2,1,0:T(1,128)S(1)} async-done(((f32[32,1,16]{2,1,0:T(1,128)}), f32[32,1,16]{2,1,0:T(1,128)S(1)}, u32[]{:S(2)}, u32[]{:S(2)}) %all-to-all-start) | async-done | bytes 2080 | tf_op jit(solution)/shard_map/all_to_all | solution.py:893
  (39 shorter events, 8.9 us)
Async XLA Ops:
  0.7 1.4 %copy-start = (f32[32,48,256]{2,1,0:T(8,128)S(1)}, f32[32,48,256]{2,1,0:T(8,128)}, u32[]{:S(2)}) copy-start(f32[32,48,256]{2,1,0:T(8,128)} %phi.1) | copy-start | bytes 4718596
  4.2 23.0 %collective-permute-start.5 = (f32[32,1536]{1,0:T(8,128)S(1)}, f32[32,1536]{1,0:T(8,128)S(1)}, u32[]{:S(2)}, u32[]{:S(2)}) collective-permute-start(f32[32,1536]{1,0:T(8,128)S(1)} %get-tuple-element.44.zb0.zb_own), channel_id=1, source_target_pairs={{0,7},{1,2},{2,1},{3,4},{4,3},{5,6},{6,5},{7,0},{8,15},{9,10},{10,... | collective-permute-start | bytes 589832 | tf_op jit(solution)/shard_map/ppermute | solution.py:852
  10.7 6.0 %collective-permute-start.4 = (f32[8,1536]{1,0:T(8,128)S(1)}, f32[8,1536]{1,0:T(8,128)S(1)}, u32[]{:S(2)}, u32[]{:S(2)}) collective-permute-start(f32[8,1536]{1,0:T(8,128)S(1)} %get-tuple-element.43.za0.za_own), channel_id=1, source_target_pairs={{0,1},{1,0},{2,3},{3,2},{4,5},{5,4},{6,7},{7,6},{8,9},{9,8},{10,11... | collective-permute-start | bytes 147464 | tf_op jit(solution)/shard_map/ppermute | solution.py:852
  12.0 15.2 %collective-permute-start = (f32[3,48,256]{2,1,0:T(8,128)S(1)}, f32[3,48,256]{2,1,0:T(8,128)S(1)}, u32[]{:S(2)}, u32[]{:S(2)}) collective-permute-start(f32[3,48,256]{2,1,0:T(8,128)S(1)} %get-tuple-element.45), channel_id=1, source_target_pairs={{0,64},{64,0},{128,192},{192,128},{1,65},{65,1},{129,193},{193,129... | collective-permute-start | bytes 442376 | tf_op jit(solution)/shard_map/ppermute | solution.py:852
  13.1 14.2 %collective-permute-start.1 = (f32[3,48,256]{2,1,0:T(8,128)S(1)}, f32[3,48,256]{2,1,0:T(8,128)S(1)}, u32[]{:S(2)}, u32[]{:S(2)}) collective-permute-start(f32[3,48,256]{2,1,0:T(8,128)S(1)} %get-tuple-element.46), channel_id=1, source_target_pairs={{0,192},{64,128},{128,64},{192,0},{1,193},{65,129},{129,65},{193,1... | collective-permute-start | bytes 442376 | tf_op jit(solution)/shard_map/ppermute | solution.py:852
  14.2 8.4 %collective-permute-start.2 = (f32[3,32,256]{2,1,0:T(8,128)S(1)}, f32[3,32,256]{2,1,0:T(8,128)S(1)}, u32[]{:S(2)}, u32[]{:S(2)}) collective-permute-start(f32[3,32,256]{2,1,0:T(8,128)S(1)} %get-tuple-element.47), channel_id=1, source_target_pairs={{0,8},{8,0},{16,24},{24,16},{32,40},{40,32},{48,56},{56,48},{1,9},... | collective-permute-start | bytes 294920 | tf_op jit(solution)/shard_map/ppermute | solution.py:852
  16.7 10.5 %collective-permute-start.3 = (f32[3,32,256]{2,1,0:T(8,128)S(1)}, f32[3,32,256]{2,1,0:T(8,128)S(1)}, u32[]{:S(2)}, u32[]{:S(2)}) collective-permute-start(f32[3,32,256]{2,1,0:T(8,128)S(1)} %get-tuple-element.48), channel_id=1, source_target_pairs={{0,56},{8,16},{16,8},{24,32},{32,24},{40,48},{48,40},{56,0},{1,57}... | collective-permute-start | bytes 294920 | tf_op jit(solution)/shard_map/ppermute | solution.py:852
  39.0 13.4 %collective-permute-start.11 = (f32[32,1536]{1,0:T(8,128)S(1)}, f32[32,1536]{1,0:T(8,128)S(1)}, u32[]{:S(2)}, u32[]{:S(2)}) collective-permute-start(f32[32,1536]{1,0:T(8,128)S(1)} %get-tuple-element.51.zb_own), channel_id=1, source_target_pairs={{0,7},{1,2},{2,1},{3,4},{4,3},{5,6},{6,5},{7,0},{8,15},{9,10},{10,... | collective-permute-start | bytes 589832 | tf_op jit(solution)/shard_map/ppermute | solution.py:852
  40.8 3.0 %collective-permute-start.10 = (f32[8,1536]{1,0:T(8,128)S(1)}, f32[8,1536]{1,0:T(8,128)S(1)}, u32[]{:S(2)}, u32[]{:S(2)}) collective-permute-start(f32[8,1536]{1,0:T(8,128)S(1)} %get-tuple-element.50.za_own), channel_id=1, source_target_pairs={{0,1},{1,0},{2,3},{3,2},{4,5},{5,4},{6,7},{7,6},{8,9},{9,8},{10,11... | collective-permute-start | bytes 147464 | tf_op jit(solution)/shard_map/ppermute | solution.py:852
  42.2 10.2 %collective-permute-start.6 = (f32[3,48,256]{2,1,0:T(8,128)S(1)}, f32[3,48,256]{2,1,0:T(8,128)S(1)}, u32[]{:S(2)}, u32[]{:S(2)}) collective-permute-start(f32[3,48,256]{2,1,0:T(8,128)S(1)} %get-tuple-element.52), channel_id=1, source_target_pairs={{0,64},{64,0},{128,192},{192,128},{1,65},{65,1},{129,193},{193,129... | collective-permute-start | bytes 442376 | tf_op jit(solution)/shard_map/ppermute | solution.py:852
  43.8 8.6 %collective-permute-start.7 = (f32[3,48,256]{2,1,0:T(8,128)S(1)}, f32[3,48,256]{2,1,0:T(8,128)S(1)}, u32[]{:S(2)}, u32[]{:S(2)}) collective-permute-start(f32[3,48,256]{2,1,0:T(8,128)S(1)} %get-tuple-element.53), channel_id=1, source_target_pairs={{0,192},{64,128},{128,64},{192,0},{1,193},{65,129},{129,65},{193,1... | collective-permute-start | bytes 442376 | tf_op jit(solution)/shard_map/ppermute | solution.py:852
  43.8 5.8 %collective-permute-start.8 = (f32[3,32,256]{2,1,0:T(8,128)S(1)}, f32[3,32,256]{2,1,0:T(8,128)S(1)}, u32[]{:S(2)}, u32[]{:S(2)}) collective-permute-start(f32[3,32,256]{2,1,0:T(8,128)S(1)} %get-tuple-element.54), channel_id=1, source_target_pairs={{0,8},{8,0},{16,24},{24,16},{32,40},{40,32},{48,56},{56,48},{1,9},... | collective-permute-start | bytes 294920 | tf_op jit(solution)/shard_map/ppermute | solution.py:852
  43.9 8.6 %collective-permute-start.9 = (f32[3,32,256]{2,1,0:T(8,128)S(1)}, f32[3,32,256]{2,1,0:T(8,128)S(1)}, u32[]{:S(2)}, u32[]{:S(2)}) collective-permute-start(f32[3,32,256]{2,1,0:T(8,128)S(1)} %get-tuple-element.55), channel_id=1, source_target_pairs={{0,56},{8,16},{16,8},{24,32},{32,24},{40,48},{48,40},{56,0},{1,57}... | collective-permute-start | bytes 294920 | tf_op jit(solution)/shard_map/ppermute | solution.py:852
  64.2 18.3 %collective-permute-start.17 = (f32[32,1536]{1,0:T(8,128)S(1)}, f32[32,1536]{1,0:T(8,128)S(1)}, u32[]{:S(2)}, u32[]{:S(2)}) collective-permute-start(f32[32,1536]{1,0:T(8,128)S(1)} %get-tuple-element.58.zb_own), channel_id=1, source_target_pairs={{0,7},{1,2},{2,1},{3,4},{4,3},{5,6},{6,5},{7,0},{8,15},{9,10},{10,... | collective-permute-start | bytes 589832 | tf_op jit(solution)/shard_map/ppermute | solution.py:852
  65.6 5.6 %collective-permute-start.16 = (f32[8,1536]{1,0:T(8,128)S(1)}, f32[8,1536]{1,0:T(8,128)S(1)}, u32[]{:S(2)}, u32[]{:S(2)}) collective-permute-start(f32[8,1536]{1,0:T(8,128)S(1)} %get-tuple-element.57.za_own), channel_id=1, source_target_pairs={{0,1},{1,0},{2,3},{3,2},{4,5},{5,4},{6,7},{7,6},{8,9},{9,8},{10,11... | collective-permute-start | bytes 147464 | tf_op jit(solution)/shard_map/ppermute | solution.py:852
  66.5 16.0 %collective-permute-start.12 = (f32[3,48,256]{2,1,0:T(8,128)S(1)}, f32[3,48,256]{2,1,0:T(8,128)S(1)}, u32[]{:S(2)}, u32[]{:S(2)}) collective-permute-start(f32[3,48,256]{2,1,0:T(8,128)S(1)} %get-tuple-element.59), channel_id=1, source_target_pairs={{0,64},{64,0},{128,192},{192,128},{1,65},{65,1},{129,193},{193,129... | collective-permute-start | bytes 442376 | tf_op jit(solution)/shard_map/ppermute | solution.py:852
  69.1 13.5 %collective-permute-start.13 = (f32[3,48,256]{2,1,0:T(8,128)S(1)}, f32[3,48,256]{2,1,0:T(8,128)S(1)}, u32[]{:S(2)}, u32[]{:S(2)}) collective-permute-start(f32[3,48,256]{2,1,0:T(8,128)S(1)} %get-tuple-element.60), channel_id=1, source_target_pairs={{0,192},{64,128},{128,64},{192,0},{1,193},{65,129},{129,65},{193,1... | collective-permute-start | bytes 442376 | tf_op jit(solution)/shard_map/ppermute | solution.py:852
  69.1 8.0 %collective-permute-start.14 = (f32[3,32,256]{2,1,0:T(8,128)S(1)}, f32[3,32,256]{2,1,0:T(8,128)S(1)}, u32[]{:S(2)}, u32[]{:S(2)}) collective-permute-start(f32[3,32,256]{2,1,0:T(8,128)S(1)} %get-tuple-element.61), channel_id=1, source_target_pairs={{0,8},{8,0},{16,24},{24,16},{32,40},{40,32},{48,56},{56,48},{1,9},... | collective-permute-start | bytes 294920 | tf_op jit(solution)/shard_map/ppermute | solution.py:852
  71.2 11.4 %collective-permute-start.15 = (f32[3,32,256]{2,1,0:T(8,128)S(1)}, f32[3,32,256]{2,1,0:T(8,128)S(1)}, u32[]{:S(2)}, u32[]{:S(2)}) collective-permute-start(f32[3,32,256]{2,1,0:T(8,128)S(1)} %get-tuple-element.62), channel_id=1, source_target_pairs={{0,56},{8,16},{16,8},{24,32},{32,24},{40,48},{48,40},{56,0},{1,57}... | collective-permute-start | bytes 294920 | tf_op jit(solution)/shard_map/ppermute | solution.py:852
  94.6 16.9 %copy-start.1 = (s32[1,1,1,64]{3,2,1,0:T(1,128)S(1)}, s32[1,1,1,64]{3,2,1,0:T(1,128)}, u32[]{:S(2)}) copy-start(s32[1,1,1,64]{3,2,1,0:T(1,128)} %param.5) | copy-start | bytes 772
  94.6 16.9 %copy-start.2 = (s32[1,1,1,64]{3,2,1,0:T(1,128)S(1)}, s32[1,1,1,64]{3,2,1,0:T(1,128)}, u32[]{:S(2)}) copy-start(s32[1,1,1,64]{3,2,1,0:T(1,128)} %param.7) | copy-start | bytes 772
  94.6 2.0 %collective-permute-start.18 = (f32[1,48,256]{2,1,0:T(8,128)S(1)}, f32[1,48,256]{2,1,0:T(8,128)S(1)}, u32[]{:S(2)}, u32[]{:S(2)}) collective-permute-start(f32[1,48,256]{2,1,0:T(8,128)S(1)} %get-tuple-element.64), channel_id=1, source_target_pairs={{0,64},{64,0},{128,192},{192,128},{1,65},{65,1},{129,193},{193,129... | collective-permute-start | bytes 147464 | tf_op jit(solution)/shard_map/ppermute | solution.py:852
  95.7 3.5 %collective-permute-start.19 = (f32[1,48,256]{2,1,0:T(8,128)S(1)}, f32[1,48,256]{2,1,0:T(8,128)S(1)}, u32[]{:S(2)}, u32[]{:S(2)}) collective-permute-start(f32[1,48,256]{2,1,0:T(8,128)S(1)} %get-tuple-element.65), channel_id=1, source_target_pairs={{0,192},{64,128},{128,64},{192,0},{1,193},{65,129},{129,65},{193,1... | collective-permute-start | bytes 147464 | tf_op jit(solution)/shard_map/ppermute | solution.py:852
  99.8 5.7 %collective-permute-start.20 = (f32[34,256]{1,0:T(8,128)S(1)}, f32[34,256]{1,0:T(8,128)S(1)}, u32[]{:S(2)}, u32[]{:S(2)}) collective-permute-start(f32[34,256]{1,0:T(8,128)S(1)} %get-tuple-element.68), channel_id=1, source_target_pairs={{0,8},{8,0},{16,24},{24,16},{32,40},{40,32},{48,56},{56,48},{1,9},... | collective-permute-start | bytes 104456 | tf_op jit(solution)/shard_map/ppermute | solution.py:852
  99.9 6.6 %collective-permute-start.21 = (f32[34,256]{1,0:T(8,128)S(1)}, f32[34,256]{1,0:T(8,128)S(1)}, u32[]{:S(2)}, u32[]{:S(2)}) collective-permute-start(f32[34,256]{1,0:T(8,128)S(1)} %get-tuple-element.69), channel_id=1, source_target_pairs={{0,56},{8,16},{16,8},{24,32},{32,24},{40,48},{48,40},{56,0},{1,57}... | collective-permute-start | bytes 104456 | tf_op jit(solution)/shard_map/ppermute | solution.py:852
  107.2 3.6 %collective-permute-start.22 = (f32[40,128]{1,0:T(8,128)S(1)}, f32[40,128]{1,0:T(8,128)S(1)}, u32[]{:S(2)}, u32[]{:S(2)}) collective-permute-start(f32[40,128]{1,0:T(8,128)S(1)} %get-tuple-element.74), channel_id=1, source_target_pairs={{0,1},{1,0},{2,3},{3,2},{4,5},{5,4},{6,7},{7,6},{8,9},{9,8},{10,11... | collective-permute-start | bytes 61448 | tf_op jit(solution)/shard_map/ppermute | solution.py:852
  107.6 3.9 %collective-permute-start.23 = (f32[40,128]{1,0:T(8,128)S(1)}, f32[40,128]{1,0:T(8,128)S(1)}, u32[]{:S(2)}, u32[]{:S(2)}) collective-permute-start(f32[40,128]{1,0:T(8,128)S(1)} %get-tuple-element.75), channel_id=1, source_target_pairs={{0,7},{1,2},{2,1},{3,4},{4,3},{5,6},{6,5},{7,0},{8,15},{9,10},{10,... | collective-permute-start | bytes 61448 | tf_op jit(solution)/shard_map/ppermute | solution.py:852
  114.2 13.6 %all-to-all-start = ((f32[32,1,16]{2,1,0:T(1,128)}), f32[32,1,16]{2,1,0:T(1,128)S(1)}, u32[]{:S(2)}, u32[]{:S(2)}) async-start(f32[32,1,16]{2,1,0:T(1,128)} %bitcast.7), calls=%async_computation | async-start | bytes 32768 | tf_op jit(solution)/shard_map/all_to_all | solution.py:893

commit v5 on v3

--- a/solution.py
+++ b/solution.py
@@ -10,6 +10,7 @@
 STEPS = 3
 BRICK = 16
 SLOTS = 64
+PEERS = 32
 CX, CY, CZ = 32, 48, 256
 ROWS = CX * CY
 YT = CY // 8
@@ -187,55 +188,8 @@
             out[planes, :, 128 * half : 128 * half + 128] = part.reshape(8, CY, 128)
 
 
-def step_kernel(
-    last,
-    parity, sigma_in, pace, za0, zb0, v, za_own, zb_own, xa_in, xb_in, ya_in, yb_in, za_in, zb_in,
-    *refs,
-):
-    faces = 6 if last else 7
-    step_body(last, parity, sigma_in, pace, za0, zb0, v, za_own, zb_own, xa_in, xb_in, ya_in,
-              yb_in, za_in, zb_in, refs[:faces], *refs[faces:])
-
-
-def step_body(
-    last,
-    parity, sigma_in, pace, za0, zb0, v, za_own, zb_own, xa_in, xb_in, ya_in, yb_in, za_in, zb_in,
-    outs,
-    vs, summed, u_ref, p_ref, window, zu_ref, zp_ref, edges, fixes, yf, zf, xh,
-    rolled, zs, zp, tots,
-):
-    out = outs[0]
-
-    def fill(x, carry):
-        for zt in range(2):
-            vs[zt, x, 8 : 8 + CY, :] = v[x, :, pl.ds(128 * zt, 128)]
-        return carry
-
-    lax.fori_loop(0, CX, fill, 0)
-    yf[0], yf[1] = low_high(parity[1], ya_in[...], yb_in[...])
-    for x in range(CX):
-        for zt in range(2):
-            lanes = slice(128 * zt, 128 * zt + 128)
-            for k in range(3):
-                vs[zt, x, 5 + k : 6 + k, :] = yf[0, k, x : x + 1, lanes]
-                vs[zt, x, 8 + CY + k : 9 + CY + k, :] = yf[1, k, x : x + 1, lanes]
+def x_kernel(parity, sigma_in, v, xa_in, xb_in, summed, xh):
     xh[0], xh[1] = low_high(parity[0], xa_in[...], xb_in[...])
-
-    z_low, z_high = low_high(parity[2], za_in[...], zb_in[...])
-    zlo0, zhi0 = low_high(parity[2], za0[...], zb0[...])
-    zlo_own, zhi_own = low_high(parity[2], za_own[...], zb_own[...])
-    window[5:8, :] = z_low[5:8]
-    window[8:16, :] = zlo_own
-    fixed = edge_column(window, zu_ref, zp_ref, 6, 7, sigma_of(zlo0))
-    for half, lane_at, cell_at in ((0, 0, 0), (0, 1, 2), (1, 0, 1)):
-        edges[half, lane_at : lane_at + 1, :] = fixed[cell_at : cell_at + 1]
-    window[8:16, :] = zhi_own
-    window[16:19, :] = z_high[0:3]
-    fixed = edge_column(window, zu_ref, zp_ref, 9, 8, sigma_of(zhi0))
-    for half, lane_at, cell_at in ((0, 127, 6), (1, 126, 5), (1, 127, 7)):
-        edges[half, lane_at : lane_at + 1, :] = fixed[cell_at : cell_at + 1]
-    for half in range(2):
-        fixes[half] = edges[half].T
 
     def x_pass(yt, carry):
         row = pl.multiple_of(8 * yt, 8)
@@ -272,6 +226,56 @@
         return carry
 
     lax.fori_loop(0, YT, x_pass, 0)
+
+
+def step_kernel(
+    last,
+    parity, sigma_in, pace, za0, zb0, v, za_own, zb_own, summed, ya_in, yb_in, za_in, zb_in,
+    *refs,
+):
+    faces = 6 if last else 7
+    step_body(last, parity, sigma_in, pace, za0, zb0, v, za_own, zb_own, summed, ya_in,
+              yb_in, za_in, zb_in, refs[:faces], *refs[faces:])
+
+
+def step_body(
+    last,
+    parity, sigma_in, pace, za0, zb0, v, za_own, zb_own, summed, ya_in, yb_in, za_in, zb_in,
+    outs,
+    vs, u_ref, p_ref, window, zu_ref, zp_ref, edges, fixes, yf, zf,
+    rolled, zs, zp, tots,
+):
+    out = outs[0]
+
+    def fill(x, carry):
+        for zt in range(2):
+            vs[zt, x, 8 : 8 + CY, :] = v[x, :, pl.ds(128 * zt, 128)]
+        return carry
+
+    lax.fori_loop(0, CX, fill, 0)
+    yf[0], yf[1] = low_high(parity[1], ya_in[...], yb_in[...])
+    for x in range(CX):
+        for zt in range(2):
+            lanes = slice(128 * zt, 128 * zt + 128)
+            for k in range(3):
+                vs[zt, x, 5 + k : 6 + k, :] = yf[0, k, x : x + 1, lanes]
+                vs[zt, x, 8 + CY + k : 9 + CY + k, :] = yf[1, k, x : x + 1, lanes]
+
+    z_low, z_high = low_high(parity[2], za_in[...], zb_in[...])
+    zlo0, zhi0 = low_high(parity[2], za0[...], zb0[...])
+    zlo_own, zhi_own = low_high(parity[2], za_own[...], zb_own[...])
+    window[5:8, :] = z_low[5:8]
+    window[8:16, :] = zlo_own
+    fixed = edge_column(window, zu_ref, zp_ref, 6, 7, sigma_of(zlo0))
+    for half, lane_at, cell_at in ((0, 0, 0), (0, 1, 2), (1, 0, 1)):
+        edges[half, lane_at : lane_at + 1, :] = fixed[cell_at : cell_at + 1]
+    window[8:16, :] = zhi_own
+    window[16:19, :] = z_high[0:3]
+    fixed = edge_column(window, zu_ref, zp_ref, 9, 8, sigma_of(zhi0))
+    for half, lane_at, cell_at in ((0, 127, 6), (1, 126, 5), (1, 127, 7)):
+        edges[half, lane_at : lane_at + 1, :] = fixed[cell_at : cell_at + 1]
+    for half in range(2):
+        fixes[half] = edges[half].T
 
     lane = lax.broadcasted_iota(jnp.int32, (8, 128), 1)
     fix_even = (lane < 2) | (lane == 127)
@@ -497,15 +501,29 @@
     )(mixed)
 
 
+def x_sums(parity, sigma, v, xa, xb):
+    return pl.pallas_call(
+        x_kernel,
+        out_shape=jax.ShapeDtypeStruct((2, CX, CY, 128), F32),
+        in_specs=parity_specs(4),
+        out_specs=vmem_specs(1)[0],
+        scratch_shapes=[pltpu.VMEM((2, 3, CY, CZ), F32)],
+        compiler_params=pltpu.CompilerParams(vmem_limit_bytes=VMEM_LIMIT),
+        cost_estimate=pl.CostEstimate(flops=20000000, bytes_accessed=6000000, transcendentals=400000),
+        name="x_sums",
+    )(parity, sigma, v, xa, xb)
+
+
 def step(parity, sigma_in, pace, za0, zb0, v, za_own, zb_own, halos, last):
+    xa, xb, *others = halos
+    summed = x_sums(parity, sigma_in, v, xa, xb)
     return pl.pallas_call(
         functools.partial(step_kernel, last),
         out_shape=[BLOCK] + face_shapes(1 if last else 3),
-        in_specs=parity_specs(13),
+        in_specs=parity_specs(12),
         out_specs=vmem_specs(6 if last else 7),
         scratch_shapes=[
             pltpu.VMEM((2, CX, 64, 128), F32),
-            pltpu.VMEM((2, CX, CY, 128), F32),
             pltpu.VMEM((2, 4, 64, 128), F32),
             pltpu.VMEM((2, 2, 64, 128), F32),
             pltpu.VMEM((24, ROWS), F32),
@@ -516,7 +534,6 @@
         ]
         + FACE_SCRATCH
         + [
-            pltpu.VMEM((2, 3, CY, CZ), F32),
             pltpu.VMEM((4, CY, 128), F32),
             pltpu.VMEM((12, CY, 128), F32),
             pltpu.VMEM((5, CY, 128), F32),
@@ -524,7 +541,7 @@
         ],
         compiler_params=pltpu.CompilerParams(vmem_limit_bytes=VMEM_LIMIT),
         name="step",
-    )(parity, sigma_in, pace, za0, zb0, v, za_own, zb_own, *halos)
+    )(parity, sigma_in, pace, za0, zb0, v, za_own, zb_own, summed, *others)
 
 
 HALF_COS = [
@@ -571,8 +588,9 @@
     down = jnp.sum(jnp.where(row == column, owner, 0.0), axis=1, keepdims=True)
     earlier = (row < column) & (row < live_count) & (down == owner)
     rank = jnp.sum(earlier.astype(F32), axis=0, keepdims=True)
-    slot = jnp.where(live, 2.0 * owner + rank, F32(SLOTS))
-    to_slot = (slot == row.astype(F32)).astype(F32)
+    owner_at = jnp.where(live, owner, F32(SLOTS))
+    peers = lax.broadcasted_iota(jnp.int32, (PEERS, SLOTS), 0).astype(F32)
+    to_slot = [((owner_at == peers) & (rank == F32(c))).astype(F32) for c in range(2)]
 
     def finder(count, brick_of):
         at = lax.broadcasted_iota(jnp.int32, (count, SLOTS), 0)
@@ -752,10 +770,35 @@
                     lambda at: jnp.where(at < CY, 48 * bx + 16 * (at // 16) + 15 * side, -1),
                 ),
             )
-    total = exact_dot(found, to_slot, (((1,), (1,)), ((), ())))
     scale = 2.0 / 3.0 / (BRICK * BRICK)
     row = lax.broadcasted_iota(jnp.int32, (8, SLOTS), 0)
-    record[...] = total * jnp.where(row == 1, F32(scale), F32(0.5 * scale))
+    found = found * jnp.where(row == 1, F32(scale), F32(0.5 * scale))
+    for c in range(2):
+        record[:, 8 * c : 8 * c + 8] = exact_dot(to_slot[c], found, (((1,), (1,)), ((), ())))
+
+
+def arrange_kernel(received, out):
+    source = lax.broadcasted_iota(jnp.int32, (PEERS, SLOTS), 0)
+    slot = lax.broadcasted_iota(jnp.int32, (PEERS, SLOTS), 1)
+    total = jnp.zeros((8, SLOTS), F32)
+    for c in range(2):
+        total = total + exact_dot(
+            received[:, 8 * c : 8 * c + 8], (slot == 2 * source + c).astype(F32),
+            (((0,), (0,)), ((), ())),
+        )
+    for n in range(5):
+        out[0, 0, n] = total[n : n + 1]
+
+
+def arrange(received):
+    return pl.pallas_call(
+        arrange_kernel,
+        out_shape=jax.ShapeDtypeStruct((1, 1, 5, 1, SLOTS), F32),
+        in_specs=vmem_specs(1),
+        out_specs=vmem_specs(1)[0],
+        compiler_params=pltpu.CompilerParams(vmem_limit_bytes=VMEM_LIMIT),
+        name="arrange",
+    )(received)
 
 
 def inner_bricks(v):
@@ -774,7 +817,7 @@
 def edge_bricks(parity, count, inner, v, halos, y_rows, planes, ids, targets):
     return pl.pallas_call(
         edge_kernel,
-        out_shape=jax.ShapeDtypeStruct((8, SLOTS), F32),
+        out_shape=jax.ShapeDtypeStruct((PEERS, 16), F32),
         in_specs=[pl.BlockSpec(memory_space=pltpu.SMEM)] * 2 + vmem_specs(12),
         out_specs=vmem_specs(1)[0],
         scratch_shapes=[
@@ -833,8 +876,8 @@
         parity, band_count.reshape(1), inner, v, (xa, xb, ya, yb, za, zb), y_rows, planes,
         band_ids.reshape(1, SLOTS), owners.reshape(1, SLOTS),
     )
-    totals = lax.all_to_all(record[:5], ("gx", "gy"), split_axis=1, concat_axis=1, tiled=True)
-    return level_set, totals.reshape(1, 1, 1, 5, SLOTS)
+    received = lax.all_to_all(record, ("gx", "gy"), split_axis=0, concat_axis=0, tiled=True)
+    return level_set, jnp.swapaxes(arrange(received), 2, 3)
 
 
 def solution(mesh):

time: 120 us -> 111 us (0.925)
  waiting for transfers between devices: 18 us -> 11.9 us
  starting transfers between devices: 49.7 us -> 45.2 us
  Pallas kernels: 47.7 us -> 51.1 us
  local copies, waits for them, and re-layouts: 2.82 us -> 1.42 us
    pallas_call x1 -> x5, Pallas kernels: 2.04 us -> 13.1 us  [the longest x3 9.54 us: x_sums(): pl.pallas_call(x_kernel, out_shape=jax.ShapeDtypeStruct((2, CX, CY, 128),...]
    pallas_call x3, Pallas kernels: 35.7 us -> 28 us  [step(): pl.pallas_call(functools.partial(step_kernel, last), out_shape=[BLOCK] +...]
    ppermute x24, waiting for transfers between devices: 13 us -> 7.11 us  [swap(): return lax.ppermute(value, axis, pairs)]
    ppermute x24, starting transfers between devices: 42.7 us -> 39 us  [swap(): return lax.ppermute(value, axis, pairs)]
  transfers between devices with their start and end apart: 25 -> 25, of which waited for: 11 -> 7; matrix products, arithmetic and copies ran while one was open for 0% -> 0% of each run, Pallas kernels for 5% -> 14%
where the time goes in v5:
time: 111 us
  Pallas kernels  51.1 us (46%)
  starting transfers between devices  45.2 us (41%)
  waiting for transfers between devices  11.9 us (11%)
  between operations  1.5 us (1%)
  local copies, waits for them, and re-layouts  1.42 us (1%)
    ppermute x24, starting transfers between devices, swap(): return lax.ppermute(value, axis, pairs)  39 us
    pallas_call x3, Pallas kernels, step(): pl.pallas_call(functools.partial(step_kernel, last), out_shape=[BLOCK] +...  28 us
    pallas_call x3, Pallas kernels, x_sums(): pl.pallas_call(x_kernel, out_shape=jax.ShapeDtypeStruct((2, CX, CY, 128),...  9.54 us
    ppermute x24, waiting for transfers between devices, swap(): return lax.ppermute(value, axis, pairs)  7.11 us
    all_to_all x1, starting transfers between devices, per_device(): lax.all_to_all(record, ('gx', 'gy'), split_axis=0, concat_axis=0, tiled=T...  6.2 us
    all_to_all x1, waiting for transfers between devices, per_device(): lax.all_to_all(record, ('gx', 'gy'), split_axis=0, concat_axis=0, tiled=T...  4.75 us
    pallas_call x1, Pallas kernels, inner_bricks(): pl.pallas_call(inner_kernel, out_shape=jax.ShapeDtypeStruct((48, 128), F3...  3.66 us
    pallas_call x1, Pallas kernels, pack(): pl.pallas_call(pack_kernel, out_shape=[BLOCK] * 3 + face_shapes(3), in_sp...  2.8 us
  transfers between devices with their start and end apart: 25, of which 7 were waited for; matrix products, arithmetic and copies ran while one was open for 0% of the time, Pallas kernels for 14%

profile of v5, /device:TPU:1, one launch (start us, length us, event | category | flops | bytes accessed | tf_op | source)
XLA Modules:
  0.0 111.2 jit_solution(10870505910371185068)
XLA Ops:
  0.7 1.4 %copy-done = f32[32,48,256]{2,1,0:T(8,128)S(1)} copy-done((f32[32,48,256]{2,1,0:T(8,128)S(1)}, f32[32,48,256]{2,1,0:T(8,128)}, u32[]{:S(2)}) %copy-start) | copy-done | bytes 1572888
  2.1 2.8 %pack.1 = (f32[32,48,256]{2,1,0:T(8,128)S(1)}, f32[32,48,256]{2,1,0:T(8,128)S(1)}, f32[32,48,256]{2,1,0:T(8,128)S(1)}, f32[3,48,256]{2,1,0:T(8,128)S(1)}, f32[3,...) custom-call(s32[3]{0:T(128)S(1)} %pad_add_fusion.parity, ...), custom_call_target="tpu_custom_call" | custom-call | tf_op jit(solution)/shard_map/pack/pallas_call | solution.py:481
  4.9 3.3 %collective-permute-start = (f32[3,48,256]{2,1,0:T(8,128)S(1)}, f32[3,48,256]{2,1,0:T(8,128)S(1)}, u32[]{:S(2)}, u32[]{:S(2)}) collective-permute-start(f32[3,48,256]{2,1,0:T(8,128)S(1)} %get-tuple-element.45), channel_id=1, source_target_pairs={{0,64},{64,0},{128,192},{192,128},{1,65},{65,1},{129,193},{193,129... | collective-permute-start | bytes 442376 | tf_op jit(solution)/shard_map/ppermute | solution.py:838
  8.3 1.9 %collective-permute-start.2 = (f32[3,32,256]{2,1,0:T(8,128)S(1)}, f32[3,32,256]{2,1,0:T(8,128)S(1)}, u32[]{:S(2)}, u32[]{:S(2)}) collective-permute-start(f32[3,32,256]{2,1,0:T(8,128)S(1)} %get-tuple-element.47), channel_id=1, source_target_pairs={{0,8},{8,0},{16,24},{24,16},{32,40},{40,32},{48,56},{56,48},{1,9},... | collective-permute-start | bytes 294920 | tf_op jit(solution)/shard_map/ppermute | solution.py:838
  10.2 3.0 %collective-permute-start.3 = (f32[3,32,256]{2,1,0:T(8,128)S(1)}, f32[3,32,256]{2,1,0:T(8,128)S(1)}, u32[]{:S(2)}, u32[]{:S(2)}) collective-permute-start(f32[3,32,256]{2,1,0:T(8,128)S(1)} %get-tuple-element.48), channel_id=1, source_target_pairs={{0,56},{8,16},{16,8},{24,32},{32,24},{40,48},{48,40},{56,0},{1,57}... | collective-permute-start | bytes 294920 | tf_op jit(solution)/shard_map/ppermute | solution.py:838
  13.2 1.6 %collective-permute-start.4 = (f32[8,1536]{1,0:T(8,128)S(1)}, f32[8,1536]{1,0:T(8,128)S(1)}, u32[]{:S(2)}, u32[]{:S(2)}) collective-permute-start(f32[8,1536]{1,0:T(8,128)S(1)} %get-tuple-element.42.za0.za_own), channel_id=1, source_target_pairs={{0,1},{1,0},{2,3},{3,2},{4,5},{5,4},{6,7},{7,6},{8,9},{9,8},{10,11... | collective-permute-start | bytes 147464 | tf_op jit(solution)/shard_map/ppermute | solution.py:838
  14.8 4.7 %collective-permute-start.5 = (f32[8,1536]{1,0:T(8,128)S(1)}, f32[8,1536]{1,0:T(8,128)S(1)}, u32[]{:S(2)}, u32[]{:S(2)}) collective-permute-start(f32[8,1536]{1,0:T(8,128)S(1)} %get-tuple-element.43.zb0.zb_own), channel_id=1, source_target_pairs={{0,7},{1,2},{2,1},{3,4},{4,3},{5,6},{6,5},{7,0},{8,15},{9,10},{10,... | collective-permute-start | bytes 147464 | tf_op jit(solution)/shard_map/ppermute | solution.py:838
  19.5 3.2 %x_sums.3.summed = f32[2,32,48,128]{3,2,1,0:T(8,128)S(1)} custom-call(s32[3]{0:T(128)S(1)} %pad_add_fusion.parity, f32[32,48,256]{2,1,0:T(8,128)S(1)} %get-tuple-element.40.sigma_in, f32[32,48,256]{2,1,0:T(8,128)S(1)} %get-tuple-element.44.v, f32[3,48,256]{2,1,0:T(8,128)S(1)} %collective-permute-done.xa_in, f32[3,48,256]{2,1,0:T(8,128)S(1)} %collective-permute-done.1.xb_in), custom_call_target="tpu_custom_call" | custom-call | flops 20000000 | bytes 6000000 | tf_op jit(solution)/shard_map/x_sums/pallas_call | solution.py:505
  22.7 9.3 %step.3 = (f32[32,48,256]{2,1,0:T(8,128)S(1)}, f32[3,48,256]{2,1,0:T(8,128)S(1)}, f32[3,48,256]{2,1,0:T(8,128)S(1)}, f32[3,32,256]{2,1,0:T(8,128)S(1)}, f32[3,32...) custom-call(s32[3]{0:T(128)S(1)} %pad_add_fusion.parity, ...), custom_call_target="tpu_custom_call" | custom-call | tf_op jit(solution)/shard_map/step/pallas_call | solution.py:520
  32.0 1.6 %collective-permute-start.6 = (f32[3,48,256]{2,1,0:T(8,128)S(1)}, f32[3,48,256]{2,1,0:T(8,128)S(1)}, u32[]{:S(2)}, u32[]{:S(2)}) collective-permute-start(f32[3,48,256]{2,1,0:T(8,128)S(1)} %get-tuple-element.52), channel_id=1, source_target_pairs={{0,64},{64,0},{128,192},{192,128},{1,65},{65,1},{129,193},{193,129... | collective-permute-start | bytes 442376 | tf_op jit(solution)/shard_map/ppermute | solution.py:838
  33.9 1.3 %collective-permute-start.8 = (f32[3,32,256]{2,1,0:T(8,128)S(1)}, f32[3,32,256]{2,1,0:T(8,128)S(1)}, u32[]{:S(2)}, u32[]{:S(2)}) collective-permute-start(f32[3,32,256]{2,1,0:T(8,128)S(1)} %get-tuple-element.54), channel_id=1, source_target_pairs={{0,8},{8,0},{16,24},{24,16},{32,40},{40,32},{48,56},{56,48},{1,9},... | collective-permute-start | bytes 294920 | tf_op jit(solution)/shard_map/ppermute | solution.py:838
  35.2 1.8 %collective-permute-start.9 = (f32[3,32,256]{2,1,0:T(8,128)S(1)}, f32[3,32,256]{2,1,0:T(8,128)S(1)}, u32[]{:S(2)}, u32[]{:S(2)}) collective-permute-start(f32[3,32,256]{2,1,0:T(8,128)S(1)} %get-tuple-element.55), channel_id=1, source_target_pairs={{0,56},{8,16},{16,8},{24,32},{32,24},{40,48},{48,40},{56,0},{1,57}... | collective-permute-start | bytes 294920 | tf_op jit(solution)/shard_map/ppermute | solution.py:838
  37.0 3.5 %collective-permute-start.11 = (f32[8,1536]{1,0:T(8,128)S(1)}, f32[8,1536]{1,0:T(8,128)S(1)}, u32[]{:S(2)}, u32[]{:S(2)}) collective-permute-start(f32[8,1536]{1,0:T(8,128)S(1)} %get-tuple-element.51.zb_own), channel_id=1, source_target_pairs={{0,7},{1,2},{2,1},{3,4},{4,3},{5,6},{6,5},{7,0},{8,15},{9,10},{10,... | collective-permute-start | bytes 147464 | tf_op jit(solution)/shard_map/ppermute | solution.py:838
  40.5 3.2 %x_sums.4.summed = f32[2,32,48,128]{3,2,1,0:T(8,128)S(1)} custom-call(s32[3]{0:T(128)S(1)} %pad_add_fusion.parity, f32[32,48,256]{2,1,0:T(8,128)S(1)} %get-tuple-element.40.sigma_in, f32[32,48,256]{2,1,0:T(8,128)S(1)} %get-tuple-element.49.v, f32[3,48,256]{2,1,0:T(8,128)S(1)} %collective-permute-done.6.xa_in, f32[3,48,256]{2,1,0:T(8,128)S(1)} %collective-permute-done.7.xb_in), custom_call_target="tpu_custom_call" | custom-call | flops 20000000 | bytes 6000000 | tf_op jit(solution)/shard_map/x_sums/pallas_call | solution.py:505
  44.3 9.3 %step.4 = (f32[32,48,256]{2,1,0:T(8,128)S(1)}, f32[3,48,256]{2,1,0:T(8,128)S(1)}, f32[3,48,256]{2,1,0:T(8,128)S(1)}, f32[3,32,256]{2,1,0:T(8,128)S(1)}, f32[3,32...) custom-call(s32[3]{0:T(128)S(1)} %pad_add_fusion.parity, ...), custom_call_target="tpu_custom_call" | custom-call | tf_op jit(solution)/shard_map/step/pallas_call | solution.py:520
  53.6 1.0 collective-permute-start.12
  54.7 1.4 %collective-permute-start.13 = (f32[3,48,256]{2,1,0:T(8,128)S(1)}, f32[3,48,256]{2,1,0:T(8,128)S(1)}, u32[]{:S(2)}, u32[]{:S(2)}) collective-permute-start(f32[3,48,256]{2,1,0:T(8,128)S(1)} %get-tuple-element.60), channel_id=1, source_target_pairs={{0,192},{64,128},{128,64},{192,0},{1,193},{65,129},{129,65},{193,1... | collective-permute-start | bytes 442376 | tf_op jit(solution)/shard_map/ppermute | solution.py:838
  56.2 2.9 %collective-permute-start.15 = (f32[3,32,256]{2,1,0:T(8,128)S(1)}, f32[3,32,256]{2,1,0:T(8,128)S(1)}, u32[]{:S(2)}, u32[]{:S(2)}) collective-permute-start(f32[3,32,256]{2,1,0:T(8,128)S(1)} %get-tuple-element.62), channel_id=1, source_target_pairs={{0,56},{8,16},{16,8},{24,32},{32,24},{40,48},{48,40},{56,0},{1,57}... | collective-permute-start | bytes 294920 | tf_op jit(solution)/shard_map/ppermute | solution.py:838
  59.2 3.7 %collective-permute-start.17 = (f32[8,1536]{1,0:T(8,128)S(1)}, f32[8,1536]{1,0:T(8,128)S(1)}, u32[]{:S(2)}, u32[]{:S(2)}) collective-permute-start(f32[8,1536]{1,0:T(8,128)S(1)} %get-tuple-element.58.zb_own), channel_id=1, source_target_pairs={{0,7},{1,2},{2,1},{3,4},{4,3},{5,6},{6,5},{7,0},{8,15},{9,10},{10,... | collective-permute-start | bytes 147464 | tf_op jit(solution)/shard_map/ppermute | solution.py:838
  62.9 3.2 %x_sums.5.summed = f32[2,32,48,128]{3,2,1,0:T(8,128)S(1)} custom-call(s32[3]{0:T(128)S(1)} %pad_add_fusion.parity, f32[32,48,256]{2,1,0:T(8,128)S(1)} %get-tuple-element.40.sigma_in, f32[32,48,256]{2,1,0:T(8,128)S(1)} %get-tuple-element.56.v, f32[3,48,256]{2,1,0:T(8,128)S(1)} %collective-permute-done.12.xa_in, f32[3,48,256]{2,1,0:T(8,128)S(1)} %collective-permute-done.13.xb_in), custom_call_target="tpu_custom_call" | custom-call | flops 20000000 | bytes 6000000 | tf_op jit(solution)/shard_map/x_sums/pallas_call | solution.py:505
  66.1 1.1 %collective-permute-done.15.yb_in = f32[3,32,256]{2,1,0:T(8,128)S(1)} collective-permute-done((f32[3,32,256]{2,1,0:T(8,128)S(1)}, f32[3,32,256]{2,1,0:T(8,128)S(1)}, u32[]{:S(2)}, u32[]{:S(2)}) %collective-permute-start.15) | collective-permute-done | bytes 98336 | tf_op jit(solution)/shard_map/ppermute | solution.py:838
  67.2 9.5 %step.5 = (f32[32,48,256]{2,1,0:T(8,128)S(1)}, f32[1,48,256]{2,1,0:T(8,128)S(1)}, f32[1,48,256]{2,1,0:T(8,128)S(1)}, f32[2,32,256]{2,1,0:T(8,128)S(1)}, f32[2,32...) custom-call(s32[3]{0:T(128)S(1)} %pad_add_fusion.parity, f32[32,48,256]{2,1,0:T(8,128)S(1)} %get-tuple-element.40.sigma_in, ...), custom_call_target="tpu_custom_call" | custom-call | tf_op jit(solution)/shard_map/step/pallas_call | solution.py:520
  76.7 1.0 collective-permute-start.18
  78.6 2.7 %collective-permute-done.19.xb = f32[1,48,256]{2,1,0:T(8,128)S(1)} collective-permute-done((f32[1,48,256]{2,1,0:T(8,128)S(1)}, f32[1,48,256]{2,1,0:T(8,128)S(1)}, u32[]{:S(2)}, u32[]{:S(2)}) %collective-permute-start.19) | collective-permute-done | bytes 49184 | tf_op jit(solution)/shard_map/ppermute | solution.py:838
  82.6 1.5 %collective-permute-start.21 = (f32[34,256]{1,0:T(8,128)S(1)}, f32[34,256]{1,0:T(8,128)S(1)}, u32[]{:S(2)}, u32[]{:S(2)}) collective-permute-start(f32[34,256]{1,0:T(8,128)S(1)} %get-tuple-element.69), channel_id=1, source_target_pairs={{0,56},{8,16},{16,8},{24,32},{32,24},{40,48},{48,40},{56,0},{1,57}... | collective-permute-start | bytes 104456 | tf_op jit(solution)/shard_map/ppermute | solution.py:838
  84.1 3.7 %inner_bricks.1.inner = f32[48,128]{1,0:T(8,128)S(1)} custom-call(f32[32,48,256]{2,1,0:T(8,128)S(1)} %get-tuple-element.63.mixed.v), custom_call_target="tpu_custom_call" | custom-call | flops 20000000 | bytes 6000000 | tf_op jit(solution)/shard_map/inner_bricks/pallas_call | solution.py:805
  87.8 1.3 %collective-permute-done.21.yb = f32[34,256]{1,0:T(8,128)S(1)} collective-permute-done((f32[34,256]{1,0:T(8,128)S(1)}, f32[34,256]{1,0:T(8,128)S(1)}, u32[]{:S(2)}, u32[]{:S(2)}) %collective-permute-start.21) | collective-permute-done | bytes 34848 | tf_op jit(solution)/shard_map/ppermute | solution.py:838
  90.1 3.1 %collective-permute-start.23 = (f32[40,128]{1,0:T(8,128)S(1)}, f32[40,128]{1,0:T(8,128)S(1)}, u32[]{:S(2)}, u32[]{:S(2)}) collective-permute-start(f32[40,128]{1,0:T(8,128)S(1)} %get-tuple-element.75), channel_id=1, source_target_pairs={{0,7},{1,2},{2,1},{3,4},{4,3},{5,6},{6,5},{7,0},{8,15},{9,10},{10,... | collective-permute-start | bytes 61448 | tf_op jit(solution)/shard_map/ppermute | solution.py:838
  94.4 2.7 %edge_bricks.1 = f32[32,16]{1,0:T(8,128)} custom-call(s32[3]{0:T(128)S(1)} %pad_add_fusion.parity, s32[1]{0:T(128)} %bitcast.13.count, f32[48,128]{1,0:T(8,128)S(1)} %inner_bricks.1.inner, f32[32,48,256]{2,1,0:T(8,128)S(1)} %get-tuple-element.63.mixed.v, f32[1,48,256]{2,1,0:T(8,128)S(1)} %collective-permute-done.18.xa, ...), custom_call_target="tpu_custom_call" | custom-call | tf_op jit(solution)/shard_map/edge_bricks/pallas_call | solution.py:818
  97.2 6.2 %all-to-all-start = ((f32[32,1,16]{2,1,0:T(1,128)}), f32[32,1,16]{2,1,0:T(1,128)S(1)}, u32[]{:S(2)}, u32[]{:S(2)}) async-start(f32[32,1,16]{2,1,0:T(1,128)} %bitcast.7), calls=%async_computation | async-start | bytes 32768 | tf_op jit(solution)/shard_map/all_to_all | solution.py:879
  103.4 2.2 %unpack.1 = f32[32,48,256]{2,1,0:T(8,128)} custom-call(f32[32,48,256]{2,1,0:T(8,128)S(1)} %get-tuple-element.63.mixed.v), custom_call_target="tpu_custom_call" | custom-call | tf_op jit(solution)/shard_map/unpack/pallas_call | solution.py:493
  105.6 4.8 %all-to-all-done = f32[32,1,16]{2,1,0:T(1,128)S(1)} async-done(((f32[32,1,16]{2,1,0:T(1,128)}), f32[32,1,16]{2,1,0:T(1,128)S(1)}, u32[]{:S(2)}, u32[]{:S(2)}) %all-to-all-start) | async-done | bytes 2080 | tf_op jit(solution)/shard_map/all_to_all | solution.py:879
  (38 shorter events, 5.8 us)
Async XLA Ops:
  0.7 1.4 %copy-start = (f32[32,48,256]{2,1,0:T(8,128)S(1)}, f32[32,48,256]{2,1,0:T(8,128)}, u32[]{:S(2)}) copy-start(f32[32,48,256]{2,1,0:T(8,128)} %phi.1) | copy-start | bytes 4718596
  4.9 9.9 %collective-permute-start = (f32[3,48,256]{2,1,0:T(8,128)S(1)}, f32[3,48,256]{2,1,0:T(8,128)S(1)}, u32[]{:S(2)}, u32[]{:S(2)}) collective-permute-start(f32[3,48,256]{2,1,0:T(8,128)S(1)} %get-tuple-element.45), channel_id=1, source_target_pairs={{0,64},{64,0},{128,192},{192,128},{1,65},{65,1},{129,193},{193,129... | collective-permute-start | bytes 442376 | tf_op jit(solution)/shard_map/ppermute | solution.py:838
  8.3 11.2 %collective-permute-start.1 = (f32[3,48,256]{2,1,0:T(8,128)S(1)}, f32[3,48,256]{2,1,0:T(8,128)S(1)}, u32[]{:S(2)}, u32[]{:S(2)}) collective-permute-start(f32[3,48,256]{2,1,0:T(8,128)S(1)} %get-tuple-element.46), channel_id=1, source_target_pairs={{0,192},{64,128},{128,64},{192,0},{1,193},{65,129},{129,65},{193,1... | collective-permute-start | bytes 442376 | tf_op jit(solution)/shard_map/ppermute | solution.py:838
  8.3 14.4 %collective-permute-start.2 = (f32[3,32,256]{2,1,0:T(8,128)S(1)}, f32[3,32,256]{2,1,0:T(8,128)S(1)}, u32[]{:S(2)}, u32[]{:S(2)}) collective-permute-start(f32[3,32,256]{2,1,0:T(8,128)S(1)} %get-tuple-element.47), channel_id=1, source_target_pairs={{0,8},{8,0},{16,24},{24,16},{32,40},{40,32},{48,56},{56,48},{1,9},... | collective-permute-start | bytes 294920 | tf_op jit(solution)/shard_map/ppermute | solution.py:838
  10.2 12.5 %collective-permute-start.3 = (f32[3,32,256]{2,1,0:T(8,128)S(1)}, f32[3,32,256]{2,1,0:T(8,128)S(1)}, u32[]{:S(2)}, u32[]{:S(2)}) collective-permute-start(f32[3,32,256]{2,1,0:T(8,128)S(1)} %get-tuple-element.48), channel_id=1, source_target_pairs={{0,56},{8,16},{16,8},{24,32},{32,24},{40,48},{48,40},{56,0},{1,57}... | collective-permute-start | bytes 294920 | tf_op jit(solution)/shard_map/ppermute | solution.py:838
  13.2 9.5 %collective-permute-start.4 = (f32[8,1536]{1,0:T(8,128)S(1)}, f32[8,1536]{1,0:T(8,128)S(1)}, u32[]{:S(2)}, u32[]{:S(2)}) collective-permute-start(f32[8,1536]{1,0:T(8,128)S(1)} %get-tuple-element.42.za0.za_own), channel_id=1, source_target_pairs={{0,1},{1,0},{2,3},{3,2},{4,5},{5,4},{6,7},{7,6},{8,9},{9,8},{10,11... | collective-permute-start | bytes 147464 | tf_op jit(solution)/shard_map/ppermute | solution.py:838
  14.8 7.9 %collective-permute-start.5 = (f32[8,1536]{1,0:T(8,128)S(1)}, f32[8,1536]{1,0:T(8,128)S(1)}, u32[]{:S(2)}, u32[]{:S(2)}) collective-permute-start(f32[8,1536]{1,0:T(8,128)S(1)} %get-tuple-element.43.zb0.zb_own), channel_id=1, source_target_pairs={{0,7},{1,2},{2,1},{3,4},{4,3},{5,6},{6,5},{7,0},{8,15},{9,10},{10,... | collective-permute-start | bytes 147464 | tf_op jit(solution)/shard_map/ppermute | solution.py:838
  32.0 5.0 %collective-permute-start.6 = (f32[3,48,256]{2,1,0:T(8,128)S(1)}, f32[3,48,256]{2,1,0:T(8,128)S(1)}, u32[]{:S(2)}, u32[]{:S(2)}) collective-permute-start(f32[3,48,256]{2,1,0:T(8,128)S(1)} %get-tuple-element.52), channel_id=1, source_target_pairs={{0,64},{64,0},{128,192},{192,128},{1,65},{65,1},{129,193},{193,129... | collective-permute-start | bytes 442376 | tf_op jit(solution)/shard_map/ppermute | solution.py:838
  33.6 6.9 %collective-permute-start.7 = (f32[3,48,256]{2,1,0:T(8,128)S(1)}, f32[3,48,256]{2,1,0:T(8,128)S(1)}, u32[]{:S(2)}, u32[]{:S(2)}) collective-permute-start(f32[3,48,256]{2,1,0:T(8,128)S(1)} %get-tuple-element.53), channel_id=1, source_target_pairs={{0,192},{64,128},{128,64},{192,0},{1,193},{65,129},{129,65},{193,1... | collective-permute-start | bytes 442376 | tf_op jit(solution)/shard_map/ppermute | solution.py:838
  33.9 9.8 %collective-permute-start.8 = (f32[3,32,256]{2,1,0:T(8,128)S(1)}, f32[3,32,256]{2,1,0:T(8,128)S(1)}, u32[]{:S(2)}, u32[]{:S(2)}) collective-permute-start(f32[3,32,256]{2,1,0:T(8,128)S(1)} %get-tuple-element.54), channel_id=1, source_target_pairs={{0,8},{8,0},{16,24},{24,16},{32,40},{40,32},{48,56},{56,48},{1,9},... | collective-permute-start | bytes 294920 | tf_op jit(solution)/shard_map/ppermute | solution.py:838
  35.2 9.2 %collective-permute-start.9 = (f32[3,32,256]{2,1,0:T(8,128)S(1)}, f32[3,32,256]{2,1,0:T(8,128)S(1)}, u32[]{:S(2)}, u32[]{:S(2)}) collective-permute-start(f32[3,32,256]{2,1,0:T(8,128)S(1)} %get-tuple-element.55), channel_id=1, source_target_pairs={{0,56},{8,16},{16,8},{24,32},{32,24},{40,48},{48,40},{56,0},{1,57}... | collective-permute-start | bytes 294920 | tf_op jit(solution)/shard_map/ppermute | solution.py:838
  37.0 6.7 %collective-permute-start.10 = (f32[8,1536]{1,0:T(8,128)S(1)}, f32[8,1536]{1,0:T(8,128)S(1)}, u32[]{:S(2)}, u32[]{:S(2)}) collective-permute-start(f32[8,1536]{1,0:T(8,128)S(1)} %get-tuple-element.50.za_own), channel_id=1, source_target_pairs={{0,1},{1,0},{2,3},{3,2},{4,5},{5,4},{6,7},{7,6},{8,9},{9,8},{10,11... | collective-permute-start | bytes 147464 | tf_op jit(solution)/shard_map/ppermute | solution.py:838
  37.0 6.7 %collective-permute-start.11 = (f32[8,1536]{1,0:T(8,128)S(1)}, f32[8,1536]{1,0:T(8,128)S(1)}, u32[]{:S(2)}, u32[]{:S(2)}) collective-permute-start(f32[8,1536]{1,0:T(8,128)S(1)} %get-tuple-element.51.zb_own), channel_id=1, source_target_pairs={{0,7},{1,2},{2,1},{3,4},{4,3},{5,6},{6,5},{7,0},{8,15},{9,10},{10,... | collective-permute-start | bytes 147464 | tf_op jit(solution)/shard_map/ppermute | solution.py:838
  53.6 5.6 %collective-permute-start.12 = (f32[3,48,256]{2,1,0:T(8,128)S(1)}, f32[3,48,256]{2,1,0:T(8,128)S(1)}, u32[]{:S(2)}, u32[]{:S(2)}) collective-permute-start(f32[3,48,256]{2,1,0:T(8,128)S(1)} %get-tuple-element.59), channel_id=1, source_target_pairs={{0,64},{64,0},{128,192},{192,128},{1,65},{65,1},{129,193},{193,129... | collective-permute-start | bytes 442376 | tf_op jit(solution)/shard_map/ppermute | solution.py:838
  54.7 8.2 %collective-permute-start.13 = (f32[3,48,256]{2,1,0:T(8,128)S(1)}, f32[3,48,256]{2,1,0:T(8,128)S(1)}, u32[]{:S(2)}, u32[]{:S(2)}) collective-permute-start(f32[3,48,256]{2,1,0:T(8,128)S(1)} %get-tuple-element.60), channel_id=1, source_target_pairs={{0,192},{64,128},{128,64},{192,0},{1,193},{65,129},{129,65},{193,1... | collective-permute-start | bytes 442376 | tf_op jit(solution)/shard_map/ppermute | solution.py:838
  56.1 10.0 %collective-permute-start.14 = (f32[3,32,256]{2,1,0:T(8,128)S(1)}, f32[3,32,256]{2,1,0:T(8,128)S(1)}, u32[]{:S(2)}, u32[]{:S(2)}) collective-permute-start(f32[3,32,256]{2,1,0:T(8,128)S(1)} %get-tuple-element.61), channel_id=1, source_target_pairs={{0,8},{8,0},{16,24},{24,16},{32,40},{40,32},{48,56},{56,48},{1,9},... | collective-permute-start | bytes 294920 | tf_op jit(solution)/shard_map/ppermute | solution.py:838
  56.2 11.0 %collective-permute-start.15 = (f32[3,32,256]{2,1,0:T(8,128)S(1)}, f32[3,32,256]{2,1,0:T(8,128)S(1)}, u32[]{:S(2)}, u32[]{:S(2)}) collective-permute-start(f32[3,32,256]{2,1,0:T(8,128)S(1)} %get-tuple-element.62), channel_id=1, source_target_pairs={{0,56},{8,16},{16,8},{24,32},{32,24},{40,48},{48,40},{56,0},{1,57}... | collective-permute-start | bytes 294920 | tf_op jit(solution)/shard_map/ppermute | solution.py:838
  59.2 6.9 %collective-permute-start.16 = (f32[8,1536]{1,0:T(8,128)S(1)}, f32[8,1536]{1,0:T(8,128)S(1)}, u32[]{:S(2)}, u32[]{:S(2)}) collective-permute-start(f32[8,1536]{1,0:T(8,128)S(1)} %get-tuple-element.57.za_own), channel_id=1, source_target_pairs={{0,1},{1,0},{2,3},{3,2},{4,5},{5,4},{6,7},{7,6},{8,9},{9,8},{10,11... | collective-permute-start | bytes 147464 | tf_op jit(solution)/shard_map/ppermute | solution.py:838
  59.2 6.9 %collective-permute-start.17 = (f32[8,1536]{1,0:T(8,128)S(1)}, f32[8,1536]{1,0:T(8,128)S(1)}, u32[]{:S(2)}, u32[]{:S(2)}) collective-permute-start(f32[8,1536]{1,0:T(8,128)S(1)} %get-tuple-element.58.zb_own), channel_id=1, source_target_pairs={{0,7},{1,2},{2,1},{3,4},{4,3},{5,6},{6,5},{7,0},{8,15},{9,10},{10,... | collective-permute-start | bytes 147464 | tf_op jit(solution)/shard_map/ppermute | solution.py:838
  76.7 17.8 %copy-start.1 = (s32[1,1,1,64]{3,2,1,0:T(1,128)S(1)}, s32[1,1,1,64]{3,2,1,0:T(1,128)}, u32[]{:S(2)}) copy-start(s32[1,1,1,64]{3,2,1,0:T(1,128)} %param.5) | copy-start | bytes 772
  76.7 17.7 %copy-start.2 = (s32[1,1,1,64]{3,2,1,0:T(1,128)S(1)}, s32[1,1,1,64]{3,2,1,0:T(1,128)}, u32[]{:S(2)}) copy-start(s32[1,1,1,64]{3,2,1,0:T(1,128)} %param.7) | copy-start | bytes 772
  76.7 1.9 %collective-permute-start.18 = (f32[1,48,256]{2,1,0:T(8,128)S(1)}, f32[1,48,256]{2,1,0:T(8,128)S(1)}, u32[]{:S(2)}, u32[]{:S(2)}) collective-permute-start(f32[1,48,256]{2,1,0:T(8,128)S(1)} %get-tuple-element.64), channel_id=1, source_target_pairs={{0,64},{64,0},{128,192},{192,128},{1,65},{65,1},{129,193},{193,129... | collective-permute-start | bytes 147464 | tf_op jit(solution)/shard_map/ppermute | solution.py:838
  77.7 3.5 %collective-permute-start.19 = (f32[1,48,256]{2,1,0:T(8,128)S(1)}, f32[1,48,256]{2,1,0:T(8,128)S(1)}, u32[]{:S(2)}, u32[]{:S(2)}) collective-permute-start(f32[1,48,256]{2,1,0:T(8,128)S(1)} %get-tuple-element.65), channel_id=1, source_target_pairs={{0,192},{64,128},{128,64},{192,0},{1,193},{65,129},{129,65},{193,1... | collective-permute-start | bytes 147464 | tf_op jit(solution)/shard_map/ppermute | solution.py:838
  81.8 5.9 %collective-permute-start.20 = (f32[34,256]{1,0:T(8,128)S(1)}, f32[34,256]{1,0:T(8,128)S(1)}, u32[]{:S(2)}, u32[]{:S(2)}) collective-permute-start(f32[34,256]{1,0:T(8,128)S(1)} %get-tuple-element.68), channel_id=1, source_target_pairs={{0,8},{8,0},{16,24},{24,16},{32,40},{40,32},{48,56},{56,48},{1,9},... | collective-permute-start | bytes 104456 | tf_op jit(solution)/shard_map/ppermute | solution.py:838
  82.6 6.5 %collective-permute-start.21 = (f32[34,256]{1,0:T(8,128)S(1)}, f32[34,256]{1,0:T(8,128)S(1)}, u32[]{:S(2)}, u32[]{:S(2)}) collective-permute-start(f32[34,256]{1,0:T(8,128)S(1)} %get-tuple-element.69), channel_id=1, source_target_pairs={{0,56},{8,16},{16,8},{24,32},{32,24},{40,48},{48,40},{56,0},{1,57}... | collective-permute-start | bytes 104456 | tf_op jit(solution)/shard_map/ppermute | solution.py:838
  89.8 4.1 %collective-permute-start.22 = (f32[40,128]{1,0:T(8,128)S(1)}, f32[40,128]{1,0:T(8,128)S(1)}, u32[]{:S(2)}, u32[]{:S(2)}) collective-permute-start(f32[40,128]{1,0:T(8,128)S(1)} %get-tuple-element.74), channel_id=1, source_target_pairs={{0,1},{1,0},{2,3},{3,2},{4,5},{5,4},{6,7},{7,6},{8,9},{9,8},{10,11... | collective-permute-start | bytes 61448 | tf_op jit(solution)/shard_map/ppermute | solution.py:838
  90.1 4.3 %collective-permute-start.23 = (f32[40,128]{1,0:T(8,128)S(1)}, f32[40,128]{1,0:T(8,128)S(1)}, u32[]{:S(2)}, u32[]{:S(2)}) collective-permute-start(f32[40,128]{1,0:T(8,128)S(1)} %get-tuple-element.75), channel_id=1, source_target_pairs={{0,7},{1,2},{2,1},{3,4},{4,3},{5,6},{6,5},{7,0},{8,15},{9,10},{10,... | collective-permute-start | bytes 61448 | tf_op jit(solution)/shard_map/ppermute | solution.py:838
  97.2 13.2 %all-to-all-start = ((f32[32,1,16]{2,1,0:T(1,128)}), f32[32,1,16]{2,1,0:T(1,128)S(1)}, u32[]{:S(2)}, u32[]{:S(2)}) async-start(f32[32,1,16]{2,1,0:T(1,128)} %bitcast.7), calls=%async_computation | async-start | bytes 32768 | tf_op jit(solution)/shard_map/all_to_all | solution.py:879

commit v6 on v5

--- a/solution.py
+++ b/solution.py
@@ -10,6 +10,7 @@
 STEPS = 3
 BRICK = 16
 SLOTS = 64
+PAIR = 8
 PEERS = 32
 CX, CY, CZ = 32, 48, 256
 ROWS = CX * CY
@@ -152,7 +153,7 @@
     return jnp.where(odd, part_a, part_b), jnp.where(odd, part_b, part_a)
 
 
-def pack_kernel(parity, phi, mixed, sigma, pace, xa, xb, ya, yb, za, zb, turned, yf, zf):
+def pack_kernel(parity, phi, mixed, xa, xb, ya, yb, za, zb, turned, yf, zf):
     for chunk in range(CX // 8):
         planes = slice(8 * chunk, 8 * chunk + 8)
         for half in range(2):
@@ -164,14 +165,17 @@
             part = [turned[c, pl.ds(which, 128, stride=2), :].T for c in range(3)]
             part = jnp.concatenate(part, axis=0)
             mixed[planes, :, 128 * which : 128 * which + 128] = part.reshape(8, CY, 128)
+    write_faces(parity, mixed, xa, xb, ya, yb, za, zb, yf, zf)
+
+
+def signs_kernel(start, sigma, pace):
     def signs(x, carry):
-        value = mixed[x]
+        value = start[x]
         sigma[x] = sigma_of(value)
         pace[x] = (0.05 * value) * lax.rsqrt(value * value + 1.0)
         return carry
 
     lax.fori_loop(0, CX, signs, 0)
-    write_faces(parity, mixed, xa, xb, ya, yb, za, zb, yf, zf)
 
 
 def unpack_kernel(mixed, out, turned):
@@ -188,7 +192,30 @@
             out[planes, :, 128 * half : 128 * half + 128] = part.reshape(8, CY, 128)
 
 
-def x_kernel(parity, sigma_in, v, xa_in, xb_in, summed, xh):
+def edge_lanes():
+    lane = lax.broadcasted_iota(jnp.int32, (8, 128), 1)
+    return [(lane < 2) | (lane == 127), (lane < 1) | (lane > 125)]
+
+
+def run_stages(stages, count):
+    depth = len(stages) - 1
+
+    def run(at, low, high):
+        for delay in range(high, low - 1, -1):
+            stages[delay](at - delay)
+
+    def body(at, carry):
+        run(at, 0, depth)
+        return carry
+
+    for at in range(depth):
+        run(at, 0, at)
+    lax.fori_loop(depth, count, body, 0)
+    for at in range(depth):
+        run(count + at, at + 1, depth)
+
+
+def xz_kernel(parity, sigma_in, v, xa_in, xb_in, summed, xh, rolled, zs, zp):
     xh[0], xh[1] = low_high(parity[0], xa_in[...], xb_in[...])
 
     def x_pass(yt, carry):
@@ -226,6 +253,50 @@
         return carry
 
     lax.fori_loop(0, YT, x_pass, 0)
+    edge = edge_lanes()
+
+    def tile(x, half, k):
+        return v[x, 8 * k : 8 * k + 8, 128 * half : 128 * half + 128]
+
+    def spots(item):
+        for sub in range(PAIR):
+            for k in range(YT):
+                start = CY * sub + 8 * k
+                yield PAIR * item + sub, k, slice(start, start + 8)
+
+    def turn(item):
+        for x, k, at in spots(item):
+            for half in range(2):
+                part = tile(x, half, k)
+                rolled[half, at, :] = lane_down(part)
+                rolled[2 + half, at, :] = lane_up(part)
+
+    def weigh(item):
+        for x, k, at in spots(item):
+            parts = z_stage_weights(
+                tile(x, 0, k), tile(x, 1, k), *[rolled[slot, at, :] for slot in range(4)]
+            )
+            for slot, part in enumerate(parts):
+                zs[slot, at, :] = part
+
+    def blend(item):
+        for x, k, at in spots(item):
+            parts = z_stage_parts(*[zs[slot, at, :] for slot in range(12)])
+            for slot, part in enumerate(parts):
+                zp[slot, at, :] = part
+
+    def add(item):
+        for x, k, at in spots(item):
+            rows = slice(8 * k, 8 * k + 8)
+            for half in range(2):
+                sigma = sigma_in[x, rows, 128 * half : 128 * half + 128]
+                if half == 0:
+                    along = upwind_pair(zp[0, at, :] - zp[1, at, :], zp[2, at, :], sigma)
+                else:
+                    along = upwind_pair(zp[3, at, :], zp[4, at, :], sigma)
+                summed[half, x, rows, :] += jnp.where(edge[half], 0.0, along)
+
+    run_stages((turn, weigh, blend, add), CX // PAIR)
 
 
 def step_kernel(
@@ -243,7 +314,6 @@
     parity, sigma_in, pace, za0, zb0, v, za_own, zb_own, summed, ya_in, yb_in, za_in, zb_in,
     outs,
     vs, u_ref, p_ref, window, zu_ref, zp_ref, edges, fixes, yf, zf,
-    rolled, zs, zp, tots,
 ):
     out = outs[0]
 
@@ -277,9 +347,7 @@
     for half in range(2):
         fixes[half] = edges[half].T
 
-    lane = lax.broadcasted_iota(jnp.int32, (8, 128), 1)
-    fix_even = (lane < 2) | (lane == 127)
-    fix_odd = (lane < 1) | (lane > 125)
+    edge = edge_lanes()
 
     def y_weights(x, zt, k):
         start = 6 + 8 * k
@@ -302,85 +370,35 @@
         p_ref[zt, 0, pl.ds(8 * k, 8), :] = left
         p_ref[zt, 1, pl.ds(8 * k, 8), :] = right
 
-    def tile(x, zt, k):
-        return v[x, 8 * k : 8 * k + 8, 128 * zt : 128 * zt + 128]
-
-    def sigma_at(x, zt, k):
-        return sigma_in[x, 8 * k : 8 * k + 8, 128 * zt : 128 * zt + 128]
-
-    def stage_0(x):
-        for k in range(YT):
-            rows = slice(8 * k, 8 * k + 8)
-            for slot, part in enumerate((tile(x, 0, k), tile(x, 1, k))):
-                rolled[slot, rows, :] = lane_down(part)
-                rolled[2 + slot, rows, :] = lane_up(part)
+    def weigh(x):
         for zt in range(2):
             for k in range(YT + 1):
                 y_weights(x, zt, k)
 
-    def stage_1(x):
-        for k in range(YT):
-            rows = slice(8 * k, 8 * k + 8)
-            parts = z_stage_weights(
-                tile(x, 0, k), tile(x, 1, k), *[rolled[slot, rows, :] for slot in range(4)]
-            )
-            for slot, part in enumerate(parts):
-                zs[slot, rows, :] = part
+    def blend(x):
         for zt in range(2):
             for k in range(YT + 1):
                 y_parts(zt, k)
 
-    def stage_2(x):
-        for k in range(YT):
-            rows = slice(8 * k, 8 * k + 8)
-            parts = z_stage_parts(*[zs[slot, rows, :] for slot in range(12)])
-            for slot, part in enumerate(parts):
-                zp[slot, rows, :] = part
+    def update(x):
+        flat = pl.multiple_of(x * CY, 8)
         for zt in range(2):
             for k in range(YT):
                 rows = slice(8 * k, 8 * k + 8)
+                lanes = slice(128 * zt, 128 * zt + 128)
                 centre = 3.0 * (
                     vs[zt, x, 9 + 8 * k : 17 + 8 * k, :] - vs[zt, x, 7 + 8 * k : 15 + 8 * k, :]
                 )
-                tots[zt, rows, :] = summed[zt, x, rows, :] + upwind_square(
+                along = upwind_square(
                     centre, p_ref[zt, 0, rows, :], p_ref[zt, 1, 8 * k + 1 : 8 * k + 9, :],
-                    sigma_at(x, zt, k),
+                    sigma_in[x, rows, lanes],
                 )
-
-    def stage_3(x):
-        flat = pl.multiple_of(x * CY, 8)
-        for k in range(YT):
-            rows = slice(8 * k, 8 * k + 8)
-            for zt in range(2):
-                sigma = sigma_at(x, zt, k)
-                if zt == 0:
-                    along = upwind_pair(zp[0, rows, :] - zp[1, rows, :], zp[2, rows, :], sigma)
-                    edge = fix_even
-                else:
-                    along = upwind_pair(zp[3, rows, :], zp[4, rows, :], sigma)
-                    edge = fix_odd
-                along = jnp.where(edge, fixes[zt, pl.ds(flat + 8 * k, 8), :], along)
-                total = tots[zt, rows, :] + along
+                fix = jnp.where(edge[zt], fixes[zt, pl.ds(flat + 8 * k, 8), :], 0.0)
+                total = summed[zt, x, rows, :] + along + fix
                 root = total * lax.rsqrt(jnp.maximum(total, 1e-30))
-                lanes = slice(128 * zt, 128 * zt + 128)
                 out[x, rows, lanes] = v[x, rows, lanes] - pace[x, rows, lanes] * (root - 6.0)
 
-    stages = (stage_3, stage_2, stage_1, stage_0)
-
-    def run(at, low, high):
-        for delay, stage in zip((3, 2, 1, 0), stages):
-            if low <= delay <= high:
-                stage(at - delay)
-
-    def yz_pass(at, carry):
-        run(at, 0, 3)
-        return carry
-
-    for at in range(3):
-        run(at, 0, at)
-    lax.fori_loop(3, CX, yz_pass, 0)
-    for at in range(3):
-        run(CX + at, at + 1, 3)
+    run_stages((weigh, blend, update), CX)
     if last:
         xa, xb, ylo, yhi, planes = outs[1:]
         write_swap(parity[0], out[0:1], out[CX - 1 : CX], xa, xb)
@@ -480,13 +498,26 @@
 def pack(parity, phi):
     return pl.pallas_call(
         pack_kernel,
-        out_shape=[BLOCK] * 3 + face_shapes(3),
+        out_shape=[BLOCK] + face_shapes(3),
         in_specs=parity_specs(1),
-        out_specs=vmem_specs(9),
-        scratch_shapes=[pltpu.VMEM((3, CZ, 128), F32)] + FACE_SCRATCH,
+        out_specs=vmem_specs(7),
+        scratch_shapes=[pltpu.VMEM((3, CZ, 128), F32)]
+        + FACE_SCRATCH,
         compiler_params=pltpu.CompilerParams(vmem_limit_bytes=VMEM_LIMIT),
         name="pack",
     )(parity, phi)
+
+
+def sign_fields(start):
+    return pl.pallas_call(
+        signs_kernel,
+        out_shape=[BLOCK] * 2,
+        in_specs=vmem_specs(1),
+        out_specs=vmem_specs(2),
+        compiler_params=pltpu.CompilerParams(vmem_limit_bytes=VMEM_LIMIT),
+        cost_estimate=pl.CostEstimate(flops=2000000, bytes_accessed=4700000, transcendentals=400000),
+        name="sign_fields",
+    )(start)
 
 
 def unpack(mixed):
@@ -501,22 +532,27 @@
     )(mixed)
 
 
-def x_sums(parity, sigma, v, xa, xb):
+def xz_sums(parity, sigma, v, xa, xb):
     return pl.pallas_call(
-        x_kernel,
+        xz_kernel,
         out_shape=jax.ShapeDtypeStruct((2, CX, CY, 128), F32),
         in_specs=parity_specs(4),
         out_specs=vmem_specs(1)[0],
-        scratch_shapes=[pltpu.VMEM((2, 3, CY, CZ), F32)],
+        scratch_shapes=[
+            pltpu.VMEM((2, 3, CY, CZ), F32),
+            pltpu.VMEM((4, PAIR * CY, 128), F32),
+            pltpu.VMEM((12, PAIR * CY, 128), F32),
+            pltpu.VMEM((5, PAIR * CY, 128), F32),
+        ],
         compiler_params=pltpu.CompilerParams(vmem_limit_bytes=VMEM_LIMIT),
         cost_estimate=pl.CostEstimate(flops=20000000, bytes_accessed=6000000, transcendentals=400000),
-        name="x_sums",
+        name="xz_sums",
     )(parity, sigma, v, xa, xb)
 
 
 def step(parity, sigma_in, pace, za0, zb0, v, za_own, zb_own, halos, last):
     xa, xb, *others = halos
-    summed = x_sums(parity, sigma_in, v, xa, xb)
+    summed = xz_sums(parity, sigma_in, v, xa, xb)
     return pl.pallas_call(
         functools.partial(step_kernel, last),
         out_shape=[BLOCK] + face_shapes(1 if last else 3),
@@ -532,13 +568,7 @@
             pltpu.VMEM((2, 128, ROWS), F32),
             pltpu.VMEM((2, ROWS, 128), F32),
         ]
-        + FACE_SCRATCH
-        + [
-            pltpu.VMEM((4, CY, 128), F32),
-            pltpu.VMEM((12, CY, 128), F32),
-            pltpu.VMEM((5, CY, 128), F32),
-            pltpu.VMEM((2, CY, 128), F32),
-        ],
+        + FACE_SCRATCH,
         compiler_params=pltpu.CompilerParams(vmem_limit_bytes=VMEM_LIMIT),
         name="step",
     )(parity, sigma_in, pace, za0, zb0, v, za_own, zb_own, summed, *others)
@@ -852,7 +882,8 @@
 def per_device(phi_start, band_ids, band_count, owners):
     parity = jnp.stack([lax.axis_index(name) % 2 for name in ("gx", "gy", "gz")])
     parity = parity.astype(jnp.int32)
-    v, sigma, pace, *faces = pack(parity, phi_start)
+    v, *faces = pack(parity, phi_start)
+    sigma, pace = sign_fields(v)
     za0, zb0 = faces[4:]
     for number in range(STEPS):
         v, *faces = step(

time: 111 us -> 109 us (0.982)
  starting transfers between devices: 45.2 us -> 41.3 us
    pallas_call x4 -> x5, Pallas kernels: 12.3 us -> 21.7 us  [the longest x3 18.9 us: xz_sums(): pl.pallas_call(xz_kernel, out_shape=jax.ShapeDtypeStruct((2, CX, CY, 128)...]
    pallas_call x3, Pallas kernels: 28 us -> 18.9 us  [step(): pl.pallas_call(functools.partial(step_kernel, last), out_shape=[BLOCK] +...]
    ppermute x24, starting transfers between devices: 39 us -> 34.9 us  [swap(): return lax.ppermute(value, axis, pairs)]
  transfers between devices with their start and end apart: 25 -> 25, of which waited for: 7 -> 6; matrix products, arithmetic and copies ran while one was open for 0% -> 0% of each run, Pallas kernels for 14% -> 23%
where the time goes in v6:
time: 109 us; the launch traced here: 108 us
  Pallas kernels  51.3 us (47%)
  starting transfers between devices  41.3 us (38%)
  waiting for transfers between devices  12.8 us (12%)
  between operations  1.54 us (1%)
  local copies, waits for them, and re-layouts  1.42 us (1%)
    ppermute x24, starting transfers between devices, swap(): return lax.ppermute(value, axis, pairs)  34.9 us
    pallas_call x3, Pallas kernels, step(): pl.pallas_call(functools.partial(step_kernel, last), out_shape=[BLOCK] +...  18.9 us
    pallas_call x3, Pallas kernels, xz_sums(): pl.pallas_call(xz_kernel, out_shape=jax.ShapeDtypeStruct((2, CX, CY, 128)...  18.9 us
    ppermute x24, waiting for transfers between devices, swap(): return lax.ppermute(value, axis, pairs)  8.06 us
    all_to_all x1, starting transfers between devices, per_device(): lax.all_to_all(record, ('gx', 'gy'), split_axis=0, concat_axis=0, tiled=T...  6.39 us
    all_to_all x1, waiting for transfers between devices, per_device(): lax.all_to_all(record, ('gx', 'gy'), split_axis=0, concat_axis=0, tiled=T...  4.7 us
    pallas_call x1, Pallas kernels, inner_bricks(): pl.pallas_call(inner_kernel, out_shape=jax.ShapeDtypeStruct((48, 128), F3...  3.66 us
    pallas_call x1, Pallas kernels, edge_bricks(): pl.pallas_call(edge_kernel, out_shape=jax.ShapeDtypeStruct((PEERS, 16), F...  2.73 us
  transfers between devices with their start and end apart: 25, of which 6 were waited for; matrix products, arithmetic and copies ran while one was open for 0% of the time, Pallas kernels for 23%

profile of v6, /device:TPU:1, one launch (start us, length us, event | category | flops | bytes accessed | tf_op | source)
XLA Modules:
  0.0 108.4 jit_solution(11651998224749855726)
XLA Ops:
  0.7 1.4 %copy-done = f32[32,48,256]{2,1,0:T(8,128)S(1)} copy-done((f32[32,48,256]{2,1,0:T(8,128)S(1)}, f32[32,48,256]{2,1,0:T(8,128)}, u32[]{:S(2)}) %copy-start) | copy-done | bytes 1572888
  2.1 2.1 %pack.1 = (f32[32,48,256]{2,1,0:T(8,128)S(1)}, f32[3,48,256]{2,1,0:T(8,128)S(1)}, f32[3,48,256]{2,1,0:T(8,128)S(1)}, f32[3,32,256]{2,1,0:T(8,128)S(1)}, f32[3,32...) custom-call(s32[3]{0:T(128)S(1)} %pad_add_fusion.parity, f32[32,48,256]{2,1,0:T(8,128)S(1)} %copy-done), custom_call_target="tpu_custom_call" | custom-call | tf_op jit(solution)/shard_map/pack/pallas_call | solution.py:499
  4.3 3.3 %collective-permute-start = (f32[3,48,256]{2,1,0:T(8,128)S(1)}, f32[3,48,256]{2,1,0:T(8,128)S(1)}, u32[]{:S(2)}, u32[]{:S(2)}) collective-permute-start(f32[3,48,256]{2,1,0:T(8,128)S(1)} %get-tuple-element.45), channel_id=1, source_target_pairs={{0,64},{64,0},{128,192},{192,128},{1,65},{65,1},{129,193},{193,129... | collective-permute-start | bytes 442376 | tf_op jit(solution)/shard_map/ppermute | solution.py:868
  7.6 1.9 %collective-permute-start.2 = (f32[3,32,256]{2,1,0:T(8,128)S(1)}, f32[3,32,256]{2,1,0:T(8,128)S(1)}, u32[]{:S(2)}, u32[]{:S(2)}) collective-permute-start(f32[3,32,256]{2,1,0:T(8,128)S(1)} %get-tuple-element.47), channel_id=1, source_target_pairs={{0,8},{8,0},{16,24},{24,16},{32,40},{40,32},{48,56},{56,48},{1,9},... | collective-permute-start | bytes 294920 | tf_op jit(solution)/shard_map/ppermute | solution.py:868
  9.5 3.0 %collective-permute-start.3 = (f32[3,32,256]{2,1,0:T(8,128)S(1)}, f32[3,32,256]{2,1,0:T(8,128)S(1)}, u32[]{:S(2)}, u32[]{:S(2)}) collective-permute-start(f32[3,32,256]{2,1,0:T(8,128)S(1)} %get-tuple-element.48), channel_id=1, source_target_pairs={{0,56},{8,16},{16,8},{24,32},{32,24},{40,48},{48,40},{56,0},{1,57}... | collective-permute-start | bytes 294920 | tf_op jit(solution)/shard_map/ppermute | solution.py:868
  12.5 1.6 %collective-permute-start.4 = (f32[8,1536]{1,0:T(8,128)S(1)}, f32[8,1536]{1,0:T(8,128)S(1)}, u32[]{:S(2)}, u32[]{:S(2)}) collective-permute-start(f32[8,1536]{1,0:T(8,128)S(1)} %get-tuple-element.43.za0.za_own), channel_id=1, source_target_pairs={{0,1},{1,0},{2,3},{3,2},{4,5},{5,4},{6,7},{7,6},{8,9},{9,8},{10,11... | collective-permute-start | bytes 147464 | tf_op jit(solution)/shard_map/ppermute | solution.py:868
  14.1 4.7 %collective-permute-start.5 = (f32[8,1536]{1,0:T(8,128)S(1)}, f32[8,1536]{1,0:T(8,128)S(1)}, u32[]{:S(2)}, u32[]{:S(2)}) collective-permute-start(f32[8,1536]{1,0:T(8,128)S(1)} %get-tuple-element.44.zb0.zb_own), channel_id=1, source_target_pairs={{0,7},{1,2},{2,1},{3,4},{4,3},{5,6},{6,5},{7,0},{8,15},{9,10},{10,... | collective-permute-start | bytes 147464 | tf_op jit(solution)/shard_map/ppermute | solution.py:868
  19.4 6.3 %xz_sums.3.summed = f32[2,32,48,128]{3,2,1,0:T(8,128)S(1)} custom-call(s32[3]{0:T(128)S(1)} %pad_add_fusion.parity, f32[32,48,256]{2,1,0:T(8,128)S(1)} %get-tuple-element.41.sigma_in, f32[32,48,256]{2,1,0:T(8,128)S(1)} %get-tuple-element.40.start.v, f32[3,48,256]{2,1,0:T(8,128)S(1)} %collective-permute-done.xa_in, f32[3,48,256]{2,1,0:T(8,128)S(1)} %collective-permute-done.1.xb_in), custom_call_target="tpu_custom_call" | custom-call | flops 20000000 | bytes 6000000 | tf_op jit(solution)/shard_map/xz_sums/pallas_call | solution.py:536
  25.8 6.3 %step.3 = (f32[32,48,256]{2,1,0:T(8,128)S(1)}, f32[3,48,256]{2,1,0:T(8,128)S(1)}, f32[3,48,256]{2,1,0:T(8,128)S(1)}, f32[3,32,256]{2,1,0:T(8,128)S(1)}, f32[3,32...) custom-call(s32[3]{0:T(128)S(1)} %pad_add_fusion.parity, ...), custom_call_target="tpu_custom_call" | custom-call | tf_op jit(solution)/shard_map/step/pallas_call | solution.py:556
  32.0 1.6 %collective-permute-start.6 = (f32[3,48,256]{2,1,0:T(8,128)S(1)}, f32[3,48,256]{2,1,0:T(8,128)S(1)}, u32[]{:S(2)}, u32[]{:S(2)}) collective-permute-start(f32[3,48,256]{2,1,0:T(8,128)S(1)} %get-tuple-element.52), channel_id=1, source_target_pairs={{0,64},{64,0},{128,192},{192,128},{1,65},{65,1},{129,193},{193,129... | collective-permute-start | bytes 442376 | tf_op jit(solution)/shard_map/ppermute | solution.py:868
  33.9 1.3 %collective-permute-start.8 = (f32[3,32,256]{2,1,0:T(8,128)S(1)}, f32[3,32,256]{2,1,0:T(8,128)S(1)}, u32[]{:S(2)}, u32[]{:S(2)}) collective-permute-start(f32[3,32,256]{2,1,0:T(8,128)S(1)} %get-tuple-element.54), channel_id=1, source_target_pairs={{0,8},{8,0},{16,24},{24,16},{32,40},{40,32},{48,56},{56,48},{1,9},... | collective-permute-start | bytes 294920 | tf_op jit(solution)/shard_map/ppermute | solution.py:868
  35.2 1.8 %collective-permute-start.9 = (f32[3,32,256]{2,1,0:T(8,128)S(1)}, f32[3,32,256]{2,1,0:T(8,128)S(1)}, u32[]{:S(2)}, u32[]{:S(2)}) collective-permute-start(f32[3,32,256]{2,1,0:T(8,128)S(1)} %get-tuple-element.55), channel_id=1, source_target_pairs={{0,56},{8,16},{16,8},{24,32},{32,24},{40,48},{48,40},{56,0},{1,57}... | collective-permute-start | bytes 294920 | tf_op jit(solution)/shard_map/ppermute | solution.py:868
  37.1 1.5 %collective-permute-start.11 = (f32[8,1536]{1,0:T(8,128)S(1)}, f32[8,1536]{1,0:T(8,128)S(1)}, u32[]{:S(2)}, u32[]{:S(2)}) collective-permute-start(f32[8,1536]{1,0:T(8,128)S(1)} %get-tuple-element.51.zb_own), channel_id=1, source_target_pairs={{0,7},{1,2},{2,1},{3,4},{4,3},{5,6},{6,5},{7,0},{8,15},{9,10},{10,... | collective-permute-start | bytes 147464 | tf_op jit(solution)/shard_map/ppermute | solution.py:868
  38.5 1.3 %collective-permute-done.7.xb_in = f32[3,48,256]{2,1,0:T(8,128)S(1)} collective-permute-done((f32[3,48,256]{2,1,0:T(8,128)S(1)}, f32[3,48,256]{2,1,0:T(8,128)S(1)}, u32[]{:S(2)}, u32[]{:S(2)}) %collective-permute-start.7) | collective-permute-done | bytes 147488 | tf_op jit(solution)/shard_map/ppermute | solution.py:868
  39.8 6.3 %xz_sums.4.summed = f32[2,32,48,128]{3,2,1,0:T(8,128)S(1)} custom-call(s32[3]{0:T(128)S(1)} %pad_add_fusion.parity, f32[32,48,256]{2,1,0:T(8,128)S(1)} %get-tuple-element.41.sigma_in, f32[32,48,256]{2,1,0:T(8,128)S(1)} %get-tuple-element.49.v, f32[3,48,256]{2,1,0:T(8,128)S(1)} %collective-permute-done.6.xa_in, f32[3,48,256]{2,1,0:T(8,128)S(1)} %collective-permute-done.7.xb_in), custom_call_target="tpu_custom_call" | custom-call | flops 20000000 | bytes 6000000 | tf_op jit(solution)/shard_map/xz_sums/pallas_call | solution.py:536
  46.1 6.3 %step.4 = (f32[32,48,256]{2,1,0:T(8,128)S(1)}, f32[3,48,256]{2,1,0:T(8,128)S(1)}, f32[3,48,256]{2,1,0:T(8,128)S(1)}, f32[3,32,256]{2,1,0:T(8,128)S(1)}, f32[3,32...) custom-call(s32[3]{0:T(128)S(1)} %pad_add_fusion.parity, ...), custom_call_target="tpu_custom_call" | custom-call | tf_op jit(solution)/shard_map/step/pallas_call | solution.py:556
  52.8 1.2 %collective-permute-start.13 = (f32[3,48,256]{2,1,0:T(8,128)S(1)}, f32[3,48,256]{2,1,0:T(8,128)S(1)}, u32[]{:S(2)}, u32[]{:S(2)}) collective-permute-start(f32[3,48,256]{2,1,0:T(8,128)S(1)} %get-tuple-element.60), channel_id=1, source_target_pairs={{0,192},{64,128},{128,64},{192,0},{1,193},{65,129},{129,65},{193,1... | collective-permute-start | bytes 442376 | tf_op jit(solution)/shard_map/ppermute | solution.py:868
  54.0 1.8 %collective-permute-start.14 = (f32[3,32,256]{2,1,0:T(8,128)S(1)}, f32[3,32,256]{2,1,0:T(8,128)S(1)}, u32[]{:S(2)}, u32[]{:S(2)}) collective-permute-start(f32[3,32,256]{2,1,0:T(8,128)S(1)} %get-tuple-element.61), channel_id=1, source_target_pairs={{0,8},{8,0},{16,24},{24,16},{32,40},{40,32},{48,56},{56,48},{1,9},... | collective-permute-start | bytes 294920 | tf_op jit(solution)/shard_map/ppermute | solution.py:868
  58.9 6.3 %xz_sums.5.summed = f32[2,32,48,128]{3,2,1,0:T(8,128)S(1)} custom-call(s32[3]{0:T(128)S(1)} %pad_add_fusion.parity, f32[32,48,256]{2,1,0:T(8,128)S(1)} %get-tuple-element.41.sigma_in, f32[32,48,256]{2,1,0:T(8,128)S(1)} %get-tuple-element.56.v, f32[3,48,256]{2,1,0:T(8,128)S(1)} %collective-permute-done.12.xa_in, f32[3,48,256]{2,1,0:T(8,128)S(1)} %collective-permute-done.13.xb_in), custom_call_target="tpu_custom_call" | custom-call | flops 20000000 | bytes 6000000 | tf_op jit(solution)/shard_map/xz_sums/pallas_call | solution.py:536
  65.2 6.4 %step.5 = (f32[32,48,256]{2,1,0:T(8,128)S(1)}, f32[1,48,256]{2,1,0:T(8,128)S(1)}, f32[1,48,256]{2,1,0:T(8,128)S(1)}, f32[2,32,256]{2,1,0:T(8,128)S(1)}, f32[2,32...) custom-call(s32[3]{0:T(128)S(1)} %pad_add_fusion.parity, f32[32,48,256]{2,1,0:T(8,128)S(1)} %get-tuple-element.41.sigma_in, ...), custom_call_target="tpu_custom_call" | custom-call | tf_op jit(solution)/shard_map/step/pallas_call | solution.py:556
  73.4 2.6 %collective-permute-done.19.xb = f32[1,48,256]{2,1,0:T(8,128)S(1)} collective-permute-done((f32[1,48,256]{2,1,0:T(8,128)S(1)}, f32[1,48,256]{2,1,0:T(8,128)S(1)}, u32[]{:S(2)}, u32[]{:S(2)}) %collective-permute-start.19) | collective-permute-done | bytes 49184 | tf_op jit(solution)/shard_map/ppermute | solution.py:868
  76.6 2.3 %collective-permute-start.20 = (f32[34,256]{1,0:T(8,128)S(1)}, f32[34,256]{1,0:T(8,128)S(1)}, u32[]{:S(2)}, u32[]{:S(2)}) collective-permute-start(f32[34,256]{1,0:T(8,128)S(1)} %get-tuple-element.68), channel_id=1, source_target_pairs={{0,8},{8,0},{16,24},{24,16},{32,40},{40,32},{48,56},{56,48},{1,9},... | collective-permute-start | bytes 104456 | tf_op jit(solution)/shard_map/ppermute | solution.py:868
  78.8 1.5 %collective-permute-start.21 = (f32[34,256]{1,0:T(8,128)S(1)}, f32[34,256]{1,0:T(8,128)S(1)}, u32[]{:S(2)}, u32[]{:S(2)}) collective-permute-start(f32[34,256]{1,0:T(8,128)S(1)} %get-tuple-element.69), channel_id=1, source_target_pairs={{0,56},{8,16},{16,8},{24,32},{32,24},{40,48},{48,40},{56,0},{1,57}... | collective-permute-start | bytes 104456 | tf_op jit(solution)/shard_map/ppermute | solution.py:868
  80.3 3.7 %inner_bricks.1.inner = f32[48,128]{1,0:T(8,128)S(1)} custom-call(f32[32,48,256]{2,1,0:T(8,128)S(1)} %get-tuple-element.63.mixed.v), custom_call_target="tpu_custom_call" | custom-call | flops 20000000 | bytes 6000000 | tf_op jit(solution)/shard_map/inner_bricks/pallas_call | solution.py:835
  84.0 1.3 %collective-permute-done.21.yb = f32[34,256]{1,0:T(8,128)S(1)} collective-permute-done((f32[34,256]{1,0:T(8,128)S(1)}, f32[34,256]{1,0:T(8,128)S(1)}, u32[]{:S(2)}, u32[]{:S(2)}) %collective-permute-start.21) | collective-permute-done | bytes 34848 | tf_op jit(solution)/shard_map/ppermute | solution.py:868
  86.1 1.6 %collective-permute-start.22 = (f32[40,128]{1,0:T(8,128)S(1)}, f32[40,128]{1,0:T(8,128)S(1)}, u32[]{:S(2)}, u32[]{:S(2)}) collective-permute-start(f32[40,128]{1,0:T(8,128)S(1)} %get-tuple-element.74), channel_id=1, source_target_pairs={{0,1},{1,0},{2,3},{3,2},{4,5},{5,4},{6,7},{7,6},{8,9},{9,8},{10,11... | collective-permute-start | bytes 61448 | tf_op jit(solution)/shard_map/ppermute | solution.py:868
  87.7 1.3 %collective-permute-start.23 = (f32[40,128]{1,0:T(8,128)S(1)}, f32[40,128]{1,0:T(8,128)S(1)}, u32[]{:S(2)}, u32[]{:S(2)}) collective-permute-start(f32[40,128]{1,0:T(8,128)S(1)} %get-tuple-element.75), channel_id=1, source_target_pairs={{0,7},{1,2},{2,1},{3,4},{4,3},{5,6},{6,5},{7,0},{8,15},{9,10},{10,... | collective-permute-start | bytes 61448 | tf_op jit(solution)/shard_map/ppermute | solution.py:868
  89.7 1.9 %collective-permute-done.23.zb = f32[40,128]{1,0:T(8,128)S(1)} collective-permute-done((f32[40,128]{1,0:T(8,128)S(1)}, f32[40,128]{1,0:T(8,128)S(1)}, u32[]{:S(2)}, u32[]{:S(2)}) %collective-permute-start.23) | collective-permute-done | bytes 20512 | tf_op jit(solution)/shard_map/ppermute | solution.py:868
  91.5 2.7 %edge_bricks.1 = f32[32,16]{1,0:T(8,128)} custom-call(s32[3]{0:T(128)S(1)} %pad_add_fusion.parity, s32[1]{0:T(128)} %bitcast.13.count, f32[48,128]{1,0:T(8,128)S(1)} %inner_bricks.1.inner, f32[32,48,256]{2,1,0:T(8,128)S(1)} %get-tuple-element.63.mixed.v, f32[1,48,256]{2,1,0:T(8,128)S(1)} %collective-permute-done.18.xa, ...), custom_call_target="tpu_custom_call" | custom-call | tf_op jit(solution)/shard_map/edge_bricks/pallas_call | solution.py:848
  94.3 6.4 %all-to-all-start = ((f32[32,1,16]{2,1,0:T(1,128)}), f32[32,1,16]{2,1,0:T(1,128)S(1)}, u32[]{:S(2)}, u32[]{:S(2)}) async-start(f32[32,1,16]{2,1,0:T(1,128)} %bitcast.7), calls=%async_computation | async-start | bytes 32768 | tf_op jit(solution)/shard_map/all_to_all | solution.py:910
  100.7 2.2 %unpack.1 = f32[32,48,256]{2,1,0:T(8,128)} custom-call(f32[32,48,256]{2,1,0:T(8,128)S(1)} %get-tuple-element.63.mixed.v), custom_call_target="tpu_custom_call" | custom-call | tf_op jit(solution)/shard_map/unpack/pallas_call | solution.py:524
  102.9 4.7 %all-to-all-done = f32[32,1,16]{2,1,0:T(1,128)S(1)} async-done(((f32[32,1,16]{2,1,0:T(1,128)}), f32[32,1,16]{2,1,0:T(1,128)S(1)}, u32[]{:S(2)}, u32[]{:S(2)}) %all-to-all-start) | async-done | bytes 2080 | tf_op jit(solution)/shard_map/all_to_all | solution.py:910
  (39 shorter events, 8.3 us)
Async XLA Ops:
  0.7 1.4 %copy-start = (f32[32,48,256]{2,1,0:T(8,128)S(1)}, f32[32,48,256]{2,1,0:T(8,128)}, u32[]{:S(2)}) copy-start(f32[32,48,256]{2,1,0:T(8,128)} %phi.1) | copy-start | bytes 4718596
  4.3 9.9 %collective-permute-start = (f32[3,48,256]{2,1,0:T(8,128)S(1)}, f32[3,48,256]{2,1,0:T(8,128)S(1)}, u32[]{:S(2)}, u32[]{:S(2)}) collective-permute-start(f32[3,48,256]{2,1,0:T(8,128)S(1)} %get-tuple-element.45), channel_id=1, source_target_pairs={{0,64},{64,0},{128,192},{192,128},{1,65},{65,1},{129,193},{193,129... | collective-permute-start | bytes 442376 | tf_op jit(solution)/shard_map/ppermute | solution.py:868
  7.6 11.8 %collective-permute-start.1 = (f32[3,48,256]{2,1,0:T(8,128)S(1)}, f32[3,48,256]{2,1,0:T(8,128)S(1)}, u32[]{:S(2)}, u32[]{:S(2)}) collective-permute-start(f32[3,48,256]{2,1,0:T(8,128)S(1)} %get-tuple-element.46), channel_id=1, source_target_pairs={{0,192},{64,128},{128,64},{192,0},{1,193},{65,129},{129,65},{193,1... | collective-permute-start | bytes 442376 | tf_op jit(solution)/shard_map/ppermute | solution.py:868
  7.6 18.1 %collective-permute-start.2 = (f32[3,32,256]{2,1,0:T(8,128)S(1)}, f32[3,32,256]{2,1,0:T(8,128)S(1)}, u32[]{:S(2)}, u32[]{:S(2)}) collective-permute-start(f32[3,32,256]{2,1,0:T(8,128)S(1)} %get-tuple-element.47), channel_id=1, source_target_pairs={{0,8},{8,0},{16,24},{24,16},{32,40},{40,32},{48,56},{56,48},{1,9},... | collective-permute-start | bytes 294920 | tf_op jit(solution)/shard_map/ppermute | solution.py:868
  9.5 16.2 %collective-permute-start.3 = (f32[3,32,256]{2,1,0:T(8,128)S(1)}, f32[3,32,256]{2,1,0:T(8,128)S(1)}, u32[]{:S(2)}, u32[]{:S(2)}) collective-permute-start(f32[3,32,256]{2,1,0:T(8,128)S(1)} %get-tuple-element.48), channel_id=1, source_target_pairs={{0,56},{8,16},{16,8},{24,32},{32,24},{40,48},{48,40},{56,0},{1,57}... | collective-permute-start | bytes 294920 | tf_op jit(solution)/shard_map/ppermute | solution.py:868
  12.5 13.2 %collective-permute-start.4 = (f32[8,1536]{1,0:T(8,128)S(1)}, f32[8,1536]{1,0:T(8,128)S(1)}, u32[]{:S(2)}, u32[]{:S(2)}) collective-permute-start(f32[8,1536]{1,0:T(8,128)S(1)} %get-tuple-element.43.za0.za_own), channel_id=1, source_target_pairs={{0,1},{1,0},{2,3},{3,2},{4,5},{5,4},{6,7},{7,6},{8,9},{9,8},{10,11... | collective-permute-start | bytes 147464 | tf_op jit(solution)/shard_map/ppermute | solution.py:868
  14.1 11.6 %collective-permute-start.5 = (f32[8,1536]{1,0:T(8,128)S(1)}, f32[8,1536]{1,0:T(8,128)S(1)}, u32[]{:S(2)}, u32[]{:S(2)}) collective-permute-start(f32[8,1536]{1,0:T(8,128)S(1)} %get-tuple-element.44.zb0.zb_own), channel_id=1, source_target_pairs={{0,7},{1,2},{2,1},{3,4},{4,3},{5,6},{6,5},{7,0},{8,15},{9,10},{10,... | collective-permute-start | bytes 147464 | tf_op jit(solution)/shard_map/ppermute | solution.py:868
  32.0 5.0 %collective-permute-start.6 = (f32[3,48,256]{2,1,0:T(8,128)S(1)}, f32[3,48,256]{2,1,0:T(8,128)S(1)}, u32[]{:S(2)}, u32[]{:S(2)}) collective-permute-start(f32[3,48,256]{2,1,0:T(8,128)S(1)} %get-tuple-element.52), channel_id=1, source_target_pairs={{0,64},{64,0},{128,192},{192,128},{1,65},{65,1},{129,193},{193,129... | collective-permute-start | bytes 442376 | tf_op jit(solution)/shard_map/ppermute | solution.py:868
  33.7 6.1 %collective-permute-start.7 = (f32[3,48,256]{2,1,0:T(8,128)S(1)}, f32[3,48,256]{2,1,0:T(8,128)S(1)}, u32[]{:S(2)}, u32[]{:S(2)}) collective-permute-start(f32[3,48,256]{2,1,0:T(8,128)S(1)} %get-tuple-element.53), channel_id=1, source_target_pairs={{0,192},{64,128},{128,64},{192,0},{1,193},{65,129},{129,65},{193,1... | collective-permute-start | bytes 442376 | tf_op jit(solution)/shard_map/ppermute | solution.py:868
  33.9 12.2 %collective-permute-start.8 = (f32[3,32,256]{2,1,0:T(8,128)S(1)}, f32[3,32,256]{2,1,0:T(8,128)S(1)}, u32[]{:S(2)}, u32[]{:S(2)}) collective-permute-start(f32[3,32,256]{2,1,0:T(8,128)S(1)} %get-tuple-element.54), channel_id=1, source_target_pairs={{0,8},{8,0},{16,24},{24,16},{32,40},{40,32},{48,56},{56,48},{1,9},... | collective-permute-start | bytes 294920 | tf_op jit(solution)/shard_map/ppermute | solution.py:868
  35.2 10.9 %collective-permute-start.9 = (f32[3,32,256]{2,1,0:T(8,128)S(1)}, f32[3,32,256]{2,1,0:T(8,128)S(1)}, u32[]{:S(2)}, u32[]{:S(2)}) collective-permute-start(f32[3,32,256]{2,1,0:T(8,128)S(1)} %get-tuple-element.55), channel_id=1, source_target_pairs={{0,56},{8,16},{16,8},{24,32},{32,24},{40,48},{48,40},{56,0},{1,57}... | collective-permute-start | bytes 294920 | tf_op jit(solution)/shard_map/ppermute | solution.py:868
  37.1 9.0 %collective-permute-start.10 = (f32[8,1536]{1,0:T(8,128)S(1)}, f32[8,1536]{1,0:T(8,128)S(1)}, u32[]{:S(2)}, u32[]{:S(2)}) collective-permute-start(f32[8,1536]{1,0:T(8,128)S(1)} %get-tuple-element.50.za_own), channel_id=1, source_target_pairs={{0,1},{1,0},{2,3},{3,2},{4,5},{5,4},{6,7},{7,6},{8,9},{9,8},{10,11... | collective-permute-start | bytes 147464 | tf_op jit(solution)/shard_map/ppermute | solution.py:868
  37.1 9.0 %collective-permute-start.11 = (f32[8,1536]{1,0:T(8,128)S(1)}, f32[8,1536]{1,0:T(8,128)S(1)}, u32[]{:S(2)}, u32[]{:S(2)}) collective-permute-start(f32[8,1536]{1,0:T(8,128)S(1)} %get-tuple-element.51.zb_own), channel_id=1, source_target_pairs={{0,7},{1,2},{2,1},{3,4},{4,3},{5,6},{6,5},{7,0},{8,15},{9,10},{10,... | collective-permute-start | bytes 147464 | tf_op jit(solution)/shard_map/ppermute | solution.py:868
  52.4 5.3 %collective-permute-start.12 = (f32[3,48,256]{2,1,0:T(8,128)S(1)}, f32[3,48,256]{2,1,0:T(8,128)S(1)}, u32[]{:S(2)}, u32[]{:S(2)}) collective-permute-start(f32[3,48,256]{2,1,0:T(8,128)S(1)} %get-tuple-element.59), channel_id=1, source_target_pairs={{0,64},{64,0},{128,192},{192,128},{1,65},{65,1},{129,193},{193,129... | collective-permute-start | bytes 442376 | tf_op jit(solution)/shard_map/ppermute | solution.py:868
  52.8 6.1 %collective-permute-start.13 = (f32[3,48,256]{2,1,0:T(8,128)S(1)}, f32[3,48,256]{2,1,0:T(8,128)S(1)}, u32[]{:S(2)}, u32[]{:S(2)}) collective-permute-start(f32[3,48,256]{2,1,0:T(8,128)S(1)} %get-tuple-element.60), channel_id=1, source_target_pairs={{0,192},{64,128},{128,64},{192,0},{1,193},{65,129},{129,65},{193,1... | collective-permute-start | bytes 442376 | tf_op jit(solution)/shard_map/ppermute | solution.py:868
  54.0 11.2 %collective-permute-start.14 = (f32[3,32,256]{2,1,0:T(8,128)S(1)}, f32[3,32,256]{2,1,0:T(8,128)S(1)}, u32[]{:S(2)}, u32[]{:S(2)}) collective-permute-start(f32[3,32,256]{2,1,0:T(8,128)S(1)} %get-tuple-element.61), channel_id=1, source_target_pairs={{0,8},{8,0},{16,24},{24,16},{32,40},{40,32},{48,56},{56,48},{1,9},... | collective-permute-start | bytes 294920 | tf_op jit(solution)/shard_map/ppermute | solution.py:868
  55.8 9.4 %collective-permute-start.15 = (f32[3,32,256]{2,1,0:T(8,128)S(1)}, f32[3,32,256]{2,1,0:T(8,128)S(1)}, u32[]{:S(2)}, u32[]{:S(2)}) collective-permute-start(f32[3,32,256]{2,1,0:T(8,128)S(1)} %get-tuple-element.62), channel_id=1, source_target_pairs={{0,56},{8,16},{16,8},{24,32},{32,24},{40,48},{48,40},{56,0},{1,57}... | collective-permute-start | bytes 294920 | tf_op jit(solution)/shard_map/ppermute | solution.py:868
  56.9 8.2 %collective-permute-start.16 = (f32[8,1536]{1,0:T(8,128)S(1)}, f32[8,1536]{1,0:T(8,128)S(1)}, u32[]{:S(2)}, u32[]{:S(2)}) collective-permute-start(f32[8,1536]{1,0:T(8,128)S(1)} %get-tuple-element.57.za_own), channel_id=1, source_target_pairs={{0,1},{1,0},{2,3},{3,2},{4,5},{5,4},{6,7},{7,6},{8,9},{9,8},{10,11... | collective-permute-start | bytes 147464 | tf_op jit(solution)/shard_map/ppermute | solution.py:868
  57.7 7.5 %collective-permute-start.17 = (f32[8,1536]{1,0:T(8,128)S(1)}, f32[8,1536]{1,0:T(8,128)S(1)}, u32[]{:S(2)}, u32[]{:S(2)}) collective-permute-start(f32[8,1536]{1,0:T(8,128)S(1)} %get-tuple-element.58.zb_own), channel_id=1, source_target_pairs={{0,7},{1,2},{2,1},{3,4},{4,3},{5,6},{6,5},{7,0},{8,15},{9,10},{10,... | collective-permute-start | bytes 147464 | tf_op jit(solution)/shard_map/ppermute | solution.py:868
  71.6 19.9 %copy-start.1 = (s32[1,1,1,64]{3,2,1,0:T(1,128)S(1)}, s32[1,1,1,64]{3,2,1,0:T(1,128)}, u32[]{:S(2)}) copy-start(s32[1,1,1,64]{3,2,1,0:T(1,128)} %param.5) | copy-start | bytes 772
  71.7 19.9 %copy-start.2 = (s32[1,1,1,64]{3,2,1,0:T(1,128)S(1)}, s32[1,1,1,64]{3,2,1,0:T(1,128)}, u32[]{:S(2)}) copy-start(s32[1,1,1,64]{3,2,1,0:T(1,128)} %param.7) | copy-start | bytes 772
  71.7 1.7 %collective-permute-start.18 = (f32[1,48,256]{2,1,0:T(8,128)S(1)}, f32[1,48,256]{2,1,0:T(8,128)S(1)}, u32[]{:S(2)}, u32[]{:S(2)}) collective-permute-start(f32[1,48,256]{2,1,0:T(8,128)S(1)} %get-tuple-element.64), channel_id=1, source_target_pairs={{0,64},{64,0},{128,192},{192,128},{1,65},{65,1},{129,193},{193,129... | collective-permute-start | bytes 147464 | tf_op jit(solution)/shard_map/ppermute | solution.py:868
  72.5 3.5 %collective-permute-start.19 = (f32[1,48,256]{2,1,0:T(8,128)S(1)}, f32[1,48,256]{2,1,0:T(8,128)S(1)}, u32[]{:S(2)}, u32[]{:S(2)}) collective-permute-start(f32[1,48,256]{2,1,0:T(8,128)S(1)} %get-tuple-element.65), channel_id=1, source_target_pairs={{0,192},{64,128},{128,64},{192,0},{1,193},{65,129},{129,65},{193,1... | collective-permute-start | bytes 147464 | tf_op jit(solution)/shard_map/ppermute | solution.py:868
  76.6 7.4 %collective-permute-start.20 = (f32[34,256]{1,0:T(8,128)S(1)}, f32[34,256]{1,0:T(8,128)S(1)}, u32[]{:S(2)}, u32[]{:S(2)}) collective-permute-start(f32[34,256]{1,0:T(8,128)S(1)} %get-tuple-element.68), channel_id=1, source_target_pairs={{0,8},{8,0},{16,24},{24,16},{32,40},{40,32},{48,56},{56,48},{1,9},... | collective-permute-start | bytes 104456 | tf_op jit(solution)/shard_map/ppermute | solution.py:868
  78.8 6.5 %collective-permute-start.21 = (f32[34,256]{1,0:T(8,128)S(1)}, f32[34,256]{1,0:T(8,128)S(1)}, u32[]{:S(2)}, u32[]{:S(2)}) collective-permute-start(f32[34,256]{1,0:T(8,128)S(1)} %get-tuple-element.69), channel_id=1, source_target_pairs={{0,56},{8,16},{16,8},{24,32},{32,24},{40,48},{48,40},{56,0},{1,57}... | collective-permute-start | bytes 104456 | tf_op jit(solution)/shard_map/ppermute | solution.py:868
  86.1 3.6 %collective-permute-start.22 = (f32[40,128]{1,0:T(8,128)S(1)}, f32[40,128]{1,0:T(8,128)S(1)}, u32[]{:S(2)}, u32[]{:S(2)}) collective-permute-start(f32[40,128]{1,0:T(8,128)S(1)} %get-tuple-element.74), channel_id=1, source_target_pairs={{0,1},{1,0},{2,3},{3,2},{4,5},{5,4},{6,7},{7,6},{8,9},{9,8},{10,11... | collective-permute-start | bytes 61448 | tf_op jit(solution)/shard_map/ppermute | solution.py:868
  87.7 3.8 %collective-permute-start.23 = (f32[40,128]{1,0:T(8,128)S(1)}, f32[40,128]{1,0:T(8,128)S(1)}, u32[]{:S(2)}, u32[]{:S(2)}) collective-permute-start(f32[40,128]{1,0:T(8,128)S(1)} %get-tuple-element.75), channel_id=1, source_target_pairs={{0,7},{1,2},{2,1},{3,4},{4,3},{5,6},{6,5},{7,0},{8,15},{9,10},{10,... | collective-permute-start | bytes 61448 | tf_op jit(solution)/shard_map/ppermute | solution.py:868
  94.3 13.3 %all-to-all-start = ((f32[32,1,16]{2,1,0:T(1,128)}), f32[32,1,16]{2,1,0:T(1,128)S(1)}, u32[]{:S(2)}, u32[]{:S(2)}) async-start(f32[32,1,16]{2,1,0:T(1,128)} %bitcast.7), calls=%async_computation | async-start | bytes 32768 | tf_op jit(solution)/shard_map/all_to_all | solution.py:910
